TPU v7x, 512 devices: a whole 4x4x16 slice. The times are simulated.
512 devices in a mesh: seq: 64 (over y, z_hi, x), section: 8 (over z_lo, core).
Axes of the slice: x: 4, y: 4, z: 16 (z_hi: 4, z_lo: 4; z = z_hi * 4 + z_lo), core: 2. Of those that a mesh axis runs over, the one named last changes fastest.
Arguments:
- normed_input: bfloat16 [8192, 3584], P('seq', 'section'), may hold values from -6 to 6
- w_down: bfloat16 [3584, 128], P('section'), may hold values from -0.09375 to 0.09375
- query_rows: bfloat16 [8192, 1792], P('seq', 'section'), may hold values from -9 to 9
- key_rows: bfloat16 [8192, 1792], P('seq', 'section'), may hold values from -9 to 9
- value_base: bfloat16 [8192, 1792], P('seq', 'section'), may hold values from -6 to 6
- cotangent: bfloat16 [8192, 1792], P('seq', 'section'), may hold values from -6 to 6
- master: float32 [128, 1792], P('seq', 'section'), may hold values from -5 to 5
- first_moment: float32 [128, 1792], P('seq', 'section'), may hold values from -4 to 4
- second_moment: float32 [128, 1792], P('seq', 'section'), may hold values from 0.1 to 2
Outputs:
- query_grad: bfloat16 [8192, 1792], P('seq', 'section')
- key_grad: bfloat16 [8192, 1792], P('seq', 'section')
- new_master: float32 [128, 1792], P('seq', 'section')
- new_first: float32 [128, 1792], P('seq', 'section')
- new_second: float32 [128, 1792], P('seq', 'section')
All inputs are finite; a program needn't handle non-finite values.
Results may differ from a plain program's by a relative error of at most 0.011.
Values may be sent and summed in bfloat16 or wider, within the bound.
No kernel may reach another device: no remote copies, remote signals or barrier semaphores. Data moves between devices by JAX's collectives and lax.ppermute only.
A program may use at most 128 MiB of HBM per device.

v0:
```python
import math

import jax
import jax.numpy as jnp
from jax import lax
from jax.sharding import PartitionSpec as P

HEAD = 112
RANK = 128
STEP = 2


BETA_ONE = 0.9
BETA_TWO = 0.95
LEARN_RATE = 0.01
WEIGHT_DECAY = 0.1
ADAM_EPSILON = 1e-08
MASK_VALUE = -1e30


def body(
    normed_input,
    w_down,
    query_rows,
    key_rows,
    value_base,
    cotangent,
    master,
    first_moment,
    second_moment,
):
    score_scale = 1.0 / math.sqrt(HEAD)
    inv_rank = 1.0 / math.sqrt(RANK)
    seq_count = lax.axis_size("seq")
    tok_rows = query_rows.shape[0]
    width = query_rows.shape[1]
    heads_dev = width // HEAD
    total_rows = seq_count * tok_rows
    shards_block = math.gcd(seq_count, max(1, 512 // tok_rows))
    block_rows = shards_block * tok_rows
    position = lax.axis_index("seq")
    own_block = position // shards_block
    w_up = lax.all_gather(master.astype(jnp.bfloat16), "seq", axis=0, tiled=True)
    partial_rank = jnp.dot(normed_input, w_down, preferred_element_type=jnp.float32)
    low_rank = lax.psum(partial_rank, "section").astype(jnp.bfloat16)
    values = (
        value_base.astype(jnp.float32)
        + jnp.dot(low_rank, w_up, preferred_element_type=jnp.float32) * inv_rank
    ).astype(jnp.bfloat16)
    all_keys, all_values = (
        lax.all_gather(key_rows, "seq", axis=0, tiled=True),
        lax.all_gather(values, "seq", axis=0, tiled=True),
    )
    query_heads = query_rows.reshape(tok_rows, heads_dev, HEAD)
    cotan_heads = cotangent.reshape(tok_rows, heads_dev, HEAD)
    row_pos = position * tok_rows + lax.broadcasted_iota(jnp.int32, (1, tok_rows, 1), 1)

    def key_block(start):
        k_blk = lax.dynamic_slice_in_dim(all_keys, start, block_rows, 0).reshape(
            block_rows, heads_dev, HEAD
        )
        v_blk = lax.dynamic_slice_in_dim(all_values, start, block_rows, 0).reshape(
            block_rows, heads_dev, HEAD
        )
        return (k_blk, v_blk)

    def score_pass(index, buffers):
        score_buf, dprob_buf = buffers
        start = (index * block_rows).astype(jnp.int32)
        k_blk, v_blk = key_block(start)
        scores = (
            jnp.einsum("qhd,khd->hqk", query_heads, k_blk, preferred_element_type=jnp.float32)
            * score_scale
        )
        col_pos = start + lax.broadcasted_iota(jnp.int32, (1, 1, block_rows), 2)
        scores = jnp.where(col_pos <= row_pos, scores, MASK_VALUE)
        d_prob = jnp.einsum("qhd,khd->hqk", cotan_heads, v_blk, preferred_element_type=jnp.float32)
        score_buf = lax.dynamic_update_slice_in_dim(score_buf, scores, start, 2)
        dprob_buf = lax.dynamic_update_slice_in_dim(dprob_buf, d_prob, start, 2)
        return (score_buf, dprob_buf)

    score_init = jnp.full((heads_dev, tok_rows, total_rows), MASK_VALUE, jnp.float32)
    dprob_init = jnp.zeros((heads_dev, tok_rows, total_rows), jnp.float32)
    score_all, dprob_all = lax.fori_loop(0, own_block + 1, score_pass, (score_init, dprob_init))
    row_max = jnp.max(score_all, axis=2, keepdims=True)
    log_total = row_max + jnp.log(jnp.sum(jnp.exp(score_all - row_max), axis=2, keepdims=True))
    row_delta = jnp.sum(jnp.exp(score_all - log_total) * dprob_all, axis=2, keepdims=True)

    def block_terms(start):
        scores = lax.dynamic_slice_in_dim(score_all, start, block_rows, 2)
        d_prob = lax.dynamic_slice_in_dim(dprob_all, start, block_rows, 2)
        attn_prob = jnp.exp(scores - log_total)
        d_score = (attn_prob * (d_prob - row_delta)).astype(jnp.bfloat16)
        return (attn_prob.astype(jnp.bfloat16), d_score)

    query_init = jnp.zeros((tok_rows, heads_dev, HEAD), jnp.float32)

    def grad_pass(index, carry):
        query_acc, key_buf, value_buf = carry
        start = (index * block_rows).astype(jnp.int32)
        k_blk, v_blk = key_block(start)
        attn_bf, d_score = block_terms(start)
        query_acc = query_acc + jnp.einsum(
            "hqk,khd->qhd", d_score, k_blk, preferred_element_type=jnp.float32
        )
        key_part = (
            jnp.einsum("hqk,qhd->khd", d_score, query_heads, preferred_element_type=jnp.float32)
            * score_scale
        ).astype(jnp.bfloat16)
        value_part = jnp.einsum(
            "hqk,qhd->khd", attn_bf, cotan_heads, preferred_element_type=jnp.float32
        ).astype(jnp.bfloat16)
        key_buf = lax.dynamic_update_slice_in_dim(
            key_buf, key_part.reshape(block_rows, width), start, 0
        )
        value_buf = lax.dynamic_update_slice_in_dim(
            value_buf, value_part.reshape(block_rows, width), start, 0
        )
        return (query_acc, key_buf, value_buf)

    empty_parts = jnp.zeros((total_rows, width), jnp.bfloat16)
    query_acc, key_buf, value_buf = lax.fori_loop(
        0, own_block + 1, grad_pass, (query_init, empty_parts, empty_parts)
    )
    key_recv, value_recv = (
        lax.all_to_all(
            key_buf.reshape(seq_count, tok_rows, width),
            "seq",
            split_axis=0,
            concat_axis=0,
            tiled=True,
        ),
        lax.all_to_all(
            value_buf.reshape(seq_count, tok_rows, width),
            "seq",
            split_axis=0,
            concat_axis=0,
            tiled=True,
        ),
    )
    key_total = jnp.sum(key_recv.astype(jnp.float32), axis=0)
    value_total = jnp.sum(value_recv.astype(jnp.float32), axis=0)
    query_grad = (query_acc * score_scale).astype(jnp.bfloat16).reshape(tok_rows, width)
    key_grad = key_total.astype(jnp.bfloat16)
    d_value = value_total.astype(jnp.bfloat16)
    grad_term = jnp.dot(low_rank.T, d_value, preferred_element_type=jnp.float32) * inv_rank
    gradient = lax.psum_scatter(grad_term, "seq", scatter_dimension=0, tiled=True)
    new_first = BETA_ONE * first_moment + (1.0 - BETA_ONE) * gradient
    new_second = BETA_TWO * second_moment + (1.0 - BETA_TWO) * gradient * gradient
    direction = (
        new_first
        / (1.0 - BETA_ONE**STEP)
        / (jnp.sqrt(new_second / (1.0 - BETA_TWO**STEP)) + ADAM_EPSILON)
    )
    new_master = master - LEARN_RATE * (direction + WEIGHT_DECAY * master)
    return (query_grad, key_grad, new_master, new_first, new_second)


def solution(mesh):
    placed = (
        P("seq", "section"),
        P("section", None),
        P("seq", "section"),
        P("seq", "section"),
        P("seq", "section"),
        P("seq", "section"),
        P("seq", "section"),
        P("seq", "section"),
        P("seq", "section"),
    )
    return jax.shard_map(
        body,
        mesh=mesh,
        in_specs=placed,
        out_specs=(
            P("seq", "section"),
            P("seq", "section"),
            P("seq", "section"),
            P("seq", "section"),
            P("seq", "section"),
        ),
        check_vma=False,
    )
```

profile of v0, /device:TPU:1, one launch (start us, length us, event | category | flops | bytes accessed | tf_op | source)
XLA Modules:
  0.0 1797.8 jit_solution(1375697787501885071)
XLA Ops:
  7.2 0.0 copy-start
  7.2 0.0 all-gather.6.cloned.1.call-start
  7.2 0.8 copy-done
  8.1 1.1 fusion.17
  9.2 29.2 %psum.7 = bf16[128,128]{1,0:T(8,128)(2,1)S(1)} all-reduce(f32[128,128]{1,0:T(8,128)S(1)} %fusion.17), channel_id=1, replica_groups=mesh['seq'=64,'section'=8] {'section'}, use_global_device_ids=true, to_apply=%region_0.1 | all-reduce | flops 16384 | bytes 98304 | tf_op jit(solution)/shard_map/psum | solution.py:45
  38.3 0.7 convert_bitcast_fusion
  39.0 196.0 %all-gather = bf16[64,2,224]{2,1,0:T(2,128)(2,1)S(1)} all-gather(bf16[1,2,224]{2,1,0:T(2,128)(2,1)S(1)} %convert_bitcast_fusion), channel_id=1, replica_groups=mesh['seq'=64,'section'=8] {'seq'}, dimensions={0}, use_global_device_ids=true | all-gather | bytes 58240 | tf_op jit(solution)/shard_map/all_gather | solution.py:43
  235.0 0.1 reshape.111
  235.1 1.7 fusion.12
  236.8 0.0 all-gather.6.cloned.1.call-update
  236.8 0.0 all-gather.4.cloned.1.call-start
  236.8 0.7 all-gather.4.cloned.1.call-update
  237.6 179.7 %all-gather.6.cloned.1.call-done = bf16[8192,224]{0,1:T(8,128)(2,1)} async-done(((bf16[128,224]{0,1:T(8,128)(2,1)}), bf16[8192,224]{0,1:T(8,128)(2,1)}) %all-gather.6.cloned.1.call-update) | async-done | bytes 3670032 | tf_op jit(solution)/shard_map/all_gather | solution.py:52
  417.3 159.6 %all-gather.4.cloned.1.call-done = bf16[8192,224]{0,1:T(8,128)(2,1)} async-done(((bf16[128,224]{0,1:T(8,128)(2,1)}), bf16[8192,224]{0,1:T(8,128)(2,1)}) %all-gather.4.cloned.1.call-update) | async-done | bytes 3670032 | tf_op jit(solution)/shard_map/all_gather | solution.py:51
  576.8 3.8 broadcast_in_dim.31
  580.6 0.0 copy-start.1
  580.6 0.0 copy-start.2
  580.6 3.8 broadcast_in_dim.32
  584.4 0.0 copy-done.1
  584.4 0.0 copy-done.2
  584.4 3.4 while.28
  584.4 1.1 constant_dynamic-slice_fusion.13
  585.5 0.1 broadcast_compare_fusion.2
  585.6 1.1 fusion.61
  586.7 1.1 fusion.62
  587.8 4.5 reduce_max.9
  592.2 4.5 exponential_reduce_fusion
  596.7 7.1 multiply_reduce_fusion
  603.9 2.2 broadcast_in_dim.30
  606.1 2.3 broadcast_in_dim.30.clone
  608.4 5.3 while.27
  608.4 1.1 constant_dynamic-slice_fusion.12
  609.5 0.2 copy.104
  609.7 1.1 constant_dynamic-slice_fusion.11
  610.8 0.2 copy.103
  611.0 0.2 multiply_convert_fusion.3
  611.2 0.2 fusion.56
  611.4 0.3 convolution_convert_fusion.2
  611.7 0.8 constant_dynamic-update-slice_fusion.3
  612.5 1.0 constant_dynamic-slice_fusion.10
  613.5 0.2 fusion.55
  613.7 4.5 copy_bitcast_fusion
  618.2 139.8 %all-to-all-start.1 = ((bf16[64,128,224]{1,2,0:T(8,128)(2,1)}), bf16[64,128,224]{1,2,0:T(8,128)(2,1)}, u32[]{:S(2)}, u32[]{:S(2)}) async-start(bf16[64,128,224]{1,2,0:T(8,128)(2,1)} %copy_bitcast_fusion), calls=%async_computation.1 | async-start | bytes 7340032 | tf_op jit(solution)/shard_map/all_to_all | solution.py:133
  758.1 4.5 copy_bitcast_fusion.1
  762.5 151.5 %all-to-all-done.1 = bf16[64,128,224]{1,2,0:T(8,128)(2,1)} async-done(((bf16[64,128,224]{1,2,0:T(8,128)(2,1)}), bf16[64,128,224]{1,2,0:T(8,128)(2,1)}, u32[]{:S(2)}, u32[]{:S(2)}) %all-to-all-start.1) | async-done | bytes 3670048 | tf_op jit(solution)/shard_map/all_to_all | solution.py:133
  914.0 13.2 all-to-all-start
  927.3 0.0 all-reduce.3.cloned.1.call-start
  927.3 1.3 dynamic-slice
  929.3 0.0 copy-start.3
  929.3 0.0 copy-start.4
  929.3 0.0 copy-start.5
  929.3 2.6 reduce_sum.45
  931.9 0.8 convolution_multiply_fusion.2
  932.6 0.0 all-reduce.3.cloned.1.call-update
  932.7 0.6 multiply_convert_fusion.1
  933.3 157.5 %all-to-all-done = bf16[64,128,224]{1,2,0:T(8,128)(2,1)} async-done(((bf16[64,128,224]{1,2,0:T(8,128)(2,1)}), bf16[64,128,224]{1,2,0:T(8,128)(2,1)}, u32[]{:S(2)}, u32[]{:S(2)}) %all-to-all-start) | async-done | bytes 3670048 | tf_op jit(solution)/shard_map/all_to_all | solution.py:126
  1090.8 3.2 reduce_sum.44
  1094.0 695.6 %all-reduce.3.cloned.1.call-done = f32[128,224]{0,1:T(8,128)} async-done(((f32[128,224]{0,1:T(8,128)}), f32[128,224]{0,1:T(8,128)}) %all-reduce.3.cloned.1.call-update) | async-done | bytes 114704
  1789.6 1.0 constant_dynamic-slice_fusion.5
  1790.6 0.1 copy.88
  1790.6 0.0 copy-done.3
  1790.6 0.0 copy-done.4
  1790.6 0.0 copy-done.5
  1790.7 0.6 multiply_subtract_fusion
  (4 shorter events, 0.0 us)
Async XLA Ops:
  7.2 0.9 copy-start
  7.2 410.1 %all-gather.6.cloned.1.call-start = ((), (), s32[]{:S(2)}) async-start(), calls=%async_computation.3 | async-start | bytes 3727360 | tf_op jit(solution)/shard_map/all_gather | solution.py:52
  236.8 340.0 %all-gather.4.cloned.1.call-start = ((), (), s32[]{:S(2)}) async-start(), calls=%async_computation.2 | async-start | bytes 3727360 | tf_op jit(solution)/shard_map/all_gather | solution.py:51
  580.6 3.8 copy-start.1
  580.6 3.8 copy-start.2
  618.2 295.8 %all-to-all-start.1 = ((bf16[64,128,224]{1,2,0:T(8,128)(2,1)}), bf16[64,128,224]{1,2,0:T(8,128)(2,1)}, u32[]{:S(2)}, u32[]{:S(2)}) async-start(bf16[64,128,224]{1,2,0:T(8,128)(2,1)} %copy_bitcast_fusion), calls=%async_computation.1 | async-start | bytes 7340032 | tf_op jit(solution)/shard_map/all_to_all | solution.py:133
  914.0 176.8 %all-to-all-start = ((bf16[64,128,224]{1,2,0:T(8,128)(2,1)}), bf16[64,128,224]{1,2,0:T(8,128)(2,1)}, u32[]{:S(2)}, u32[]{:S(2)}) async-start(bf16[64,128,224]{1,2,0:T(8,128)(2,1)} %copy_bitcast_fusion.1), calls=%async_computation | async-start | bytes 7340032 | tf_op jit(solution)/shard_map/all_to_all | solution.py:126
  927.3 862.3 %all-reduce.3.cloned.1.call-start = ((), (), s32[]{:S(2)}) async-start(), calls=%async_computation.4 | async-start | bytes 229376
  929.3 861.4 %copy-start.3 = (f32[2,224]{1,0:T(2,128)S(1)}, f32[2,224]{1,0:T(2,128)}, u32[]{:S(2)}) copy-start(f32[2,224]{1,0:T(2,128)} %param.19) | copy-start | bytes 5380
  929.3 861.4 %copy-start.4 = (f32[2,224]{1,0:T(2,128)S(1)}, f32[2,224]{1,0:T(2,128)}, u32[]{:S(2)}) copy-start(f32[2,224]{1,0:T(2,128)} %param.20) | copy-start | bytes 5380
  929.3 861.4 %copy-start.5 = (f32[2,224]{1,0:T(2,128)S(1)}, f32[2,224]{1,0:T(2,128)}, u32[]{:S(2)}) copy-start(f32[2,224]{1,0:T(2,128)} %param.21) | copy-start | bytes 5380
Sparse Core Ops, SparseCore 0:
  236.9 180.3 all-gather.5
  421.2 155.5 all-gather.3
  932.8 856.7 all-reduce.2
where the time goes:
time: 1820 us; the launch traced here: 1800 us
  waiting for transfers between devices  1340 us (74%)
  blocking collectives  225 us (12%)
  starting transfers between devices  153 us (8%)
  local copies, waits for them, and re-layouts  29.7 us (2%)
  other arithmetic  24.1 us (1%)
    unnamed x4, waiting for transfers between devices  696 us
    all_gather x1, blocking collectives, body(): lax.all_gather(master.astype(jnp.bfloat16), 'seq', axis=0, tiled=True)  196 us
    all_gather x1, waiting for transfers between devices, body(): lax.all_gather(values, 'seq', axis=0, tiled=True)  180 us
    all_gather x1, waiting for transfers between devices, body(): lax.all_gather(key_rows, 'seq', axis=0, tiled=True)  160 us
    all_to_all x1, waiting for transfers between devices, body(): lax.all_to_all(key_buf.reshape(seq_count, tok_rows, width), 'seq', split_...  158 us
    all_to_all x1, waiting for transfers between devices, body(): lax.all_to_all(value_buf.reshape(seq_count, tok_rows, width), 'seq', spli...  152 us
    all_to_all x1, starting transfers between devices, body(): lax.all_to_all(value_buf.reshape(seq_count, tok_rows, width), 'seq', spli...  140 us
  transfers between devices with their start and end apart: 5, of which 5 were waited for; matrix products, arithmetic and copies ran while one was open for 1% of the time, Pallas kernels for 0%

commit v1 on v0

v1 whole, which is shorter than its diff:
```python
import math

import jax
import jax.numpy as jnp
from jax import lax
from jax.experimental import pallas as pl
from jax.experimental.pallas import tpu as pltpu
from jax.sharding import Mesh, PartitionSpec as P

HEAD = 112
LANES = 128
RANK = 128
STEP = 2

BETA_ONE = 0.9
BETA_TWO = 0.95
LEARN_RATE = 0.01
WEIGHT_DECAY = 0.1
ADAM_EPSILON = 1e-08
MASK_VALUE = -1e30
LOW_MAX = -1e20
SCORE_SCALE = 1.0 / math.sqrt(HEAD)
INV_RANK = 1.0 / math.sqrt(RANK)

BF = jnp.bfloat16
F32 = jnp.float32

TOK = 128
HALF = 64
N_Q = 1024
N_K = 2048
Q_STEP = 256
VMEM_LIMIT = 56 * 1024 * 1024

VMEM = pl.BlockSpec(memory_space=pltpu.VMEM)
SMEM = pl.BlockSpec(memory_space=pltpu.SMEM)


def call(kernel, shapes, specs, scratch=()):
    return pl.pallas_call(
        kernel,
        out_shape=[jax.ShapeDtypeStruct(s, d) for s, d in shapes],
        in_specs=specs,
        out_specs=[VMEM] * len(shapes),
        scratch_shapes=list(scratch),
        compiler_params=pltpu.CompilerParams(vmem_limit_bytes=VMEM_LIMIT),
    )


def dot_nt(a, b):
    return lax.dot_general(a, b, (((1,), (1,)), ((), ())), preferred_element_type=F32)


def dot_tn(a, b):
    return lax.dot_general(a, b, (((0,), (0,)), ((), ())), preferred_element_type=F32)


def rank_of(order):
    return (
        (order >> 5) * 32 + (order & 3) * 8 + ((order >> 3) & 3) * 2 + ((order >> 2) & 1)
    )


def pack_kernel(pos, x_ref, wd_ref, q_ref, do_ref, k_ref, vb_ref, part_ref, keep_ref, send_ref):
    core = pos[4]
    part = jnp.dot(x_ref[...], wd_ref[...], preferred_element_type=F32)
    for s in range(8):
        h = s % 2
        part_ref[s] = part[h * HALF : (h + 1) * HALF]
    keep_ref[...] = jnp.zeros_like(keep_ref)
    send_ref[...] = jnp.zeros_like(send_ref)
    own = pl.ds(pl.multiple_of(core * HALF, HALF), HALF)
    other = pl.ds(pl.multiple_of((1 - core) * HALF, HALF), HALF)
    for i, ref in enumerate((q_ref, do_ref, k_ref, vb_ref)):
        for rows, out in ((own, keep_ref), (other, send_ref)):
            tile = ref[rows, :]
            for h in range(2):
                out[h, :, i * LANES : i * LANES + HEAD] = tile[:, h * HEAD : (h + 1) * HEAD]


def route_kernel(pos, part_ref, keep_ref, recv_ref, out_ref):
    core = pos[4]
    total = part_ref[0]
    for s in range(1, 8):
        total = total + part_ref[s]
    src = lax.broadcasted_iota(jnp.int32, (RANK, RANK), 0)
    dst = lax.broadcasted_iota(jnp.int32, (RANK, RANK), 1)
    order = jnp.where(src == rank_of(dst), 1.0, 0.0).astype(BF)
    low = jnp.dot(total.astype(BF), order, preferred_element_type=F32).astype(BF)
    for j in range(4):
        out_ref[j, :, 512:640] = low
    for h in range(2):
        out_ref[core * 2 + h, :, 0:512] = keep_ref[h]
        out_ref[(1 - core) * 2 + h, :, 0:512] = recv_ref[h]


def token_ids(pos):
    y, x, core = pos[0], pos[2], pos[4]
    n = lax.broadcasted_iota(jnp.int32, (1, N_Q), 1)
    q_tok = y * 2048 + ((n >> 6) & 3) * 512 + (n >> 8) * 128 + core * HALF + (n & 63)
    m = lax.broadcasted_iota(jnp.int32, (N_K, 1), 0)
    half = (m >> 10) ^ core
    k_tok = ((m >> 8) & 3) * 2048 + ((m >> 6) & 3) * 512 + x * 128 + half * HALF + (m & 63)
    return q_tok, k_tok


def first_kernel(pos, q_ref, own_ref, other_ref, w_ref, stat_ref, v_ref):
    dst = lax.broadcasted_iota(jnp.int32, (RANK, RANK), 0)
    src = lax.broadcasted_iota(jnp.int32, (RANK, RANK), 1)
    order = jnp.where(src == rank_of(dst), 1.0, 0.0).astype(BF)
    w_up = jnp.dot(order, w_ref[...], preferred_element_type=F32).astype(BF)
    for h, ref in enumerate((own_ref, other_ref)):
        add = jnp.dot(ref[:, 256:384], w_up, preferred_element_type=F32) * INV_RANK
        v_ref[h * 1024 : (h + 1) * 1024] = (ref[:, 128:256].astype(F32) + add).astype(BF)
    q_tok, k_tok = token_ids(pos)
    keys = jnp.concatenate([own_ref[:, 0:128], other_ref[:, 0:128]], axis=0)
    values = v_ref[...]
    for s in range(N_Q // Q_STEP):
        cols = slice(s * Q_STEP, (s + 1) * Q_STEP)
        scores = dot_nt(keys, q_ref[cols, 0:128]) * SCORE_SCALE
        scores = jnp.where(k_tok <= q_tok[:, cols], scores, MASK_VALUE)
        top = jnp.maximum(jnp.max(scores, axis=0, keepdims=True), LOW_MAX)
        weight = jnp.exp(scores - top)
        total = jnp.sum(weight, axis=0, keepdims=True)
        d_prob = dot_nt(values, q_ref[cols, 128:256])
        delta = jnp.sum(weight * d_prob, axis=0, keepdims=True)
        some = total > 0.0
        safe = jnp.where(some, total, 1.0)
        stat_ref[0:1, cols] = jnp.where(some, top + jnp.log(safe), MASK_VALUE)
        stat_ref[1:2, cols] = delta / safe
    stat_ref[2:8, :] = jnp.zeros((6, N_Q), F32)


def second_kernel(pos, q_ref, own_ref, other_ref, v_ref, stat_ref,
                  dq_ref, keep_ref, send_ref, grad_ref, dk_acc, dv_acc):
    q_tok, k_tok = token_ids(pos)
    keys = jnp.concatenate([own_ref[:, 0:128], other_ref[:, 0:128]], axis=0)
    low = jnp.concatenate([own_ref[:, 256:384], other_ref[:, 256:384]], axis=0)
    values = v_ref[...]
    for s in range(N_Q // Q_STEP):
        cols = slice(s * Q_STEP, (s + 1) * Q_STEP)
        lse = [stat_ref[i, 0:1, cols] for i in range(4)]
        top = jnp.maximum(jnp.maximum(lse[0], lse[1]), jnp.maximum(lse[2], lse[3]))
        share = [jnp.exp(l - top) for l in lse]
        total = share[0] + share[1] + share[2] + share[3]
        delta = sum(share[i] * stat_ref[i, 1:2, cols] for i in range(4)) / total
        log_total = top + jnp.log(total)
        queries, cotan = q_ref[cols, 0:128], q_ref[cols, 128:256]
        scores = dot_nt(keys, queries) * SCORE_SCALE
        scores = jnp.where(k_tok <= q_tok[:, cols], scores, MASK_VALUE)
        prob = jnp.exp(scores - log_total)
        d_prob = dot_nt(values, cotan)
        d_score = (prob * (d_prob - delta)).astype(BF)
        d_key = jnp.dot(d_score, queries, preferred_element_type=F32)
        d_val = jnp.dot(prob.astype(BF), cotan, preferred_element_type=F32)
        if s == 0:
            dk_acc[...] = d_key
            dv_acc[...] = d_val
        else:
            dk_acc[...] += d_key
            dv_acc[...] += d_val
        dq_ref[cols, :] = (dot_tn(d_score, keys) * SCORE_SCALE).astype(BF)
    keep_ref[...] = (dk_acc[0:1024] * SCORE_SCALE)
    send_ref[...] = (dk_acc[1024:2048] * SCORE_SCALE).astype(BF)
    grad_ref[...] = dot_tn(low, dv_acc[...].astype(BF)) * INV_RANK


def sums_kernel(dq_ref, dk_ref, grad_ref, out_ref):
    dq = dq_ref[0].astype(F32)
    dk = dk_ref[0].astype(F32)
    for i in range(1, 4):
        dq = dq + dq_ref[i].astype(F32)
        dk = dk + dk_ref[i].astype(F32)
    grad = grad_ref[0]
    for i in range(1, 32):
        grad = grad + grad_ref[i]
    high = grad.astype(BF)
    rest = (grad - high.astype(F32)).astype(BF)
    for z in range(4):
        rows = slice(z * HALF, (z + 1) * HALF)
        out_ref[z, 0:HALF, 0:128] = dq[rows].astype(BF)
        out_ref[z, 0:HALF, 128:256] = dk[rows].astype(BF)
        out_ref[z, HALF : HALF + 16, 0:128] = jnp.broadcast_to(high[z : z + 1], (16, 128))
        out_ref[z, HALF : HALF + 16, 128:256] = jnp.broadcast_to(rest[z : z + 1], (16, 128))


def last_kernel(pos, keep_ref, recv_ref, master_ref, first_ref, second_ref,
                qg_ref, kg_ref, nm_ref, nf_ref, ns_ref):
    core = pos[4]
    for rows, ref in ((core, keep_ref), (1 - core, recv_ref)):
        at = pl.ds(pl.multiple_of(rows * HALF, HALF), HALF)
        for out, lane in ((qg_ref, 0), (kg_ref, 128)):
            tile = jnp.concatenate(
                [ref[h, 0:HALF, lane : lane + HEAD] for h in range(2)], axis=1
            )
            out[at, :] = tile
    halves = []
    for ref in (keep_ref, recv_ref):
        halves.append(jnp.concatenate(
            [
                ref[h, HALF : HALF + 1, 0:HEAD].astype(F32)
                + ref[h, HALF : HALF + 1, 128 : 128 + HEAD].astype(F32)
                for h in range(2)
            ],
            axis=1,
        ))
    row = lax.broadcasted_iota(jnp.int32, (2, 2 * HEAD), 0)
    gradient = jnp.where(row == core, halves[0], halves[1])
    master = master_ref[...]
    new_first = BETA_ONE * first_ref[...] + (1.0 - BETA_ONE) * gradient
    new_second = BETA_TWO * second_ref[...] + (1.0 - BETA_TWO) * gradient * gradient
    direction = (
        new_first
        / (1.0 - BETA_ONE**STEP)
        / (jnp.sqrt(new_second / (1.0 - BETA_TWO**STEP)) + ADAM_EPSILON)
    )
    nm_ref[...] = master - LEARN_RATE * (direction + WEIGHT_DECAY * master)
    nf_ref[...] = new_first
    ns_ref[...] = new_second


def exchange(value, axes):
    return lax.all_to_all(value, axes, split_axis=0, concat_axis=0, tiled=True)


def swap(value):
    return lax.ppermute(value, "core", [(0, 1), (1, 0)])


def copies(value, count):
    return jnp.broadcast_to(value[None], (count, *value.shape)).reshape(
        count * value.shape[0], *value.shape[1:]
    )


def body(normed, w_down, query, key, value_base, cotangent, master, first, second):
    core = lax.axis_index("core")
    pos = jnp.stack([lax.axis_index(a) for a in ("y", "zh", "x", "zl", "core")]).astype(jnp.int32)

    rows = lax.all_gather(master.astype(BF), "core", axis=0)
    rows = rows.reshape(2, 2, 2, HEAD).transpose(0, 2, 1, 3).reshape(4, 2, HEAD)
    rows = jnp.pad(rows, ((0, 0), (0, 0), (0, LANES - HEAD)))
    rows = jnp.broadcast_to(rows[None, :, None], (4, 4, 4, 2, LANES)).reshape(64, 2, LANES)
    w_up = exchange(rows, ("y", "zh", "x")).reshape(RANK, LANES)

    part, keep, send = call(
        pack_kernel,
        [((8, HALF, RANK), F32), ((2, HALF, 512), BF), ((2, HALF, 512), BF)],
        [SMEM] + [VMEM] * 6,
    )(pos, normed, w_down, query, cotangent, key, value_base)
    part = exchange(part, ("zl", "core"))
    recv = swap(send)
    (pieces,) = call(route_kernel, [((4, HALF, 640), BF)], [SMEM] + [VMEM] * 3)(
        pos, part, keep, recv
    )
    pieces = exchange(pieces, "zh").reshape(256, 640)
    q_tile = exchange(copies(pieces[:, 0:256], 4), "x")
    k_own = exchange(copies(pieces[:, 256:640], 4), "y")
    k_other = swap(k_own)

    stat, values = call(
        first_kernel, [((8, N_Q), F32), ((N_K, LANES), BF)], [SMEM] + [VMEM] * 4
    )(pos, q_tile, k_own, k_other, w_up)
    stats = exchange(jnp.broadcast_to(stat[None], (4, 8, N_Q)), "x")
    dq, dk_keep, dk_send, grad = call(
        second_kernel,
        [((N_Q, LANES), BF), ((1024, LANES), F32), ((1024, LANES), BF), ((RANK, LANES), F32)],
        [SMEM] + [VMEM] * 5,
        [pltpu.VMEM((N_K, LANES), F32)] * 2,
    )(pos, q_tile, k_own, k_other, values, stats)
    dq = exchange(dq.reshape(4, 256, LANES), "x")
    dk = (dk_keep + swap(dk_send).astype(F32)).astype(BF)
    dk = exchange(dk.reshape(4, 256, LANES), "y")
    grad = exchange(grad.reshape(32, 4, LANES), ("y", "x", "core"))
    (back,) = call(sums_kernel, [((4, HALF + 16, 256), BF)], [VMEM] * 3)(dq, dk, grad)
    back = exchange(back, "zh")
    keep = lax.dynamic_slice_in_dim(back, core * 2, 2, 0)
    recv = swap(lax.dynamic_slice_in_dim(back, (1 - core) * 2, 2, 0))
    return tuple(call(
        last_kernel,
        [((TOK, 2 * HEAD), BF)] * 2 + [((2, 2 * HEAD), F32)] * 3,
        [SMEM] + [VMEM] * 5,
    )(pos, keep, recv, master, first, second))


def solution(mesh):
    fine = Mesh(mesh.devices.reshape(4, 4, 4, 4, 2), ("y", "zh", "x", "zl", "core"))
    seq, section = ("y", "zh", "x"), ("zl", "core")
    split = P(seq, section)
    return jax.shard_map(
        body,
        mesh=fine,
        in_specs=(split, P(section, None)) + (split,) * 7,
        out_specs=(split,) * 5,
        check_vma=False,
    )
```

time: 1820 us -> 208 us (0.11); the launches traced: 1800 us -> 207 us
  waiting for transfers between devices: 1340 us -> 44.8 us
  blocking collectives: 225 us -> 72.9 us
  starting transfers between devices: 153 us -> 51.1 us
  other arithmetic: 24.1 us -> 0.07 us
  Pallas kernels: 0 us -> 23 us
    unnamed x4 -> x0, waiting for transfers between devices: 696 us -> none
    all_gather x2 -> x0, waiting for transfers between devices: 339 us -> none  [the longest x1 180 us: body(): lax.all_gather(values, 'seq', axis=0, tiled=True)]
    all_to_all x2 -> x5, waiting for transfers between devices: 309 us -> 42.7 us  [exchange(): return lax.all_to_all(value, axes, split_axis=0, concat_axis=0, tiled=True)]
    all_gather x1, blocking collectives: 196 us -> 6.16 us  [body(): rows = lax.all_gather(master.astype(BF), 'core', axis=0)]
    all_to_all x2 -> x5, starting transfers between devices: 153 us -> 31.1 us  [exchange(): return lax.all_to_all(value, axes, split_axis=0, concat_axis=0, tiled=True)]
    all_to_all x0 -> x5, blocking collectives: none -> 66.8 us  [exchange(): return lax.all_to_all(value, axes, split_axis=0, concat_axis=0, tiled=True)]
    psum x1 -> x0, blocking collectives: 29.2 us -> none  [body(): low_rank = lax.psum(partial_rank, 'section').astype(jnp.bfloat16)]
    pallas_call x0 -> x6, Pallas kernels: none -> 23 us  [the longest x1 8.72 us: body(): call(second_kernel, [((N_Q, LANES), BF), ((1024, LANES), F32), ((1024, LA...]
  transfers between devices with their start and end apart: 5 -> 9, of which waited for: 5 -> 7; matrix products, arithmetic and copies ran while one was open for 1% -> 0% of each run, Pallas kernels for 0% -> 0%
where the time goes in v1:
time: 208 us; the launch traced here: 207 us
  blocking collectives  72.9 us (35%)
  starting transfers between devices  51.1 us (25%)
  waiting for transfers between devices  44.8 us (22%)
  Pallas kernels  23 us (11%)
  local copies, waits for them, and re-layouts  13.8 us (7%)
    all_to_all x5, blocking collectives, exchange(): return lax.all_to_all(value, axes, split_axis=0, concat_axis=0, tiled=True)  66.8 us
    all_to_all x5, waiting for transfers between devices, exchange(): return lax.all_to_all(value, axes, split_axis=0, concat_axis=0, tiled=True)  42.7 us
    all_to_all x5, starting transfers between devices, exchange(): return lax.all_to_all(value, axes, split_axis=0, concat_axis=0, tiled=True)  31.1 us
    ppermute x4, starting transfers between devices, swap(): return lax.ppermute(value, 'core', [(0, 1), (1, 0)])  20.1 us
    pallas_call x1, Pallas kernels, body(): call(second_kernel, [((N_Q, LANES), BF), ((1024, LANES), F32), ((1024, LA...  8.72 us
    unnamed x35, local copies, waits for them, and re-layouts  7.7 us
    pallas_call x1, Pallas kernels, body(): call(first_kernel, [((8, N_Q), F32), ((N_K, LANES), BF)], [SMEM] + [VMEM]...  6.81 us
    all_gather x1, blocking collectives, body(): rows = lax.all_gather(master.astype(BF), 'core', axis=0)  6.16 us
  transfers between devices with their start and end apart: 9, of which 7 were waited for; matrix products, arithmetic and copies ran while one was open for 0% of the time, Pallas kernels for 0%

profile of v1, /device:TPU:1, one launch (start us, length us, event | category | flops | bytes accessed | tf_op | source)
XLA Modules:
  0.0 206.5 jit_solution(8461147022990490968)
XLA Ops:
  0.6 0.0 copy-start.9
  0.6 1.7 copy.21.x_ref
  2.3 0.0 copy-done.9
  2.3 0.0 copy-start.10
  2.3 0.7 copy.22.q_ref
  3.1 0.1 copy-done.10
  3.1 0.0 copy-start.11
  3.1 0.7 copy.23.do_ref
  3.9 0.1 copy-done.11
  4.0 0.0 copy-start.12
  4.0 0.7 copy.24.k_ref
  4.7 0.1 copy-done.12
  4.8 0.7 copy.25.vb_ref
  5.5 0.6 stack.23.pos
  6.1 2.0 shard_map.128
  8.1 0.0 copy-start.14
  8.1 10.3 %all-to-all-start = ((f32[8,64,128]{2,1,0:T(8,128)}), f32[8,64,128]{2,1,0:T(8,128)S(1)}, u32[]{:S(2)}, u32[]{:S(2)}) async-start(f32[8,64,128]{2,1,0:T(8,128)} %get-tuple-element.14), calls=%async_computation | async-start | bytes 524288 | tf_op jit(solution)/shard_map/all_to_all | solution.py:223
  18.5 0.0 copy-done.14
  18.5 2.0 collective-permute-start
  20.5 1.2 collective-permute-done.recv_ref
  21.7 5.5 %all-to-all-done.part_ref = f32[8,64,128]{2,1,0:T(8,128)S(1)} async-done(((f32[8,64,128]{2,1,0:T(8,128)}), f32[8,64,128]{2,1,0:T(8,128)S(1)}, u32[]{:S(2)}, u32[]{:S(2)}) %all-to-all-start) | async-done | bytes 262176 | tf_op jit(solution)/shard_map/all_to_all | solution.py:223
  27.2 0.0 copy-done.6
  27.2 0.7 copy-done.3
  27.9 2.0 shard_map.129
  29.8 27.8 %all_to_all.56 = bf16[4,64,640]{2,1,0:T(8,128)(2,1)S(1)} all-to-all(bf16[4,64,640]{2,1,0:T(8,128)(2,1)} %shard_map.129), channel_id=1, replica_groups=mesh['y'=4,'zh'=4,'x'=4,'zl'=4,'core'=2] {'zh'}, dimensions={0} | all-to-all | bytes 655360 | tf_op jit(solution)/shard_map/all_to_all | solution.py:223
  57.7 1.0 broadcast_in_dim.9
  58.6 4.3 %all-to-all-start.3 = ((bf16[4,256,384]{2,1,0:T(8,128)(2,1)}), bf16[4,256,384]{2,1,0:T(8,128)(2,1)S(1)}, u32[]{:S(2)}, u32[]{:S(2)}) async-start(bf16[4,256,384]{2,1,0:T(8,128)(2,1)} %broadcast_in_dim.9), calls=%async_computation.3 | async-start | bytes 1572864 | tf_op jit(solution)/shard_map/all_to_all | solution.py:223
  63.0 0.0 copy-done.13
  63.0 6.2 %all-gather.1 = bf16[2,2,224]{2,1,0:T(2,128)(2,1)S(1)} all-gather(bf16[1,2,224]{2,1,0:T(2,128)(2,1)S(1)} %convert_bitcast_fusion), channel_id=2, replica_groups=mesh['y'=4,'zh'=4,'x'=4,'zl'=4,'core'=2] {'core'}, dimensions={0}, use_global_device_ids=true | all-gather | bytes 2688 | tf_op jit(solution)/shard_map/all_gather | solution.py:240
  69.1 2.2 %all-to-all-done.3 = bf16[4,256,384]{2,1,0:T(8,128)(2,1)S(1)} async-done(((bf16[4,256,384]{2,1,0:T(8,128)(2,1)}), bf16[4,256,384]{2,1,0:T(8,128)(2,1)S(1)}, u32[]{:S(2)}, u32[]{:S(2)}) %all-to-all-start.3) | async-done | bytes 786464 | tf_op jit(solution)/shard_map/all_to_all | solution.py:223
  71.3 7.7 %collective-permute-start.1 = (bf16[1024,384]{1,0:T(8,128)(2,1)S(1)}, bf16[1024,384]{1,0:T(8,128)(2,1)S(1)}, u32[]{:S(2)}, u32[]{:S(2)}) collective-permute-start(bf16[1024,384]{1,0:T(8,128)(2,1)S(1)} %bitcast.16), channel_id=1, source_target_pairs={{0,1},{1,0},{2,3},{3,2},{4,5},{5,4},{6,7},{7,6},{8,9},{9,8},{10,11... | collective-permute-start | bytes 2359304 | tf_op jit(solution)/shard_map/ppermute | solution.py:227
  79.0 0.1 fusion
  79.2 0.6 broadcast_in_dim.10
  79.8 9.7 %all-to-all-start.4 = ((bf16[64,2,128]{2,1,0:T(2,128)(2,1)}), bf16[64,2,128]{2,1,0:T(2,128)(2,1)S(1)}, u32[]{:S(2)}, u32[]{:S(2)}) async-start(bf16[64,2,128]{2,1,0:T(2,128)(2,1)} %bitcast.10), calls=%async_computation.4 | async-start | bytes 65536 | tf_op jit(solution)/shard_map/all_to_all | solution.py:223
  89.5 15.5 %all-to-all-done.4 = bf16[64,2,128]{2,1,0:T(2,128)(2,1)S(1)} async-done(((bf16[64,2,128]{2,1,0:T(2,128)(2,1)}), bf16[64,2,128]{2,1,0:T(2,128)(2,1)S(1)}, u32[]{:S(2)}, u32[]{:S(2)}) %all-to-all-start.4) | async-done | bytes 32800 | tf_op jit(solution)/shard_map/all_to_all | solution.py:223
  105.0 0.6 copy-done.5
  105.6 10.9 %all_to_all.57 = bf16[4,256,256]{2,1,0:T(8,128)(2,1)} all-to-all(bf16[4,256,256]{2,1,0:T(8,128)(2,1)S(1)} %broadcast_in_dim.8), channel_id=1, replica_groups=mesh['y'=4,'zh'=4,'x'=4,'zl'=4,'core'=2] {'x'}, dimensions={0} | all-to-all | bytes 1048576 | tf_op jit(solution)/shard_map/all_to_all | solution.py:223
  116.5 0.0 copy-done
  116.5 0.0 collective-permute-done.1.other_ref
  116.5 0.9 copy-done.1
  117.4 6.8 %shard_map.130 = (f32[8,1024]{1,0:T(8,128)}, bf16[2048,128]{1,0:T(8,128)(2,1)}) custom-call(s32[5]{0:T(128)} %stack.23.pos, bf16[1024,256]{1,0:T(8,128)(2,1)} %bitcast.19, bf16[1024,384]{1,0:T(8,128)(2,1)} %bitcast.17, bf16[1024,384]{1,0:T(8,128)(2,1)} %copy-done.1, bf16[128,128]{1,0:T(8,128)(2,1)} %bitcast.25), custom_call_target="tpu_custom_call" | custom-call | tf_op jit(solution)/shard_map/pallas_call | solution.py:261
  124.2 0.8 broadcast_in_dim.11
  125.0 7.9 %all_to_all.58.stat_ref = f32[4,8,1024]{2,1,0:T(8,128)} all-to-all(f32[4,8,1024]{2,1,0:T(8,128)S(1)} %broadcast_in_dim.11), channel_id=1, replica_groups=mesh['y'=4,'zh'=4,'x'=4,'zl'=4,'core'=2] {'x'}, dimensions={0} | all-to-all | bytes 262144 | tf_op jit(solution)/shard_map/all_to_all | solution.py:223
  132.9 8.7 %shard_map.131 = (bf16[1024,128]{1,0:T(8,128)(2,1)}, f32[1024,128]{1,0:T(8,128)}, bf16[1024,128]{1,0:T(8,128)(2,1)}, f32[128,128]{1,0:T(8,128)}) custom-call(s32[5]{0:T(128)} %stack.23.pos, bf16[1024,256]{1,0:T(8,128)(2,1)} %bitcast.20, bf16[1024,384]{1,0:T(8,128)(2,1)} %bitcast.18, bf16[1024,384]{1,0:T(8,128)(2,1)} %copy-done.1, ...), custom_call_target="tpu_custom_call" | custom-call | tf_op jit(solution)/shard_map/pallas_call | solution.py:265
  141.6 5.8 %collective-permute-start.2 = (bf16[1024,128]{1,0:T(8,128)(2,1)}, bf16[1024,128]{1,0:T(8,128)(2,1)S(1)}, u32[]{:S(2)}, u32[]{:S(2)}) collective-permute-start(bf16[1024,128]{1,0:T(8,128)(2,1)} %get-tuple-element.21), channel_id=1, source_target_pairs={{0,1},{1,0},{2,3},{3,2},{4,5},{5,4},{6,7},{7,6},{8,9},{9,8},{10,11... | collective-permute-start | bytes 786440 | tf_op jit(solution)/shard_map/ppermute | solution.py:227
  147.4 11.6 %all_to_all.59.grad_ref = f32[32,4,128]{2,1,0:T(4,128)} all-to-all(f32[32,4,128]{2,1,0:T(4,128)} %bitcast.26), channel_id=1, replica_groups=mesh['y'=4,'zh'=4,'x'=4,'zl'=4,'core'=2] {'y','x','core'}, dimensions={0} | all-to-all | bytes 131072 | tf_op jit(solution)/shard_map/all_to_all | solution.py:223
  159.1 3.4 %all-to-all-start.6 = ((bf16[4,256,128]{2,1,0:T(8,128)(2,1)}), bf16[4,256,128]{2,1,0:T(8,128)(2,1)S(1)}, u32[]{:S(2)}, u32[]{:S(2)}) async-start(bf16[4,256,128]{2,1,0:T(8,128)(2,1)} %bitcast.24), calls=%async_computation.6 | async-start | bytes 524288 | tf_op jit(solution)/shard_map/all_to_all | solution.py:223
  162.5 0.0 collective-permute-done.2
  162.5 0.0 copy-done.4
  162.5 0.1 add_convert_fusion
  162.6 6.0 %all-to-all-done.6.dq_ref = bf16[4,256,128]{2,1,0:T(8,128)(2,1)S(1)} async-done(((bf16[4,256,128]{2,1,0:T(8,128)(2,1)}), bf16[4,256,128]{2,1,0:T(8,128)(2,1)S(1)}, u32[]{:S(2)}, u32[]{:S(2)}) %all-to-all-start.6) | async-done | bytes 262176 | tf_op jit(solution)/shard_map/all_to_all | solution.py:223
  168.5 8.6 %all_to_all.60.dk_ref = bf16[4,256,128]{2,1,0:T(8,128)(2,1)} all-to-all(bf16[4,256,128]{2,1,0:T(8,128)(2,1)S(1)} %bitcast.23), channel_id=1, replica_groups=mesh['y'=4,'zh'=4,'x'=4,'zl'=4,'core'=2] {'y'}, dimensions={0} | all-to-all | bytes 524288 | tf_op jit(solution)/shard_map/all_to_all | solution.py:223
  177.1 0.0 copy-done.2
  177.1 1.8 shard_map.132
  178.9 3.3 %all-to-all-start.9 = ((bf16[4,80,256]{2,1,0:T(8,128)(2,1)}), bf16[4,80,256]{2,1,0:T(8,128)(2,1)S(1)}, u32[]{:S(2)}, u32[]{:S(2)}) async-start(bf16[4,80,256]{2,1,0:T(8,128)(2,1)} %shard_map.132), calls=%async_computation.9 | async-start | bytes 327680 | tf_op jit(solution)/shard_map/all_to_all | solution.py:223
  182.3 13.5 %all-to-all-done.9 = bf16[4,80,256]{2,1,0:T(8,128)(2,1)S(1)} async-done(((bf16[4,80,256]{2,1,0:T(8,128)(2,1)}), bf16[4,80,256]{2,1,0:T(8,128)(2,1)S(1)}, u32[]{:S(2)}, u32[]{:S(2)}) %all-to-all-start.9) | async-done | bytes 163872 | tf_op jit(solution)/shard_map/all_to_all | solution.py:223
  195.8 0.6 constant_dynamic-slice_fusion
  196.4 4.5 %collective-permute-start.3 = (bf16[2,80,256]{2,1,0:T(8,128)(2,1)S(1)}, bf16[2,80,256]{2,1,0:T(8,128)(2,1)S(1)}, u32[]{:S(2)}, u32[]{:S(2)}) collective-permute-start(bf16[2,80,256]{2,1,0:T(8,128)(2,1)S(1)} %get-tuple-element.33), channel_id=1, source_target_pairs={{0,1},{1,0},{2,3},{3,2},{4,5},{5,4},{6,7},{7,6},{8,9},{9,8},{10,11... | collective-permute-start | bytes 245768 | tf_op jit(solution)/shard_map/ppermute | solution.py:227
  201.0 0.9 collective-permute-done.3.recv_ref
  201.9 0.6 copy-done.7
  202.5 1.7 shard_map.133
  204.2 1.6 copy.26
  205.8 0.0 copy-done.8
  205.8 0.7 copy.27
  (16 shorter events, 0.1 us)
Async XLA Ops:
  0.6 1.7 copy-start.9
  2.3 0.8 copy-start.10
  3.1 0.8 copy-start.11
  4.0 0.8 copy-start.12
  8.1 10.3 %copy-start.14 = (bf16[2,64,512]{2,1,0:T(8,128)(2,1)S(1)}, bf16[2,64,512]{2,1,0:T(8,128)(2,1)}, u32[]{:S(2)}) copy-start(bf16[2,64,512]{2,1,0:T(8,128)(2,1)} %get-tuple-element.16) | copy-start | bytes 393220
  8.1 19.0 %all-to-all-start = ((f32[8,64,128]{2,1,0:T(8,128)}), f32[8,64,128]{2,1,0:T(8,128)S(1)}, u32[]{:S(2)}, u32[]{:S(2)}) async-start(f32[8,64,128]{2,1,0:T(8,128)} %get-tuple-element.14), calls=%async_computation | async-start | bytes 524288 | tf_op jit(solution)/shard_map/all_to_all | solution.py:223
  18.5 3.2 %collective-permute-start = (bf16[2,64,512]{2,1,0:T(8,128)(2,1)S(1)}, bf16[2,64,512]{2,1,0:T(8,128)(2,1)S(1)}, u32[]{:S(2)}, u32[]{:S(2)}) collective-permute-start(bf16[2,64,512]{2,1,0:T(8,128)(2,1)S(1)} %copy-done.14), channel_id=1, source_target_pairs={{0,1},{1,0},{2,3},{3,2},{4,5},{5,4},{6,7},{7,6},{8,9},{9,8},{10,11... | collective-permute-start | bytes 393224 | tf_op jit(solution)/shard_map/ppermute | solution.py:227
  21.7 5.5 %copy-start.6 = (bf16[2,64,512]{2,1,0:T(8,128)(2,1)}, bf16[2,64,512]{2,1,0:T(8,128)(2,1)S(1)}, u32[]{:S(2)}) copy-start(bf16[2,64,512]{2,1,0:T(8,128)(2,1)S(1)} %collective-permute-done.recv_ref) | copy-start | bytes 393220
  27.2 0.7 copy-start.3
  58.6 4.3 %copy-start.13 = (f32[2,224]{1,0:T(2,128)S(1)}, f32[2,224]{1,0:T(2,128)}, u32[]{:S(2)}) copy-start(f32[2,224]{1,0:T(2,128)} %master_ref.1) | copy-start | bytes 5380
  58.6 12.7 %all-to-all-start.3 = ((bf16[4,256,384]{2,1,0:T(8,128)(2,1)}), bf16[4,256,384]{2,1,0:T(8,128)(2,1)S(1)}, u32[]{:S(2)}, u32[]{:S(2)}) async-start(bf16[4,256,384]{2,1,0:T(8,128)(2,1)} %broadcast_in_dim.9), calls=%async_computation.3 | async-start | bytes 1572864 | tf_op jit(solution)/shard_map/all_to_all | solution.py:223
  71.3 45.2 %copy-start = (bf16[4,256,384]{2,1,0:T(8,128)(2,1)}, bf16[4,256,384]{2,1,0:T(8,128)(2,1)S(1)}, u32[]{:S(2)}) copy-start(bf16[4,256,384]{2,1,0:T(8,128)(2,1)S(1)} %all-to-all-done.3) | copy-start | bytes 2359300
  71.3 45.2 %collective-permute-start.1 = (bf16[1024,384]{1,0:T(8,128)(2,1)S(1)}, bf16[1024,384]{1,0:T(8,128)(2,1)S(1)}, u32[]{:S(2)}, u32[]{:S(2)}) collective-permute-start(bf16[1024,384]{1,0:T(8,128)(2,1)S(1)} %bitcast.16), channel_id=1, source_target_pairs={{0,1},{1,0},{2,3},{3,2},{4,5},{5,4},{6,7},{7,6},{8,9},{9,8},{10,11... | collective-permute-start | bytes 2359304 | tf_op jit(solution)/shard_map/ppermute | solution.py:227
  79.8 25.2 %all-to-all-start.4 = ((bf16[64,2,128]{2,1,0:T(2,128)(2,1)}), bf16[64,2,128]{2,1,0:T(2,128)(2,1)S(1)}, u32[]{:S(2)}, u32[]{:S(2)}) async-start(bf16[64,2,128]{2,1,0:T(2,128)(2,1)} %bitcast.10), calls=%async_computation.4 | async-start | bytes 65536 | tf_op jit(solution)/shard_map/all_to_all | solution.py:223
  105.0 0.6 copy-start.5
  116.5 0.9 copy-start.1
  141.6 20.9 %copy-start.4 = (f32[1024,128]{1,0:T(8,128)S(1)}, f32[1024,128]{1,0:T(8,128)}, u32[]{:S(2)}) copy-start(f32[1024,128]{1,0:T(8,128)} %get-tuple-element.20) | copy-start | bytes 1572868
  141.6 20.9 %collective-permute-start.2 = (bf16[1024,128]{1,0:T(8,128)(2,1)}, bf16[1024,128]{1,0:T(8,128)(2,1)S(1)}, u32[]{:S(2)}, u32[]{:S(2)}) collective-permute-start(bf16[1024,128]{1,0:T(8,128)(2,1)} %get-tuple-element.21), channel_id=1, source_target_pairs={{0,1},{1,0},{2,3},{3,2},{4,5},{5,4},{6,7},{7,6},{8,9},{9,8},{10,11... | collective-permute-start | bytes 786440 | tf_op jit(solution)/shard_map/ppermute | solution.py:227
  159.1 9.5 %all-to-all-start.6 = ((bf16[4,256,128]{2,1,0:T(8,128)(2,1)}), bf16[4,256,128]{2,1,0:T(8,128)(2,1)S(1)}, u32[]{:S(2)}, u32[]{:S(2)}) async-start(bf16[4,256,128]{2,1,0:T(8,128)(2,1)} %bitcast.24), calls=%async_computation.6 | async-start | bytes 524288 | tf_op jit(solution)/shard_map/all_to_all | solution.py:223
  168.5 8.6 %copy-start.2 = (bf16[4,256,128]{2,1,0:T(8,128)(2,1)}, bf16[4,256,128]{2,1,0:T(8,128)(2,1)S(1)}, u32[]{:S(2)}) copy-start(bf16[4,256,128]{2,1,0:T(8,128)(2,1)S(1)} %all-to-all-done.6.dq_ref) | copy-start | bytes 786436
  178.9 16.9 %all-to-all-start.9 = ((bf16[4,80,256]{2,1,0:T(8,128)(2,1)}), bf16[4,80,256]{2,1,0:T(8,128)(2,1)S(1)}, u32[]{:S(2)}, u32[]{:S(2)}) async-start(bf16[4,80,256]{2,1,0:T(8,128)(2,1)} %shard_map.132), calls=%async_computation.9 | async-start | bytes 327680 | tf_op jit(solution)/shard_map/all_to_all | solution.py:223
  196.4 5.4 %collective-permute-start.3 = (bf16[2,80,256]{2,1,0:T(8,128)(2,1)S(1)}, bf16[2,80,256]{2,1,0:T(8,128)(2,1)S(1)}, u32[]{:S(2)}, u32[]{:S(2)}) collective-permute-start(bf16[2,80,256]{2,1,0:T(8,128)(2,1)S(1)} %get-tuple-element.33), channel_id=1, source_target_pairs={{0,1},{1,0},{2,3},{3,2},{4,5},{5,4},{6,7},{7,6},{8,9},{9,8},{10,11... | collective-permute-start | bytes 245768 | tf_op jit(solution)/shard_map/ppermute | solution.py:227
  201.9 0.6 copy-start.7
  204.2 1.6 copy-start.8

commit v2 on v1

v2 whole, which is shorter than its diff:
```python
import math

import jax
import jax.numpy as jnp
from jax import lax
from jax.experimental import pallas as pl
from jax.experimental.pallas import tpu as pltpu
from jax.sharding import Mesh, PartitionSpec as P

HEAD = 112
LANES = 128
RANK = 128
STEP = 2

BETA_ONE = 0.9
BETA_TWO = 0.95
LEARN_RATE = 0.01
WEIGHT_DECAY = 0.1
ADAM_EPSILON = 1e-08
MASK_VALUE = -1e30
LOW_MAX = -1e20
SCORE_SCALE = 1.0 / math.sqrt(HEAD)
INV_RANK = 1.0 / math.sqrt(RANK)

BF = jnp.bfloat16
F32 = jnp.float32

TOK = 128
HALF = 64
N_Q = 1024
N_K = 2048
Q_STEP = 256
VMEM_LIMIT = 56 * 1024 * 1024

VMEM = pl.BlockSpec(memory_space=pltpu.VMEM)
SMEM = pl.BlockSpec(memory_space=pltpu.SMEM)


def call(kernel, shapes, specs, scratch=()):
    return pl.pallas_call(
        kernel,
        out_shape=[jax.ShapeDtypeStruct(s, d) for s, d in shapes],
        in_specs=specs,
        out_specs=[VMEM] * len(shapes),
        scratch_shapes=list(scratch),
        compiler_params=pltpu.CompilerParams(vmem_limit_bytes=VMEM_LIMIT),
    )


def dot_nt(a, b):
    return lax.dot_general(a, b, (((1,), (1,)), ((), ())), preferred_element_type=F32)


def dot_tn(a, b):
    return lax.dot_general(a, b, (((0,), (0,)), ((), ())), preferred_element_type=F32)


def rank_of(order):
    return (
        ((order >> 4) & 3) * 32 + (order & 3) * 8 + ((order >> 2) & 3) * 2 + (order >> 6)
    )


def iotas(rows, cols):
    return (
        lax.broadcasted_iota(jnp.int32, (rows, cols), 0),
        lax.broadcasted_iota(jnp.int32, (rows, cols), 1),
    )


def one_hot(mask):
    return jnp.where(mask, 1.0, 0.0).astype(BF)


def split(value):
    high = value.astype(BF)
    return high, (value - high.astype(F32)).astype(BF)


def pack_kernel(pos, x_ref, wd_ref, q_ref, do_ref, k_ref, vb_ref, m_ref,
                part_ref, keep_ref, send_ref, full, w_pad):
    core = pos[4]
    part = dot_tn(x_ref[...], wd_ref[...])
    for s in range(8):
        h = s % 2
        part_ref[s] = part[h * HALF : (h + 1) * HALF]
    full[...] = jnp.zeros_like(full)
    for i, ref in enumerate((q_ref, do_ref, k_ref, vb_ref)):
        for h in range(2):
            tile = ref[h * HEAD : (h + 1) * HEAD, :].T
            full[h, :, i * LANES : i * LANES + HEAD] = tile
    w_pad[...] = jnp.zeros_like(w_pad)
    w_pad[0:2, 0 : 2 * HEAD] = m_ref[...]
    rows = w_pad[...].astype(BF)
    src, dst = iotas(8, LANES)
    for h in range(2):
        spread = sum(
            dot_tn(
                rows[:, h * HEAD + d * HALF : h * HEAD + (d + 1) * HALF],
                one_hot((src < 2) & (dst == HEAD + 2 * d + src)),
            )
            for d in range(2)
        ).astype(BF)
        for t in range(2):
            at = slice(t * HALF, (t + 1) * HALF)
            full[h, at, 384:512] = full[h, at, 384:512] + spread
    own = pl.ds(pl.multiple_of(core * HALF, HALF), HALF)
    other = pl.ds(pl.multiple_of((1 - core) * HALF, HALF), HALF)
    for h in range(2):
        keep_ref[h] = full[h, own, :]
        send_ref[h] = full[h, other, :]


def route_kernel(pos, part_ref, keep_ref, recv_ref, out_ref):
    core = pos[4]
    total = part_ref[0]
    for s in range(1, 8):
        total = total + part_ref[s]
    src, dst = iotas(RANK, RANK)
    order = one_hot(src == rank_of(dst))
    low = jnp.dot(total.astype(BF), order, preferred_element_type=F32).astype(BF)
    for j in range(4):
        out_ref[j, :, 512:640] = low
    for h in range(2):
        out_ref[core * 2 + h, :, 0:512] = keep_ref[h]
        out_ref[(1 - core) * 2 + h, :, 0:512] = recv_ref[h]


def mix_kernel(q_ref, k_ref, out_ref):
    lane = lax.broadcasted_iota(jnp.int32, (256, LANES), 1)
    here = (lane >= HEAD) & (lane < HEAD + 4)
    total = q_ref[:, 0:128].astype(F32)
    for y in range(4):
        tile = k_ref[y * 256 : (y + 1) * 256, 128:256].astype(F32)
        tile = jnp.where(here, tile, 0.0)
        total = total + (pltpu.roll(tile, 4 * y, 1) if y else tile)
    total = total.astype(BF)
    for i in range(4):
        out_ref[i, :, 0:128] = total
        out_ref[i, :, 128:256] = q_ref[:, 128:256]


def token_ids(pos):
    y, x, core = pos[0], pos[2], pos[4]
    n = lax.broadcasted_iota(jnp.int32, (1, N_Q), 1)
    q_tok = y * 2048 + ((n >> 6) & 3) * 512 + (n >> 8) * 128 + core * HALF + (n & 63)
    m = lax.broadcasted_iota(jnp.int32, (N_K, 1), 0)
    half = (m >> 10) ^ core
    k_tok = ((m >> 8) & 3) * 2048 + ((m >> 6) & 3) * 512 + x * 128 + half * HALF + (m & 63)
    return q_tok, k_tok


def up_rows(q_ref):
    src, dst = iotas(LANES, RANK)
    lane = src - HEAD
    halves = []
    for d in range(2):
        place = one_hot(
            (lane >= 0) & (((lane >> 1) & 1) == d) & (dst == (lane & 1) * 64 + (lane >> 2) * 16)
        )
        spread = jnp.dot(q_ref[:, 0:128], place, preferred_element_type=F32)
        total = spread[0:HALF]
        for b in range(1, 16):
            tile = spread[b * HALF : (b + 1) * HALF]
            total = total + pltpu.roll(tile, b, 1)
        halves.append(total)
    return jnp.concatenate(halves, axis=0).astype(BF)


def first_kernel(pos, q_ref, own_ref, other_ref, stat_ref, v_ref):
    w_up = up_rows(q_ref)
    for h, ref in enumerate((own_ref, other_ref)):
        add = dot_nt(ref[:, 256:384], w_up) * INV_RANK
        v_ref[h * 1024 : (h + 1) * 1024] = (ref[:, 128:256].astype(F32) + add).astype(BF)
    q_tok, k_tok = token_ids(pos)
    keys = jnp.concatenate([own_ref[:, 0:128], other_ref[:, 0:128]], axis=0)
    values = v_ref[...]
    for s in range(N_Q // Q_STEP):
        cols = slice(s * Q_STEP, (s + 1) * Q_STEP)
        scores = dot_nt(keys, q_ref[cols, 0:128]) * SCORE_SCALE
        scores = jnp.where(k_tok <= q_tok[:, cols], scores, MASK_VALUE)
        top = jnp.maximum(jnp.max(scores, axis=0, keepdims=True), LOW_MAX)
        weight = jnp.exp(scores - top)
        total = jnp.sum(weight, axis=0, keepdims=True)
        d_prob = dot_nt(values, q_ref[cols, 128:256])
        delta = jnp.sum(weight * d_prob, axis=0, keepdims=True)
        some = total > 0.0
        safe = jnp.where(some, total, 1.0)
        log_total = jnp.where(some, top + jnp.log(safe), MASK_VALUE)
        for i in range(4):
            stat_ref[i, s : s + 1, :] = log_total
            stat_ref[i, 4 + s : 5 + s, :] = delta / safe


def second_kernel(pos, q_ref, own_ref, other_ref, v_ref, stat_ref,
                  dq_ref, keep_ref, send_ref, gkeep_ref, dk_acc, dv_acc, grad_acc):
    core = pos[4]
    q_tok, k_tok = token_ids(pos)
    keys = jnp.concatenate([own_ref[:, 0:128], other_ref[:, 0:128]], axis=0)
    low = jnp.concatenate([own_ref[:, 256:384], other_ref[:, 256:384]], axis=0)
    values = v_ref[...]
    for s in range(N_Q // Q_STEP):
        cols = slice(s * Q_STEP, (s + 1) * Q_STEP)
        lse = [stat_ref[i, s : s + 1, :] for i in range(4)]
        top = jnp.maximum(jnp.maximum(lse[0], lse[1]), jnp.maximum(lse[2], lse[3]))
        share = [jnp.exp(l - top) for l in lse]
        total = share[0] + share[1] + share[2] + share[3]
        delta = sum(share[i] * stat_ref[i, 4 + s : 5 + s, :] for i in range(4)) / total
        log_total = top + jnp.log(total)
        queries, cotan = q_ref[cols, 0:128], q_ref[cols, 128:256]
        scores = dot_nt(keys, queries) * SCORE_SCALE
        scores = jnp.where(k_tok <= q_tok[:, cols], scores, MASK_VALUE)
        prob = jnp.exp(scores - log_total)
        d_prob = dot_nt(values, cotan)
        d_score = (prob * (d_prob - delta)).astype(BF)
        d_key = jnp.dot(d_score, queries, preferred_element_type=F32)
        d_val = jnp.dot(prob.astype(BF), cotan, preferred_element_type=F32)
        if s == 0:
            dk_acc[...] = d_key
            dv_acc[...] = d_val
        else:
            dk_acc[...] += d_key
            dv_acc[...] += d_val
        dq_ref[cols, :] = (dot_tn(d_score, keys) * SCORE_SCALE).astype(BF)
    keep_ref[...] = dk_acc[0:1024] * SCORE_SCALE
    send_ref[0:1024] = (dk_acc[1024:2048] * SCORE_SCALE).astype(BF)
    grad_acc[...] = dot_tn(low, dv_acc[...].astype(BF)) * INV_RANK
    gkeep_ref[...] = grad_acc[pl.ds(pl.multiple_of(core * 64, 64), 64), :]
    high, rest = split(grad_acc[pl.ds(pl.multiple_of((1 - core) * 64, 64), 64), :])
    send_ref[1024:1088] = high
    send_ref[1088:1152] = rest


def core_sum_kernel(keep_ref, gkeep_ref, recv_ref, out_ref):
    for y in range(4):
        at = slice(y * 256, (y + 1) * 256)
        out_ref[y, 0:256] = (keep_ref[at] + recv_ref[at].astype(F32)).astype(BF)
        rows = slice(y * 16, (y + 1) * 16)
        grad = (
            gkeep_ref[rows]
            + recv_ref[1024 + y * 16 : 1040 + y * 16].astype(F32)
            + recv_ref[1088 + y * 16 : 1104 + y * 16].astype(F32)
        )
        out_ref[y, 256:272], out_ref[y, 272:288] = split(grad)


def total_of(ref, rows):
    total = ref[0, rows].astype(F32)
    for i in range(1, 4):
        total = total + ref[i, rows].astype(F32)
    return total


def y_sum_kernel(dk_ref, dq_ref, dk_out, out_ref):
    dk_out[...] = total_of(dk_ref, slice(0, 256)).astype(BF)
    grad = total_of(dk_ref, slice(256, 272)) + total_of(dk_ref, slice(272, 288))
    high, rest = split(grad)
    for i in range(4):
        out_ref[i, 0:256] = dq_ref[i * 256 : (i + 1) * 256]
        out_ref[i, 256:272] = high
        out_ref[i, 272:288] = rest


def x_sum_kernel(dq_ref, dk_ref, out_ref):
    dq = total_of(dq_ref, slice(0, 256)).astype(BF)
    grad = total_of(dq_ref, slice(256, 272)) + total_of(dq_ref, slice(272, 288))
    high, rest = split(grad)
    for z in range(4):
        rows = slice(z * HALF, (z + 1) * HALF)
        out_ref[z, 0:HALF, 0:128] = dq[rows]
        out_ref[z, 0:HALF, 128:256] = dk_ref[rows]
        out_ref[z, HALF : HALF + 16, 0:128] = high
        out_ref[z, HALF : HALF + 16, 128:256] = rest


def last_kernel(pos, keep_ref, recv_ref, master_ref, first_ref, second_ref,
                qg_ref, kg_ref, nm_ref, nf_ref, ns_ref, tile_ref):
    z_hi, x, core = pos[1], pos[2], pos[4]
    for half, ref in ((core, keep_ref), (1 - core, recv_ref)):
        at = pl.ds(pl.multiple_of(half * HALF, HALF), HALF)
        for h in range(2):
            tile_ref[h, at, :] = ref[h, 0:HALF, :]
    for out, lane in ((qg_ref, 0), (kg_ref, 128)):
        for h in range(2):
            out[h * HEAD : (h + 1) * HEAD, :] = tile_ref[h, :, lane : lane + LANES].T[0:HEAD]
    row16 = lax.broadcasted_iota(jnp.int32, (16, LANES), 0)
    mine = row16 == x * 4 + z_hi
    halves = []
    for ref in (keep_ref, recv_ref):
        parts = []
        for h in range(2):
            rows = ref[h, HALF : HALF + 16, :].astype(F32)
            rows = jnp.where(mine, rows[:, 0:128] + rows[:, 128:256], 0.0)
            parts.append(jnp.sum(rows, axis=0, keepdims=True)[:, 0:HEAD])
        halves.append(jnp.concatenate(parts, axis=1))
    row = lax.broadcasted_iota(jnp.int32, (2, 2 * HEAD), 0)
    gradient = jnp.where(row == core, halves[0], halves[1])
    master = master_ref[...]
    new_first = BETA_ONE * first_ref[...] + (1.0 - BETA_ONE) * gradient
    new_second = BETA_TWO * second_ref[...] + (1.0 - BETA_TWO) * gradient * gradient
    direction = (
        new_first
        / (1.0 - BETA_ONE**STEP)
        / (jnp.sqrt(new_second / (1.0 - BETA_TWO**STEP)) + ADAM_EPSILON)
    )
    nm_ref[...] = master - LEARN_RATE * (direction + WEIGHT_DECAY * master)
    nf_ref[...] = new_first
    ns_ref[...] = new_second


def exchange(value, axes):
    return lax.all_to_all(value, axes, split_axis=0, concat_axis=0, tiled=True)


def swap(value):
    return lax.ppermute(value, "core", [(0, 1), (1, 0)])


def copies(value, count):
    return jnp.broadcast_to(value[None], (count, *value.shape)).reshape(
        count * value.shape[0], *value.shape[1:]
    )


def body(normed, w_down, query, key, value_base, cotangent, master, first, second):
    core = lax.axis_index("core")
    pos = jnp.stack([lax.axis_index(a) for a in ("y", "zh", "x", "zl", "core")]).astype(jnp.int32)

    part, keep, send = call(
        pack_kernel,
        [((8, HALF, RANK), F32), ((2, HALF, 512), BF), ((2, HALF, 512), BF)],
        [SMEM] + [VMEM] * 7,
        [pltpu.VMEM((2, TOK, 512), BF), pltpu.VMEM((8, 256), F32)],
    )(pos, normed.T, w_down, query.T, cotangent.T, key.T, value_base.T, master)
    part = exchange(part, ("zl", "core"))
    recv = swap(send)
    (pieces,) = call(route_kernel, [((4, HALF, 640), BF)], [SMEM] + [VMEM] * 3)(
        pos, part, keep, recv
    )
    pieces = exchange(pieces, "zh").reshape(256, 640)
    k_own = exchange(copies(pieces[:, 256:640], 4), "y")
    k_other = swap(k_own)
    (q_tile,) = call(mix_kernel, [((4, 256, 256), BF)], [VMEM] * 2)(pieces[:, 0:256], k_own)
    q_tile = exchange(q_tile, "x").reshape(N_Q, 256)

    stat, values = call(
        first_kernel, [((4, 8, Q_STEP), F32), ((N_K, LANES), BF)], [SMEM] + [VMEM] * 3
    )(pos, q_tile, k_own, k_other)
    stats = exchange(stat, "x")
    dq, dk_keep, dk_send, g_keep = call(
        second_kernel,
        [((N_Q, LANES), BF), ((1024, LANES), F32), ((1152, LANES), BF), ((64, LANES), F32)],
        [SMEM] + [VMEM] * 5,
        [pltpu.VMEM((N_K, LANES), F32)] * 2 + [pltpu.VMEM((RANK, LANES), F32)],
    )(pos, q_tile, k_own, k_other, values, stats)
    (dk,) = call(core_sum_kernel, [((4, 288, LANES), BF)], [VMEM] * 3)(
        dk_keep, g_keep, swap(dk_send)
    )
    dk, dq = call(y_sum_kernel, [((256, LANES), BF), ((4, 288, LANES), BF)], [VMEM] * 2)(
        exchange(dk, "y"), dq
    )
    (back,) = call(x_sum_kernel, [((4, HALF + 16, 256), BF)], [VMEM] * 2)(exchange(dq, "x"), dk)
    back = exchange(back, "zh")
    keep = lax.dynamic_slice_in_dim(back, core * 2, 2, 0)
    recv = swap(lax.dynamic_slice_in_dim(back, (1 - core) * 2, 2, 0))
    q_grad, k_grad, new_master, new_first, new_second = call(
        last_kernel,
        [((2 * HEAD, TOK), BF)] * 2 + [((2, 2 * HEAD), F32)] * 3,
        [SMEM] + [VMEM] * 5,
        [pltpu.VMEM((2, TOK, 2 * LANES), BF)],
    )(pos, keep, recv, master, first, second)
    return q_grad.T, k_grad.T, new_master, new_first, new_second


def solution(mesh):
    fine = Mesh(mesh.devices.reshape(4, 4, 4, 4, 2), ("y", "zh", "x", "zl", "core"))
    seq, section = ("y", "zh", "x"), ("zl", "core")
    split = P(seq, section)
    return jax.shard_map(
        body,
        mesh=fine,
        in_specs=(split, P(section, None)) + (split,) * 7,
        out_specs=(split,) * 5,
        check_vma=False,
    )
```

time: 208 us -> 175 us (0.84)
  waiting for transfers between devices: 44.8 us -> 21.3 us
  starting transfers between devices: 51.1 us -> 35.6 us
  blocking collectives: 72.9 us -> 82.4 us
  local copies, waits for them, and re-layouts: 13.8 us -> 4.99 us
  Pallas kernels: 23 us -> 29.3 us
    all_to_all x5 -> x2, waiting for transfers between devices: 42.7 us -> 17.8 us  [exchange(): return lax.all_to_all(value, axes, split_axis=0, concat_axis=0, tiled=True)]
    all_to_all x5 -> x6, blocking collectives: 66.8 us -> 82.4 us  [exchange(): return lax.all_to_all(value, axes, split_axis=0, concat_axis=0, tiled=True)]
    all_to_all x5 -> x2, starting transfers between devices: 31.1 us -> 15.9 us  [exchange(): return lax.all_to_all(value, axes, split_axis=0, concat_axis=0, tiled=True)]
    pallas_call x4 -> x7, Pallas kernels: 19 us -> 25.3 us  [the longest x1 8.81 us: body(): call(second_kernel, [((N_Q, LANES), BF), ((1024, LANES), F32), ((1152, LA...]
    all_gather x1 -> x0, blocking collectives: 6.16 us -> none  [body(): rows = lax.all_gather(master.astype(BF), 'core', axis=0)]
    unnamed x35 -> x14, local copies, waits for them, and re-layouts: 7.7 us -> 2.97 us
    pallas_call x2 -> x0, local copies, waits for them, and re-layouts: 2.32 us -> none  [body(): call(last_kernel, [((TOK, 2 * HEAD), BF)] * 2 + [((2, 2 * HEAD), F32)] *...]
  transfers between devices with their start and end apart: 9 -> 6, of which waited for: 7 -> 5; matrix products, arithmetic and copies ran while one was open for 0% -> 0% of each run, Pallas kernels for 0% -> 1%
where the time goes in v2:
time: 175 us; the launch traced here: 174 us
  blocking collectives  82.4 us (47%)
  starting transfers between devices  35.6 us (20%)
  Pallas kernels  29.3 us (17%)
  waiting for transfers between devices  21.3 us (12%)
  local copies, waits for them, and re-layouts  4.99 us (3%)
    all_to_all x6, blocking collectives, exchange(): return lax.all_to_all(value, axes, split_axis=0, concat_axis=0, tiled=True)  82.4 us
    ppermute x4, starting transfers between devices, swap(): return lax.ppermute(value, 'core', [(0, 1), (1, 0)])  19.7 us
    all_to_all x2, waiting for transfers between devices, exchange(): return lax.all_to_all(value, axes, split_axis=0, concat_axis=0, tiled=True)  17.8 us
    all_to_all x2, starting transfers between devices, exchange(): return lax.all_to_all(value, axes, split_axis=0, concat_axis=0, tiled=True)  15.9 us
    pallas_call x1, Pallas kernels, body(): call(second_kernel, [((N_Q, LANES), BF), ((1024, LANES), F32), ((1152, LA...  8.81 us
    pallas_call x1, Pallas kernels, body(): call(first_kernel, [((4, 8, Q_STEP), F32), ((N_K, LANES), BF)], [SMEM] +...  7.22 us
    ppermute x4, waiting for transfers between devices, swap(): return lax.ppermute(value, 'core', [(0, 1), (1, 0)])  3.5 us
  transfers between devices with their start and end apart: 6, of which 5 were waited for; matrix products, arithmetic and copies ran while one was open for 0% of the time, Pallas kernels for 1%

profile of v2, /device:TPU:1, one launch (start us, length us, event | category | flops | bytes accessed | tf_op | source)
XLA Modules:
  0.0 174.4 jit_solution(13366418105159228040)
XLA Ops:
  0.6 0.6 stack.23.pos
  1.3 2.1 %shard_map.128 = (f32[8,64,128]{2,1,0:T(8,128)}, bf16[2,64,512]{2,1,0:T(8,128)(2,1)}, bf16[2,64,512]{2,1,0:T(8,128)(2,1)}) custom-call(s32[5]{0:T(128)} %stack.23.pos, bf16[448,128]{1,0:T(8,128)(2,1)} %bitcast.23, bf16[448,128]{1,0:T(8,128)(2,1)} %wd_ref.1, bf16[224,128]{1,0:T(8,128)(2,1)} %bitcast.24, bf16[224,128]{1,0:T(8,128)(2,1)} %bitcast.25, ...), custom_call_target="tpu_custom_call" | custom-call | tf_op jit(solution)/shard_map/pallas_call | solution.py:329
  3.4 0.0 copy-start.6
  3.4 10.3 %all-to-all-start = ((f32[8,64,128]{2,1,0:T(8,128)}), f32[8,64,128]{2,1,0:T(8,128)S(1)}, u32[]{:S(2)}, u32[]{:S(2)}) async-start(f32[8,64,128]{2,1,0:T(8,128)} %get-tuple-element.21), calls=%async_computation | async-start | bytes 524288 | tf_op jit(solution)/shard_map/all_to_all | solution.py:312
  13.7 0.0 copy-done.6
  13.7 2.0 %collective-permute-start = (bf16[2,64,512]{2,1,0:T(8,128)(2,1)S(1)}, bf16[2,64,512]{2,1,0:T(8,128)(2,1)S(1)}, u32[]{:S(2)}, u32[]{:S(2)}) collective-permute-start(bf16[2,64,512]{2,1,0:T(8,128)(2,1)S(1)} %copy-done.6), channel_id=1, source_target_pairs={{0,1},{1,0},{2,3},{3,2},{4,5},{5,4},{6,7},{7,6},{8,9},{9,8},{10,11... | collective-permute-start | bytes 393224 | tf_op jit(solution)/shard_map/ppermute | solution.py:316
  15.7 1.2 collective-permute-done.recv_ref
  16.9 0.0 copy-start.4
  16.9 5.5 %all-to-all-done.part_ref = f32[8,64,128]{2,1,0:T(8,128)S(1)} async-done(((f32[8,64,128]{2,1,0:T(8,128)}), f32[8,64,128]{2,1,0:T(8,128)S(1)}, u32[]{:S(2)}, u32[]{:S(2)}) %all-to-all-start) | async-done | bytes 262176 | tf_op jit(solution)/shard_map/all_to_all | solution.py:312
  22.4 0.0 copy-start.2
  22.4 0.0 copy-done.4
  22.4 0.7 copy-done.2
  23.1 2.0 %shard_map.129 = bf16[4,64,640]{2,1,0:T(8,128)(2,1)} custom-call(s32[5]{0:T(128)} %stack.23.pos, f32[8,64,128]{2,1,0:T(8,128)} %copy-done.2, bf16[2,64,512]{2,1,0:T(8,128)(2,1)} %get-tuple-element.22.keep_ref, bf16[2,64,512]{2,1,0:T(8,128)(2,1)} %copy-done.4), custom_call_target="tpu_custom_call" | custom-call | tf_op jit(solution)/shard_map/pallas_call | solution.py:337
  25.1 27.8 %all_to_all.43 = bf16[4,64,640]{2,1,0:T(8,128)(2,1)S(1)} all-to-all(bf16[4,64,640]{2,1,0:T(8,128)(2,1)} %shard_map.129), channel_id=1, replica_groups=mesh['y'=4,'zh'=4,'x'=4,'zl'=4,'core'=2] {'zh'}, dimensions={0} | all-to-all | bytes 655360 | tf_op jit(solution)/shard_map/all_to_all | solution.py:312
  52.9 0.1 broadcast_in_dim.2
  53.0 12.3 %all_to_all.44 = bf16[4,256,384]{2,1,0:T(8,128)(2,1)S(1)} all-to-all(bf16[4,256,384]{2,1,0:T(8,128)(2,1)S(1)} %broadcast_in_dim.2), channel_id=1, replica_groups=mesh['y'=4,'zh'=4,'x'=4,'zl'=4,'core'=2] {'y'}, dimensions={0} | all-to-all | bytes 1572864 | tf_op jit(solution)/shard_map/all_to_all | solution.py:312
  65.3 0.0 copy-start
  65.3 7.7 %collective-permute-start.1 = (bf16[1024,384]{1,0:T(8,128)(2,1)S(1)}, bf16[1024,384]{1,0:T(8,128)(2,1)S(1)}, u32[]{:S(2)}, u32[]{:S(2)}) collective-permute-start(bf16[1024,384]{1,0:T(8,128)(2,1)S(1)} %bitcast.15), channel_id=1, source_target_pairs={{0,1},{1,0},{2,3},{3,2},{4,5},{5,4},{6,7},{7,6},{8,9},{9,8},{10,11... | collective-permute-start | bytes 2359304 | tf_op jit(solution)/shard_map/ppermute | solution.py:316
  73.0 0.7 slice.8.q_ref
  73.7 0.0 copy-done
  73.7 2.2 %shard_map.130 = bf16[4,256,256]{2,1,0:T(8,128)(2,1)} custom-call(bf16[256,256]{1,0:T(8,128)(2,1)} %slice.8.q_ref, bf16[1024,384]{1,0:T(8,128)(2,1)} %bitcast.16), custom_call_target="tpu_custom_call" | custom-call | tf_op jit(solution)/shard_map/pallas_call | solution.py:343
  75.9 13.4 %all_to_all.45 = bf16[4,256,256]{2,1,0:T(8,128)(2,1)} all-to-all(bf16[4,256,256]{2,1,0:T(8,128)(2,1)} %shard_map.130), channel_id=1, replica_groups=mesh['y'=4,'zh'=4,'x'=4,'zl'=4,'core'=2] {'x'}, dimensions={0} | all-to-all | bytes 1048576 | tf_op jit(solution)/shard_map/all_to_all | solution.py:312
  89.3 0.0 collective-permute-done.1.other_ref
  89.3 0.0 copy-start.1
  89.3 0.9 copy-done.1
  90.2 7.2 %shard_map.131 = (f32[4,8,256]{2,1,0:T(8,128)}, bf16[2048,128]{1,0:T(8,128)(2,1)}) custom-call(s32[5]{0:T(128)} %stack.23.pos, bf16[1024,256]{1,0:T(8,128)(2,1)} %bitcast.19, bf16[1024,384]{1,0:T(8,128)(2,1)} %bitcast.17, bf16[1024,384]{1,0:T(8,128)(2,1)} %copy-done.1), custom_call_target="tpu_custom_call" | custom-call | tf_op jit(solution)/shard_map/pallas_call | solution.py:346
  97.5 8.2 %all_to_all.46.stat_ref = f32[4,8,256]{2,1,0:T(8,128)} all-to-all(f32[4,8,256]{2,1,0:T(8,128)} %get-tuple-element.25), channel_id=1, replica_groups=mesh['y'=4,'zh'=4,'x'=4,'zl'=4,'core'=2] {'x'}, dimensions={0} | all-to-all | bytes 65536 | tf_op jit(solution)/shard_map/all_to_all | solution.py:312
  105.7 8.8 %shard_map.132 = (bf16[1024,128]{1,0:T(8,128)(2,1)}, f32[1024,128]{1,0:T(8,128)}, bf16[1152,128]{1,0:T(8,128)(2,1)}, f32[64,128]{1,0:T(8,128)}) custom-call(s32[5]{0:T(128)} %stack.23.pos, bf16[1024,256]{1,0:T(8,128)(2,1)} %bitcast.20, bf16[1024,384]{1,0:T(8,128)(2,1)} %bitcast.18, bf16[1024,384]{1,0:T(8,128)(2,1)} %copy-done.1, ...), custom_call_target="tpu_custom_call" | custom-call | tf_op jit(solution)/shard_map/pallas_call | solution.py:350
  114.5 4.2 %collective-permute-start.2 = (bf16[1152,128]{1,0:T(8,128)(2,1)}, bf16[1152,128]{1,0:T(8,128)(2,1)S(1)}, u32[]{:S(2)}, u32[]{:S(2)}) collective-permute-start(bf16[1152,128]{1,0:T(8,128)(2,1)} %get-tuple-element.28), channel_id=1, source_target_pairs={{0,1},{1,0},{2,3},{3,2},{4,5},{5,4},{6,7},{7,6},{8,9},{9,8},{10,11... | collective-permute-start | bytes 884744 | tf_op jit(solution)/shard_map/ppermute | solution.py:316
  118.7 1.4 collective-permute-done.2.recv_ref
  120.1 0.0 copy-start.3
  120.1 0.7 copy-done.3
  120.9 1.9 %shard_map.133 = bf16[4,288,128]{2,1,0:T(8,128)(2,1)} custom-call(f32[1024,128]{1,0:T(8,128)} %get-tuple-element.26.keep_ref, f32[64,128]{1,0:T(8,128)} %get-tuple-element.27.gkeep_ref, bf16[1152,128]{1,0:T(8,128)(2,1)} %copy-done.3), custom_call_target="tpu_custom_call" | custom-call | tf_op jit(solution)/shard_map/pallas_call | solution.py:356
  122.8 10.8 %all_to_all.47.dk_ref = bf16[4,288,128]{2,1,0:T(8,128)(2,1)} all-to-all(bf16[4,288,128]{2,1,0:T(8,128)(2,1)} %shard_map.133), channel_id=1, replica_groups=mesh['y'=4,'zh'=4,'x'=4,'zl'=4,'core'=2] {'y'}, dimensions={0} | all-to-all | bytes 589824 | tf_op jit(solution)/shard_map/all_to_all | solution.py:312
  133.5 1.8 %shard_map.134 = (bf16[256,128]{1,0:T(8,128)(2,1)}, bf16[4,288,128]{2,1,0:T(8,128)(2,1)}) custom-call(bf16[4,288,128]{2,1,0:T(8,128)(2,1)} %all_to_all.47.dk_ref, bf16[1024,128]{1,0:T(8,128)(2,1)} %get-tuple-element.29.dq_ref), custom_call_target="tpu_custom_call" | custom-call | tf_op jit(solution)/shard_map/pallas_call | solution.py:359
  135.4 9.8 %all_to_all.48.dq_ref = bf16[4,288,128]{2,1,0:T(8,128)(2,1)} all-to-all(bf16[4,288,128]{2,1,0:T(8,128)(2,1)} %get-tuple-element.30), channel_id=1, replica_groups=mesh['y'=4,'zh'=4,'x'=4,'zl'=4,'core'=2] {'x'}, dimensions={0} | all-to-all | bytes 589824 | tf_op jit(solution)/shard_map/all_to_all | solution.py:312
  145.2 1.7 shard_map.135
  146.9 5.6 %all-to-all-start.7 = ((bf16[4,80,256]{2,1,0:T(8,128)(2,1)}), bf16[4,80,256]{2,1,0:T(8,128)(2,1)S(1)}, u32[]{:S(2)}, u32[]{:S(2)}) async-start(bf16[4,80,256]{2,1,0:T(8,128)(2,1)} %shard_map.135), calls=%async_computation.7 | async-start | bytes 327680 | tf_op jit(solution)/shard_map/all_to_all | solution.py:312
  152.5 12.3 %all-to-all-done.7 = bf16[4,80,256]{2,1,0:T(8,128)(2,1)S(1)} async-done(((bf16[4,80,256]{2,1,0:T(8,128)(2,1)}), bf16[4,80,256]{2,1,0:T(8,128)(2,1)S(1)}, u32[]{:S(2)}, u32[]{:S(2)}) %all-to-all-start.7) | async-done | bytes 163872 | tf_op jit(solution)/shard_map/all_to_all | solution.py:312
  164.8 0.6 constant_dynamic-slice_fusion
  165.4 5.7 %collective-permute-start.3 = (bf16[2,80,256]{2,1,0:T(8,128)(2,1)S(1)}, bf16[2,80,256]{2,1,0:T(8,128)(2,1)S(1)}, u32[]{:S(2)}, u32[]{:S(2)}) collective-permute-start(bf16[2,80,256]{2,1,0:T(8,128)(2,1)S(1)} %get-tuple-element.37), channel_id=1, source_target_pairs={{0,1},{1,0},{2,3},{3,2},{4,5},{5,4},{6,7},{7,6},{8,9},{9,8},{10,11... | collective-permute-start | bytes 245768 | tf_op jit(solution)/shard_map/ppermute | solution.py:316
  171.2 0.9 collective-permute-done.3.recv_ref
  172.1 0.0 copy-start.5
  172.1 0.6 copy-done.5
  172.7 1.7 shard_map.136
  (1 shorter events, 0.0 us)
Async XLA Ops:
  3.4 10.3 %copy-start.6 = (bf16[2,64,512]{2,1,0:T(8,128)(2,1)S(1)}, bf16[2,64,512]{2,1,0:T(8,128)(2,1)}, u32[]{:S(2)}) copy-start(bf16[2,64,512]{2,1,0:T(8,128)(2,1)} %get-tuple-element.23) | copy-start | bytes 393220
  3.4 19.0 %all-to-all-start = ((f32[8,64,128]{2,1,0:T(8,128)}), f32[8,64,128]{2,1,0:T(8,128)S(1)}, u32[]{:S(2)}, u32[]{:S(2)}) async-start(f32[8,64,128]{2,1,0:T(8,128)} %get-tuple-element.21), calls=%async_computation | async-start | bytes 524288 | tf_op jit(solution)/shard_map/all_to_all | solution.py:312
  13.7 3.2 %collective-permute-start = (bf16[2,64,512]{2,1,0:T(8,128)(2,1)S(1)}, bf16[2,64,512]{2,1,0:T(8,128)(2,1)S(1)}, u32[]{:S(2)}, u32[]{:S(2)}) collective-permute-start(bf16[2,64,512]{2,1,0:T(8,128)(2,1)S(1)} %copy-done.6), channel_id=1, source_target_pairs={{0,1},{1,0},{2,3},{3,2},{4,5},{5,4},{6,7},{7,6},{8,9},{9,8},{10,11... | collective-permute-start | bytes 393224 | tf_op jit(solution)/shard_map/ppermute | solution.py:316
  16.9 5.5 %copy-start.4 = (bf16[2,64,512]{2,1,0:T(8,128)(2,1)}, bf16[2,64,512]{2,1,0:T(8,128)(2,1)S(1)}, u32[]{:S(2)}) copy-start(bf16[2,64,512]{2,1,0:T(8,128)(2,1)S(1)} %collective-permute-done.recv_ref) | copy-start | bytes 393220
  22.4 0.7 copy-start.2
  65.3 8.4 %copy-start = (bf16[4,256,384]{2,1,0:T(8,128)(2,1)}, bf16[4,256,384]{2,1,0:T(8,128)(2,1)S(1)}, u32[]{:S(2)}) copy-start(bf16[4,256,384]{2,1,0:T(8,128)(2,1)S(1)} %all_to_all.44) | copy-start | bytes 2359300
  65.3 24.0 %collective-permute-start.1 = (bf16[1024,384]{1,0:T(8,128)(2,1)S(1)}, bf16[1024,384]{1,0:T(8,128)(2,1)S(1)}, u32[]{:S(2)}, u32[]{:S(2)}) collective-permute-start(bf16[1024,384]{1,0:T(8,128)(2,1)S(1)} %bitcast.15), channel_id=1, source_target_pairs={{0,1},{1,0},{2,3},{3,2},{4,5},{5,4},{6,7},{7,6},{8,9},{9,8},{10,11... | collective-permute-start | bytes 2359304 | tf_op jit(solution)/shard_map/ppermute | solution.py:316
  89.3 0.9 copy-start.1
  114.5 5.6 %collective-permute-start.2 = (bf16[1152,128]{1,0:T(8,128)(2,1)}, bf16[1152,128]{1,0:T(8,128)(2,1)S(1)}, u32[]{:S(2)}, u32[]{:S(2)}) collective-permute-start(bf16[1152,128]{1,0:T(8,128)(2,1)} %get-tuple-element.28), channel_id=1, source_target_pairs={{0,1},{1,0},{2,3},{3,2},{4,5},{5,4},{6,7},{7,6},{8,9},{9,8},{10,11... | collective-permute-start | bytes 884744 | tf_op jit(solution)/shard_map/ppermute | solution.py:316
  120.1 0.7 copy-start.3
  146.9 17.9 %all-to-all-start.7 = ((bf16[4,80,256]{2,1,0:T(8,128)(2,1)}), bf16[4,80,256]{2,1,0:T(8,128)(2,1)S(1)}, u32[]{:S(2)}, u32[]{:S(2)}) async-start(bf16[4,80,256]{2,1,0:T(8,128)(2,1)} %shard_map.135), calls=%async_computation.7 | async-start | bytes 327680 | tf_op jit(solution)/shard_map/all_to_all | solution.py:312
  165.4 6.6 %collective-permute-start.3 = (bf16[2,80,256]{2,1,0:T(8,128)(2,1)S(1)}, bf16[2,80,256]{2,1,0:T(8,128)(2,1)S(1)}, u32[]{:S(2)}, u32[]{:S(2)}) collective-permute-start(bf16[2,80,256]{2,1,0:T(8,128)(2,1)S(1)} %get-tuple-element.37), channel_id=1, source_target_pairs={{0,1},{1,0},{2,3},{3,2},{4,5},{5,4},{6,7},{7,6},{8,9},{9,8},{10,11... | collective-permute-start | bytes 245768 | tf_op jit(solution)/shard_map/ppermute | solution.py:316
  172.1 0.6 copy-start.5

commit v3 on v2

v3 whole, which is shorter than its diff:
```python
import math

import jax
import jax.numpy as jnp
from jax import lax
from jax.experimental import pallas as pl
from jax.experimental.pallas import tpu as pltpu
from jax.sharding import Mesh, PartitionSpec as P

HEAD = 112
LANES = 128
RANK = 128
STEP = 2

BETA_ONE = 0.9
BETA_TWO = 0.95
LEARN_RATE = 0.01
WEIGHT_DECAY = 0.1
ADAM_EPSILON = 1e-08
MASK_VALUE = -1e30
LOW_MAX = -1e20
SCORE_SCALE = 1.0 / math.sqrt(HEAD)
INV_RANK = 1.0 / math.sqrt(RANK)

BF = jnp.bfloat16
F32 = jnp.float32

TOK = 128
HALF = 64
N_Q = 1024
N_K = 2048
Q_STEP = 256
K_STEP = 512
LOG2_E = math.log2(math.e)

VMEM = pl.BlockSpec(memory_space=pltpu.VMEM)


def call(kernel, shapes, args, outer=(), scratch=(), limit=8, pinned=True):
    return pl.pallas_call(
        kernel,
        out_shape=[(pltpu.VMEM if pinned else jax.ShapeDtypeStruct)(s, d) for s, d in shapes],
        in_specs=[VMEM] * (len(args) + len(outer)),
        out_specs=[VMEM] * len(shapes),
        scratch_shapes=list(scratch),
        compiler_params=pltpu.CompilerParams(vmem_limit_bytes=limit * 1024 * 1024),
    )(*[pltpu.with_memory_space_constraint(a, pltpu.VMEM) for a in args], *outer)


def dot_nt(a, b):
    return lax.dot_general(a, b, (((1,), (1,)), ((), ())), preferred_element_type=F32)


def dot_tn(a, b):
    return lax.dot_general(a, b, (((0,), (0,)), ((), ())), preferred_element_type=F32)


def rank_of(order):
    return (
        ((order >> 3) & 3) * 32 + (order & 3) * 8 + (order >> 5) * 2 + ((order >> 2) & 1)
    )


def iotas(rows, cols):
    return (
        lax.broadcasted_iota(jnp.int32, (rows, cols), 0),
        lax.broadcasted_iota(jnp.int32, (rows, cols), 1),
    )


def one_hot(mask):
    return jnp.where(mask, 1.0, 0.0).astype(BF)


def split(value):
    high = value.astype(BF)
    return high, (value - high.astype(F32)).astype(BF)


def pack_kernel(x_ref, wd_ref, q_ref, do_ref, k_ref, vb_ref, m_ref,
                part_ref, keep_ref, send_ref, full, w_pad):
    core = lax.axis_index("core")
    part = dot_tn(x_ref[...], wd_ref[...]).astype(BF)
    for s in range(8):
        h = s % 2
        part_ref[s] = part[h * HALF : (h + 1) * HALF]
    full[...] = jnp.zeros_like(full)
    for i, ref in enumerate((q_ref, do_ref, k_ref, vb_ref)):
        for h in range(2):
            tile = ref[h * HEAD : (h + 1) * HEAD, :].T
            full[h, :, i * LANES : i * LANES + HEAD] = tile
    w_pad[...] = jnp.zeros_like(w_pad)
    w_pad[0:2, 0 : 2 * HEAD] = m_ref[...]
    rows = w_pad[...].astype(BF)
    src, dst = iotas(8, LANES)
    for h in range(2):
        spread = sum(
            dot_tn(
                rows[:, h * HEAD + d * HALF : h * HEAD + (d + 1) * HALF],
                one_hot((src < 2) & (dst == HEAD + 2 * d + src)),
            )
            for d in range(2)
        ).astype(BF)
        for t in range(2):
            at = slice(t * HALF, (t + 1) * HALF)
            full[h, at, 384:512] = full[h, at, 384:512] + spread
    own = pl.ds(pl.multiple_of(core * HALF, HALF), HALF)
    other = pl.ds(pl.multiple_of((1 - core) * HALF, HALF), HALF)
    for h in range(2):
        keep_ref[h] = full[h, own, :]
        send_ref[h] = full[h, other, :]


def route_kernel(part_ref, keep_ref, recv_ref, out_ref):
    core = lax.axis_index("core")
    total = part_ref[0].astype(F32)
    for s in range(1, 8):
        total = total + part_ref[s].astype(F32)
    src, dst = iotas(RANK, RANK)
    order = one_hot(src == rank_of(dst))
    low = jnp.dot(total.astype(BF), order, preferred_element_type=F32).astype(BF)
    for j in range(4):
        out_ref[j, :, 512:640] = low
    for h in range(2):
        out_ref[core * 2 + h, :, 0:512] = keep_ref[h]
        out_ref[(1 - core) * 2 + h, :, 0:512] = recv_ref[h]


def mix_kernel(piece_ref, k_ref, out_ref):
    lane = lax.broadcasted_iota(jnp.int32, (256, LANES), 1)
    here = (lane >= HEAD) & (lane < HEAD + 4)
    total = piece_ref[:, 0:128].astype(F32)
    for y in range(4):
        tile = k_ref[y * 256 : (y + 1) * 256, 128:256].astype(F32)
        tile = jnp.where(here, tile, 0.0)
        total = total + (pltpu.roll(tile, 4 * y, 1) if y else tile)
    total = total.astype(BF)
    for i in range(4):
        out_ref[i, :, 0:128] = total
        out_ref[i, :, 128:256] = piece_ref[:, 128:256]


def diagonal_mask(half):
    x, core = lax.axis_index("x"), lax.axis_index("core")
    n = lax.broadcasted_iota(jnp.int32, (1, N_Q), 1)
    q_tok = ((n >> 6) & 3) * 512 + (n >> 8) * 128 + core * HALF + (n & 63)
    m = lax.broadcasted_iota(jnp.int32, (256, 1), 0)
    k_tok = (m >> 6) * 512 + x * 128 + (core ^ half) * HALF + (m & 63)
    return q_tok, k_tok


def up_rows(q_ref):
    src, dst = iotas(LANES, RANK)
    lane = src - HEAD
    halves = []
    for d in range(2):
        place = one_hot(
            (lane >= 0) & (((lane >> 1) & 1) == d) & (dst == (lane & 1) * 4 + (lane >> 2) * 8)
        )
        spread = jnp.dot(q_ref[:, 0:128], place, preferred_element_type=F32)
        total = spread[0:HALF]
        for b in range(1, 16):
            tile = spread[b * HALF : (b + 1) * HALF]
            total = total + pltpu.roll(tile, (b >> 2) * 32 + (b & 3), 1)
        halves.append(total)
    return jnp.concatenate(halves, axis=0).astype(BF)


def first_kernel(q_ref, own_ref, other_ref, stat_ref, top_ref, w_ref, d_ref, v_ref):
    w_up = up_rows(q_ref)
    for h, ref in enumerate((own_ref, other_ref)):
        add = dot_nt(ref[:, 256:384], w_up) * INV_RANK
        v_ref[h * 1024 : (h + 1) * 1024] = (ref[:, 128:256].astype(F32) + add).astype(BF)
    y = lax.axis_index("y")
    keys = jnp.concatenate([own_ref[:, 0:128], other_ref[:, 0:128]], axis=0)
    values = v_ref[...]
    for s in range(N_Q // Q_STEP):
        cols = slice(s * Q_STEP, (s + 1) * Q_STEP)
        w_ref[:, cols] = dot_nt(keys, q_ref[cols, 0:128]) * (SCORE_SCALE * LOG2_E)
        for half in range(2):
            q_tok, k_tok = diagonal_mask(half)
            rows = pl.ds(pl.multiple_of(half * 1024 + y * 256, 256), 256)
            w_ref[rows, cols] = jnp.where(k_tok <= q_tok[:, cols], w_ref[rows, cols], MASK_VALUE)
            for block in range(1, 4):
                @pl.when(block > y)
                def _():
                    later = slice(half * 1024 + block * 256, half * 1024 + block * 256 + 256)
                    w_ref[later, cols] = jnp.full((256, Q_STEP), MASK_VALUE, F32)
        d_ref[:, cols] = dot_nt(values, q_ref[cols, 128:256])
        scores = w_ref[:, cols]
        top = jnp.maximum(jnp.max(scores, axis=0, keepdims=True), LOW_MAX)
        weight = jnp.exp2(scores - top)
        w_ref[:, cols] = weight
        total = jnp.sum(weight, axis=0, keepdims=True)
        delta = jnp.sum(weight * d_ref[:, cols], axis=0, keepdims=True)
        some = total > 0.0
        safe = jnp.where(some, total, 1.0)
        log_total = jnp.where(some, top + jnp.log2(safe), MASK_VALUE)
        top_ref[0:1, cols] = top
        for i in range(4):
            stat_ref[i, 0:1, cols] = log_total
            stat_ref[i, 1:2, cols] = delta / safe


def second_kernel(q_ref, own_ref, other_ref, w_ref, d_ref, top_ref, stat_ref,
                  dq_ref, keep_ref, send_ref, dv_ref, dq_acc):
    lse = [stat_ref[i, 0:1, :] for i in range(4)]
    top = jnp.maximum(jnp.maximum(lse[0], lse[1]), jnp.maximum(lse[2], lse[3]))
    share = [jnp.exp2(l - top) for l in lse]
    total = share[0] + share[1] + share[2] + share[3]
    delta = sum(share[i] * stat_ref[i, 1:2, :] for i in range(4)) / total
    factor = jnp.exp2(top_ref[0:1, :] - (top + jnp.log2(total)))
    queries, cotan = q_ref[:, 0:128], q_ref[:, 128:256]
    for s in range(N_K // K_STEP):
        rows = slice(s * K_STEP, (s + 1) * K_STEP)
        ref, out = (own_ref, keep_ref) if s < 2 else (other_ref, send_ref)
        part = slice((s % 2) * K_STEP, (s % 2 + 1) * K_STEP)
        prob = w_ref[rows] * factor
        d_score = (prob * (d_ref[rows] - delta)).astype(BF)
        dv_ref[rows] = jnp.dot(prob.astype(BF), cotan, preferred_element_type=F32).astype(BF)
        d_key = jnp.dot(d_score, queries, preferred_element_type=F32) * SCORE_SCALE
        out[part] = d_key.astype(out.dtype)
        d_query = dot_tn(ref[part, 0:128], d_score)
        if s == 0:
            dq_acc[...] = d_query
        else:
            dq_acc[...] += d_query
    d_query = (dq_acc[...] * SCORE_SCALE).T.astype(BF)
    low = jnp.concatenate([own_ref[:, 256:384], other_ref[:, 256:384]], axis=0)
    high, rest = split(dot_tn(low, dv_ref[...]) * INV_RANK)
    for i in range(4):
        dq_ref[i, 0:256] = d_query[i * 256 : (i + 1) * 256]
        dq_ref[i, 256:288] = high[i * 32 : (i + 1) * 32]
        dq_ref[i, 288:320] = rest[i * 32 : (i + 1) * 32]


def total_of(ref, rows):
    total = ref[0, rows].astype(F32)
    for i in range(1, 4):
        total = total + ref[i, rows].astype(F32)
    return total


def pair(value):
    high, rest = split(value)
    return jnp.concatenate([high.astype(F32), rest.astype(F32)], axis=0).astype(BF)


def x_sum_kernel(dq_ref, keep_ref, recv_ref, dq_out, out_ref):
    dq_out[...] = total_of(dq_ref, slice(0, 256)).astype(BF)
    grad = total_of(dq_ref, slice(256, 288)) + total_of(dq_ref, slice(288, 320))
    for y in range(4):
        at = slice(y * 256, (y + 1) * 256)
        out_ref[y, 0:256] = (keep_ref[at] + recv_ref[at].astype(F32)).astype(BF)
        out_ref[y, 256:272] = pair(grad[y * 8 : (y + 1) * 8])


def y_sum_kernel(dk_ref, dq_ref, out_ref):
    dk = total_of(dk_ref, slice(0, 256)).astype(BF)
    grad = total_of(dk_ref, slice(256, 272))
    grad = pair(grad[0:8] + grad[8:16])
    for z in range(4):
        rows = slice(z * HALF, (z + 1) * HALF)
        out_ref[z, 0:HALF, 0:128] = dq_ref[rows]
        out_ref[z, 0:HALF, 128:256] = dk[rows]
        out_ref[z, HALF : HALF + 16, 0:128] = grad
        out_ref[z, HALF : HALF + 16, 128:256] = jnp.zeros((16, 128), BF)


def last_kernel(back_ref, master_ref, first_ref, second_ref,
                qg_ref, kg_ref, nm_ref, nf_ref, ns_ref, tile_ref):
    z_hi, core = lax.axis_index("zh"), lax.axis_index("core")
    for half in range(2):
        for h in range(2):
            tile_ref[h, half * HALF : (half + 1) * HALF] = back_ref[half, core * 2 + h, 0:HALF, :]
    for out, lane in ((qg_ref, 0), (kg_ref, 128)):
        for h in range(2):
            out[h * HEAD : (h + 1) * HEAD, :] = tile_ref[h, :, lane : lane + LANES].T[0:HEAD]
    row8 = lax.broadcasted_iota(jnp.int32, (8, LANES), 0)
    columns = []
    for h in range(2):
        rows = (
            back_ref[0, core * 2 + h, HALF : HALF + 16, 0:128].astype(F32)
            + back_ref[1, core * 2 + h, HALF : HALF + 16, 0:128].astype(F32)
        )
        rows = rows[0:8] + rows[8:16]
        columns.append(jnp.concatenate(
            [
                jnp.sum(jnp.where(row8 == e * 4 + z_hi, rows, 0.0), axis=0, keepdims=True)
                for e in range(2)
            ],
            axis=0,
        )[:, 0:HEAD])
    gradient = jnp.concatenate(columns, axis=1)
    master = master_ref[...]
    new_first = BETA_ONE * first_ref[...] + (1.0 - BETA_ONE) * gradient
    new_second = BETA_TWO * second_ref[...] + (1.0 - BETA_TWO) * gradient * gradient
    direction = (
        new_first
        / (1.0 - BETA_ONE**STEP)
        / (jnp.sqrt(new_second / (1.0 - BETA_TWO**STEP)) + ADAM_EPSILON)
    )
    nm_ref[...] = master - LEARN_RATE * (direction + WEIGHT_DECAY * master)
    nf_ref[...] = new_first
    ns_ref[...] = new_second


def exchange(value, axes):
    return lax.all_to_all(value, axes, split_axis=0, concat_axis=0, tiled=True)


def swap(value):
    return lax.ppermute(value, "core", [(0, 1), (1, 0)])


def copies(value, count):
    return jnp.broadcast_to(value[None], (count, *value.shape)).reshape(
        count * value.shape[0], *value.shape[1:]
    )


def body(normed, w_down, query, key, value_base, cotangent, master, first, second):
    part, keep, send = call(
        pack_kernel,
        [((8, HALF, RANK), BF), ((2, HALF, 512), BF), ((2, HALF, 512), BF)],
        (),
        (normed.T, w_down, query.T, cotangent.T, key.T, value_base.T, master),
        [pltpu.VMEM((2, TOK, 512), BF), pltpu.VMEM((8, 256), F32)],
        limit=56,
    )
    part = exchange(part, ("zl", "core"))
    recv = swap(send)
    (pieces,) = call(route_kernel, [((4, HALF, 640), BF)], (part, keep, recv))
    pieces = exchange(pieces, "zh").reshape(256, 640)
    k_own = exchange(copies(pieces[:, 256:640], 4), "y")
    k_other = swap(k_own)
    (q_tile,) = call(mix_kernel, [((4, 256, 256), BF)], (pieces, k_own))
    q_tile = exchange(q_tile, "x").reshape(N_Q, 256)

    stat, top, weight, d_prob = call(
        first_kernel,
        [((4, 2, N_Q), F32), ((1, N_Q), F32), ((N_K, N_Q), F32), ((N_K, N_Q), F32)],
        (q_tile, k_own, k_other),
        scratch=[pltpu.VMEM((N_K, LANES), BF)],
        limit=16,
    )
    stats = exchange(stat, "x")
    dq, dk_keep, dk_send = call(
        second_kernel,
        [((4, 320, LANES), BF), ((1024, LANES), F32), ((1024, LANES), BF)],
        (q_tile, k_own, k_other, weight, d_prob, top, stats),
        scratch=[pltpu.VMEM((N_K, LANES), BF), pltpu.VMEM((LANES, N_Q), F32)],
        limit=16,
    )
    dk_recv = swap(dk_send)
    dq, dk = call(
        x_sum_kernel,
        [((256, LANES), BF), ((4, 272, LANES), BF)],
        (exchange(dq, "x"), dk_keep, dk_recv),
    )
    (back,) = call(y_sum_kernel, [((4, HALF + 16, 256), BF)], (exchange(dk, "y"), dq))
    back = exchange(back, "zh")
    back = lax.all_gather(back, "core", axis=0)
    q_grad, k_grad, new_master, new_first, new_second = call(
        last_kernel,
        [((2 * HEAD, TOK), BF)] * 2 + [((2, 2 * HEAD), F32)] * 3,
        (back,),
        (master, first, second),
        [pltpu.VMEM((2, TOK, 2 * LANES), BF)],
        pinned=False,
    )
    return q_grad.T, k_grad.T, new_master, new_first, new_second


def solution(mesh):
    fine = Mesh(mesh.devices.reshape(4, 4, 4, 4, 2), ("y", "zh", "x", "zl", "core"))
    seq, section = ("y", "zh", "x"), ("zl", "core")
    split = P(seq, section)
    return jax.shard_map(
        body,
        mesh=fine,
        in_specs=(split, P(section, None)) + (split,) * 7,
        out_specs=(split,) * 5,
        check_vma=False,
    )
```

time: 175 us -> 144 us (0.82)
  blocking collectives: 82.4 us -> 102 us
  waiting for transfers between devices: 21.3 us -> 3.82 us
  Pallas kernels: 29.3 us -> 12.7 us
  starting transfers between devices: 35.6 us -> 24 us
  local copies, waits for them, and re-layouts: 4.99 us -> 0.1 us
    pallas_call x9 -> x8, Pallas kernels: 29.3 us -> 12.7 us  [call(): pl.pallas_call(kernel, out_shape=[(pltpu.VMEM if pinned else jax.ShapeDty...]
    all_to_all x2 -> x1, waiting for transfers between devices: 17.8 us -> 2.61 us  [exchange(): return lax.all_to_all(value, axes, split_axis=0, concat_axis=0, tiled=True)]
    all_to_all x6 -> x7, blocking collectives: 82.4 us -> 97.4 us  [exchange(): return lax.all_to_all(value, axes, split_axis=0, concat_axis=0, tiled=True)]
    ppermute x4 -> x3, starting transfers between devices: 19.7 us -> 13.9 us  [swap(): return lax.ppermute(value, 'core', [(0, 1), (1, 0)])]
    all_to_all x2 -> x1, starting transfers between devices: 15.9 us -> 10.1 us  [exchange(): return lax.all_to_all(value, axes, split_axis=0, concat_axis=0, tiled=True)]
    all_gather x0 -> x1, blocking collectives: none -> 4.53 us  [body(): back = lax.all_gather(back, 'core', axis=0)]
    unnamed x14 -> x6, local copies, waits for them, and re-layouts: 2.97 us -> 0.01 us
    ppermute x4 -> x3, waiting for transfers between devices: 3.5 us -> 1.21 us  [swap(): return lax.ppermute(value, 'core', [(0, 1), (1, 0)])]
  transfers between devices with their start and end apart: 6 -> 4, of which waited for: 5 -> 2; matrix products, arithmetic and copies ran while one was open for 0% -> 0% of each run, Pallas kernels for 1% -> 0%
where the time goes in v3:
time: 144 us; the launch traced here: 143 us
  blocking collectives  102 us (71%)
  starting transfers between devices  24 us (17%)
  Pallas kernels  12.7 us (9%)
  waiting for transfers between devices  3.82 us (3%)
    all_to_all x7, blocking collectives, exchange(): return lax.all_to_all(value, axes, split_axis=0, concat_axis=0, tiled=True)  97.4 us
    ppermute x3, starting transfers between devices, swap(): return lax.ppermute(value, 'core', [(0, 1), (1, 0)])  13.9 us
    pallas_call x8, Pallas kernels, call(): pl.pallas_call(kernel, out_shape=[(pltpu.VMEM if pinned else jax.ShapeDty...  12.7 us
    all_to_all x1, starting transfers between devices, exchange(): return lax.all_to_all(value, axes, split_axis=0, concat_axis=0, tiled=True)  10.1 us
    all_gather x1, blocking collectives, body(): back = lax.all_gather(back, 'core', axis=0)  4.53 us
  transfers between devices with their start and end apart: 4, of which 2 were waited for; matrix products, arithmetic and copies ran while one was open for 0% of the time, Pallas kernels for 0%

profile of v3, /device:TPU:1, one launch (start us, length us, event | category | flops | bytes accessed | tf_op | source)
XLA Modules:
  0.0 143.2 jit_solution(10675220863944226817)
XLA Ops:
  0.6 2.0 %shard_map.128 = (bf16[8,64,128]{2,1,0:T(8,128)(2,1)}, bf16[2,64,512]{2,1,0:T(8,128)(2,1)S(1)}, bf16[2,64,512]{2,1,0:T(8,128)(2,1)S(1)}) custom-call(bf16[448,128]{1,0:T(8,128)(2,1)} %bitcast.20, bf16[448,128]{1,0:T(8,128)(2,1)} %wd_ref.1, bf16[224,128]{1,0:T(8,128)(2,1)} %bitcast.21, bf16[224,128]{1,0:T(8,128)(2,1)} %bitcast.22, bf16[224,128]{1,0:T(8,128)(2,1)} %bitcast.23, ...), custom_call_target="tpu_custom_call" | custom-call | tf_op jit(solution)/shard_map/pallas_call | solution.py:40
  2.6 10.1 %all-to-all-start = ((bf16[8,64,128]{2,1,0:T(8,128)(2,1)}), bf16[8,64,128]{2,1,0:T(8,128)(2,1)S(1)}, u32[]{:S(2)}, u32[]{:S(2)}) async-start(bf16[8,64,128]{2,1,0:T(8,128)(2,1)} %get-tuple-element.22), calls=%async_computation | async-start | bytes 262144 | tf_op jit(solution)/shard_map/all_to_all | solution.py:309
  12.7 2.0 %collective-permute-start = (bf16[2,64,512]{2,1,0:T(8,128)(2,1)S(1)}, bf16[2,64,512]{2,1,0:T(8,128)(2,1)S(1)}, u32[]{:S(2)}, u32[]{:S(2)}) collective-permute-start(bf16[2,64,512]{2,1,0:T(8,128)(2,1)S(1)} %get-tuple-element.24), channel_id=1, source_target_pairs={{0,1},{1,0},{2,3},{3,2},{4,5},{5,4},{6,7},{7,6},{8,9},{9,8},{10,11... | collective-permute-start | bytes 393224 | tf_op jit(solution)/shard_map/ppermute | solution.py:313
  14.8 1.2 collective-permute-done.recv_ref
  16.0 2.6 %all-to-all-done.part_ref = bf16[8,64,128]{2,1,0:T(8,128)(2,1)S(1)} async-done(((bf16[8,64,128]{2,1,0:T(8,128)(2,1)}), bf16[8,64,128]{2,1,0:T(8,128)(2,1)S(1)}, u32[]{:S(2)}, u32[]{:S(2)}) %all-to-all-start) | async-done | bytes 131104 | tf_op jit(solution)/shard_map/all_to_all | solution.py:309
  18.6 0.1 shard_map.129
  18.7 27.8 %all_to_all.43 = bf16[4,64,640]{2,1,0:T(8,128)(2,1)S(1)} all-to-all(bf16[4,64,640]{2,1,0:T(8,128)(2,1)S(1)} %shard_map.129), channel_id=1, replica_groups=mesh['y'=4,'zh'=4,'x'=4,'zl'=4,'core'=2] {'zh'}, dimensions={0} | all-to-all | bytes 655360 | tf_op jit(solution)/shard_map/all_to_all | solution.py:309
  46.6 0.1 broadcast_in_dim.2
  46.7 12.3 %all_to_all.44 = bf16[4,256,384]{2,1,0:T(8,128)(2,1)S(1)} all-to-all(bf16[4,256,384]{2,1,0:T(8,128)(2,1)S(1)} %broadcast_in_dim.2), channel_id=1, replica_groups=mesh['y'=4,'zh'=4,'x'=4,'zl'=4,'core'=2] {'y'}, dimensions={0} | all-to-all | bytes 1572864 | tf_op jit(solution)/shard_map/all_to_all | solution.py:309
  59.0 7.7 %collective-permute-start.1 = (bf16[1024,384]{1,0:T(8,128)(2,1)S(1)}, bf16[1024,384]{1,0:T(8,128)(2,1)S(1)}, u32[]{:S(2)}, u32[]{:S(2)}) collective-permute-start(bf16[1024,384]{1,0:T(8,128)(2,1)S(1)} %bitcast.11), channel_id=1, source_target_pairs={{0,1},{1,0},{2,3},{3,2},{4,5},{5,4},{6,7},{7,6},{8,9},{9,8},{10,11... | collective-permute-start | bytes 2359304 | tf_op jit(solution)/shard_map/ppermute | solution.py:313
  66.7 0.1 shard_map.130
  66.9 13.1 %all_to_all.45 = bf16[4,256,256]{2,1,0:T(8,128)(2,1)S(1)} all-to-all(bf16[4,256,256]{2,1,0:T(8,128)(2,1)S(1)} %shard_map.130), channel_id=1, replica_groups=mesh['y'=4,'zh'=4,'x'=4,'zl'=4,'core'=2] {'x'}, dimensions={0} | all-to-all | bytes 1048576 | tf_op jit(solution)/shard_map/all_to_all | solution.py:309
  80.0 0.0 collective-permute-done.1.other_ref
  80.0 6.4 %shard_map.131 = (f32[4,2,1024]{2,1,0:T(2,128)S(1)}, f32[1,1024]{1,0:T(1,128)S(1)}, f32[2048,1024]{1,0:T(8,128)S(1)}, f32[2048,1024]{1,0:T(8,128)S(1)}) custom-call(bf16[1024,256]{1,0:T(8,128)(2,1)S(1)} %bitcast.15, bf16[1024,384]{1,0:T(8,128)(2,1)S(1)} %bitcast.13, bf16[1024,384]{1,0:T(8,128)(2,1)S(1)} %collective-permute-done.1.other_ref), custom_call_target="tpu_custom_call" | custom-call | tf_op jit(solution)/shard_map/pallas_call | solution.py:40
  86.4 6.7 %all_to_all.46.stat_ref = f32[4,2,1024]{2,1,0:T(2,128)S(1)} all-to-all(f32[4,2,1024]{2,1,0:T(2,128)S(1)} %get-tuple-element.28), channel_id=1, replica_groups=mesh['y'=4,'zh'=4,'x'=4,'zl'=4,'core'=2] {'x'}, dimensions={0} | all-to-all | bytes 65536 | tf_op jit(solution)/shard_map/all_to_all | solution.py:309
  93.1 0.0 copy-start
  93.1 0.0 copy-start.1
  93.1 0.0 copy-start.2
  93.1 3.1 %shard_map.132 = (bf16[4,320,128]{2,1,0:T(8,128)(2,1)S(1)}, f32[1024,128]{1,0:T(8,128)S(1)}, bf16[1024,128]{1,0:T(8,128)(2,1)S(1)}) custom-call(bf16[1024,256]{1,0:T(8,128)(2,1)S(1)} %bitcast.16, bf16[1024,384]{1,0:T(8,128)(2,1)S(1)} %bitcast.14, bf16[1024,384]{1,0:T(8,128)(2,1)S(1)} %collective-permute-done.1.other_ref, ...), custom_call_target="tpu_custom_call" | custom-call | tf_op jit(solution)/shard_map/pallas_call | solution.py:40
  96.2 4.1 %collective-permute-start.2 = (bf16[1024,128]{1,0:T(8,128)(2,1)S(1)}, bf16[1024,128]{1,0:T(8,128)(2,1)S(1)}, u32[]{:S(2)}, u32[]{:S(2)}) collective-permute-start(bf16[1024,128]{1,0:T(8,128)(2,1)S(1)} %get-tuple-element.31), channel_id=1, source_target_pairs={{0,1},{1,0},{2,3},{3,2},{4,5},{5,4},{6,7},{7,6},{8,9},{9,8},{10,11... | collective-permute-start | bytes 786440 | tf_op jit(solution)/shard_map/ppermute | solution.py:313
  100.3 9.9 %all_to_all.47.dq_ref = bf16[4,320,128]{2,1,0:T(8,128)(2,1)S(1)} all-to-all(bf16[4,320,128]{2,1,0:T(8,128)(2,1)S(1)} %get-tuple-element.29), channel_id=1, replica_groups=mesh['y'=4,'zh'=4,'x'=4,'zl'=4,'core'=2] {'x'}, dimensions={0} | all-to-all | bytes 655360 | tf_op jit(solution)/shard_map/all_to_all | solution.py:309
  110.2 0.0 collective-permute-done.2.recv_ref
  110.2 0.1 shard_map.133
  110.3 8.2 %all_to_all.48.dk_ref = bf16[4,272,128]{2,1,0:T(8,128)(2,1)S(1)} all-to-all(bf16[4,272,128]{2,1,0:T(8,128)(2,1)S(1)} %get-tuple-element.32), channel_id=1, replica_groups=mesh['y'=4,'zh'=4,'x'=4,'zl'=4,'core'=2] {'y'}, dimensions={0} | all-to-all | bytes 557056 | tf_op jit(solution)/shard_map/all_to_all | solution.py:309
  118.6 19.4 %all_to_all.49 = bf16[4,80,256]{2,1,0:T(8,128)(2,1)S(1)} all-to-all(bf16[4,80,256]{2,1,0:T(8,128)(2,1)S(1)} %shard_map.134), channel_id=1, replica_groups=mesh['y'=4,'zh'=4,'x'=4,'zl'=4,'core'=2] {'zh'}, dimensions={0} | all-to-all | bytes 327680 | tf_op jit(solution)/shard_map/all_to_all | solution.py:309
  137.9 4.5 %all-gather = bf16[8,80,256]{2,1,0:T(8,128)(2,1)S(1)} all-gather(bf16[4,80,256]{2,1,0:T(8,128)(2,1)S(1)} %all_to_all.49), channel_id=2, replica_groups=mesh['y'=4,'zh'=4,'x'=4,'zl'=4,'core'=2] {'core'}, dimensions={0}, use_global_device_ids=true | all-gather | bytes 491520 | tf_op jit(solution)/shard_map/all_gather | solution.py:363
  142.5 0.0 copy-done
  142.5 0.0 copy-done.1
  142.5 0.0 copy-done.2
  142.5 0.8 shard_map.135
  (2 shorter events, 0.1 us)
Async XLA Ops:
  2.6 16.0 %all-to-all-start = ((bf16[8,64,128]{2,1,0:T(8,128)(2,1)}), bf16[8,64,128]{2,1,0:T(8,128)(2,1)S(1)}, u32[]{:S(2)}, u32[]{:S(2)}) async-start(bf16[8,64,128]{2,1,0:T(8,128)(2,1)} %get-tuple-element.22), calls=%async_computation | async-start | bytes 262144 | tf_op jit(solution)/shard_map/all_to_all | solution.py:309
  12.7 3.2 %collective-permute-start = (bf16[2,64,512]{2,1,0:T(8,128)(2,1)S(1)}, bf16[2,64,512]{2,1,0:T(8,128)(2,1)S(1)}, u32[]{:S(2)}, u32[]{:S(2)}) collective-permute-start(bf16[2,64,512]{2,1,0:T(8,128)(2,1)S(1)} %get-tuple-element.24), channel_id=1, source_target_pairs={{0,1},{1,0},{2,3},{3,2},{4,5},{5,4},{6,7},{7,6},{8,9},{9,8},{10,11... | collective-permute-start | bytes 393224 | tf_op jit(solution)/shard_map/ppermute | solution.py:313
  59.0 21.0 %collective-permute-start.1 = (bf16[1024,384]{1,0:T(8,128)(2,1)S(1)}, bf16[1024,384]{1,0:T(8,128)(2,1)S(1)}, u32[]{:S(2)}, u32[]{:S(2)}) collective-permute-start(bf16[1024,384]{1,0:T(8,128)(2,1)S(1)} %bitcast.11), channel_id=1, source_target_pairs={{0,1},{1,0},{2,3},{3,2},{4,5},{5,4},{6,7},{7,6},{8,9},{9,8},{10,11... | collective-permute-start | bytes 2359304 | tf_op jit(solution)/shard_map/ppermute | solution.py:313
  93.1 49.4 %copy-start = (f32[2,224]{1,0:T(2,128)S(1)}, f32[2,224]{1,0:T(2,128)}, u32[]{:S(2)}) copy-start(f32[2,224]{1,0:T(2,128)} %master_ref.1) | copy-start | bytes 5380
  93.1 49.4 %copy-start.1 = (f32[2,224]{1,0:T(2,128)S(1)}, f32[2,224]{1,0:T(2,128)}, u32[]{:S(2)}) copy-start(f32[2,224]{1,0:T(2,128)} %first_ref.1) | copy-start | bytes 5380
  93.1 49.4 %copy-start.2 = (f32[2,224]{1,0:T(2,128)S(1)}, f32[2,224]{1,0:T(2,128)}, u32[]{:S(2)}) copy-start(f32[2,224]{1,0:T(2,128)} %second_ref.1) | copy-start | bytes 5380
  96.2 14.1 %collective-permute-start.2 = (bf16[1024,128]{1,0:T(8,128)(2,1)S(1)}, bf16[1024,128]{1,0:T(8,128)(2,1)S(1)}, u32[]{:S(2)}, u32[]{:S(2)}) collective-permute-start(bf16[1024,128]{1,0:T(8,128)(2,1)S(1)} %get-tuple-element.31), channel_id=1, source_target_pairs={{0,1},{1,0},{2,3},{3,2},{4,5},{5,4},{6,7},{7,6},{8,9},{9,8},{10,11... | collective-permute-start | bytes 786440 | tf_op jit(solution)/shard_map/ppermute | solution.py:313

commit v4 on v3

--- a/solution.py
+++ b/solution.py
@@ -29,7 +29,7 @@
 HALF = 64
 N_Q = 1024
 N_K = 2048
-Q_STEP = 256
+K_BLOCK = 256
 K_STEP = 512
 LOG2_E = math.log2(math.e)
 
@@ -77,13 +77,15 @@
     return high, (value - high.astype(F32)).astype(BF)
 
 
-def pack_kernel(x_ref, wd_ref, q_ref, do_ref, k_ref, vb_ref, m_ref,
-                part_ref, keep_ref, send_ref, full, w_pad):
-    core = lax.axis_index("core")
+def low_kernel(x_ref, wd_ref, part_ref):
     part = dot_tn(x_ref[...], wd_ref[...]).astype(BF)
     for s in range(8):
         h = s % 2
         part_ref[s] = part[h * HALF : (h + 1) * HALF]
+
+
+def pack_kernel(q_ref, do_ref, k_ref, vb_ref, m_ref, keep_ref, send_ref, full, w_pad):
+    core = lax.axis_index("core")
     full[...] = jnp.zeros_like(full)
     for i, ref in enumerate((q_ref, do_ref, k_ref, vb_ref)):
         for h in range(2):
@@ -140,13 +142,18 @@
         out_ref[i, :, 128:256] = piece_ref[:, 128:256]
 
 
-def diagonal_mask(half):
-    x, core = lax.axis_index("x"), lax.axis_index("core")
+def token_ids():
+    y, x, core = lax.axis_index("y"), lax.axis_index("x"), lax.axis_index("core")
     n = lax.broadcasted_iota(jnp.int32, (1, N_Q), 1)
-    q_tok = ((n >> 6) & 3) * 512 + (n >> 8) * 128 + core * HALF + (n & 63)
-    m = lax.broadcasted_iota(jnp.int32, (256, 1), 0)
-    k_tok = (m >> 6) * 512 + x * 128 + (core ^ half) * HALF + (m & 63)
+    q_tok = y * 2048 + ((n >> 6) & 3) * 512 + (n >> 8) * 128 + core * HALF + (n & 63)
+    m = lax.broadcasted_iota(jnp.int32, (N_K, 1), 0)
+    k_y, half = (m >> 10) * 2 + ((m >> 8) & 1), (m >> 9) & 1
+    k_tok = k_y * 2048 + ((m >> 6) & 3) * 512 + x * 128 + half * HALF + (m & 63)
     return q_tok, k_tok
+
+
+def fold(value, op):
+    return op(value.reshape(value.shape[0] // 8, 8, value.shape[1]), axis=0)
 
 
 def up_rows(q_ref):
@@ -166,44 +173,45 @@
     return jnp.concatenate(halves, axis=0).astype(BF)
 
 
-def first_kernel(q_ref, own_ref, other_ref, stat_ref, top_ref, w_ref, d_ref, v_ref):
+def first_kernel(q_ref, low_ref, high_ref, stat_ref, top_ref, w_ref, d_ref, v_ref):
     w_up = up_rows(q_ref)
-    for h, ref in enumerate((own_ref, other_ref)):
+    for h, ref in enumerate((low_ref, high_ref)):
         add = dot_nt(ref[:, 256:384], w_up) * INV_RANK
         v_ref[h * 1024 : (h + 1) * 1024] = (ref[:, 128:256].astype(F32) + add).astype(BF)
-    y = lax.axis_index("y")
-    keys = jnp.concatenate([own_ref[:, 0:128], other_ref[:, 0:128]], axis=0)
-    values = v_ref[...]
-    for s in range(N_Q // Q_STEP):
-        cols = slice(s * Q_STEP, (s + 1) * Q_STEP)
-        w_ref[:, cols] = dot_nt(keys, q_ref[cols, 0:128]) * (SCORE_SCALE * LOG2_E)
-        for half in range(2):
-            q_tok, k_tok = diagonal_mask(half)
-            rows = pl.ds(pl.multiple_of(half * 1024 + y * 256, 256), 256)
-            w_ref[rows, cols] = jnp.where(k_tok <= q_tok[:, cols], w_ref[rows, cols], MASK_VALUE)
-            for block in range(1, 4):
-                @pl.when(block > y)
-                def _():
-                    later = slice(half * 1024 + block * 256, half * 1024 + block * 256 + 256)
-                    w_ref[later, cols] = jnp.full((256, Q_STEP), MASK_VALUE, F32)
-        d_ref[:, cols] = dot_nt(values, q_ref[cols, 128:256])
-        scores = w_ref[:, cols]
-        top = jnp.maximum(jnp.max(scores, axis=0, keepdims=True), LOW_MAX)
-        weight = jnp.exp2(scores - top)
-        w_ref[:, cols] = weight
-        total = jnp.sum(weight, axis=0, keepdims=True)
-        delta = jnp.sum(weight * d_ref[:, cols], axis=0, keepdims=True)
-        some = total > 0.0
-        safe = jnp.where(some, total, 1.0)
-        log_total = jnp.where(some, top + jnp.log2(safe), MASK_VALUE)
-        top_ref[0:1, cols] = top
-        for i in range(4):
-            stat_ref[i, 0:1, cols] = log_total
-            stat_ref[i, 1:2, cols] = delta / safe
-
-
-def second_kernel(q_ref, own_ref, other_ref, w_ref, d_ref, top_ref, stat_ref,
-                  dq_ref, keep_ref, send_ref, dv_ref, dq_acc):
+    q_tok, k_tok = token_ids()
+    queries, cotan = q_ref[:, 0:128], q_ref[:, 128:256]
+    highest = None
+    for start in range(0, N_K, K_BLOCK):
+        ref = low_ref if start < 1024 else high_ref
+        part = slice(start % 1024, start % 1024 + K_BLOCK)
+        rows = slice(start, start + K_BLOCK)
+        scores = jnp.where(k_tok[rows] <= q_tok, dot_nt(ref[part, 0:128], queries), MASK_VALUE)
+        w_ref[rows] = scores
+        block = fold(scores, jnp.max)
+        highest = block if highest is None else jnp.maximum(highest, block)
+    scale = SCORE_SCALE * LOG2_E
+    top = jnp.maximum(jnp.max(highest, axis=0, keepdims=True) * scale, LOW_MAX)
+    total = delta = jnp.zeros((8, N_Q), F32)
+    for start in range(0, N_K, K_BLOCK):
+        rows = slice(start, start + K_BLOCK)
+        weight = jnp.exp2(w_ref[rows] * scale - top)
+        w_ref[rows] = weight
+        d_prob = dot_nt(v_ref[rows], cotan)
+        d_ref[rows] = d_prob
+        total = total + fold(weight, jnp.sum)
+        delta = delta + fold(weight * d_prob, jnp.sum)
+    total = jnp.sum(total, axis=0, keepdims=True)
+    delta = jnp.sum(delta, axis=0, keepdims=True)
+    some = total > 0.0
+    safe = jnp.where(some, total, 1.0)
+    top_ref[...] = top
+    for i in range(4):
+        stat_ref[i, 0:1] = jnp.where(some, top + jnp.log2(safe), MASK_VALUE)
+        stat_ref[i, 1:2] = delta / safe
+
+
+def second_kernel(q_ref, low_ref, high_ref, w_ref, d_ref, top_ref, stat_ref,
+                  dq_ref, dk_ref, dv_ref, dq_acc):
     lse = [stat_ref[i, 0:1, :] for i in range(4)]
     top = jnp.maximum(jnp.maximum(lse[0], lse[1]), jnp.maximum(lse[2], lse[3]))
     share = [jnp.exp2(l - top) for l in lse]
@@ -213,20 +221,19 @@
     queries, cotan = q_ref[:, 0:128], q_ref[:, 128:256]
     for s in range(N_K // K_STEP):
         rows = slice(s * K_STEP, (s + 1) * K_STEP)
-        ref, out = (own_ref, keep_ref) if s < 2 else (other_ref, send_ref)
+        ref = low_ref if s < 2 else high_ref
         part = slice((s % 2) * K_STEP, (s % 2 + 1) * K_STEP)
         prob = w_ref[rows] * factor
         d_score = (prob * (d_ref[rows] - delta)).astype(BF)
         dv_ref[rows] = jnp.dot(prob.astype(BF), cotan, preferred_element_type=F32).astype(BF)
-        d_key = jnp.dot(d_score, queries, preferred_element_type=F32) * SCORE_SCALE
-        out[part] = d_key.astype(out.dtype)
+        dk_ref[rows] = jnp.dot(d_score, queries, preferred_element_type=F32)
         d_query = dot_tn(ref[part, 0:128], d_score)
         if s == 0:
             dq_acc[...] = d_query
         else:
             dq_acc[...] += d_query
     d_query = (dq_acc[...] * SCORE_SCALE).T.astype(BF)
-    low = jnp.concatenate([own_ref[:, 256:384], other_ref[:, 256:384]], axis=0)
+    low = jnp.concatenate([low_ref[:, 256:384], high_ref[:, 256:384]], axis=0)
     high, rest = split(dot_tn(low, dv_ref[...]) * INV_RANK)
     for i in range(4):
         dq_ref[i, 0:256] = d_query[i * 256 : (i + 1) * 256]
@@ -234,6 +241,15 @@
         dq_ref[i, 288:320] = rest[i * 32 : (i + 1) * 32]
 
 
+def scale_kernel(dk_ref, keep_ref, send_ref):
+    core = lax.axis_index("core")
+    for g in range(2):
+        own = pl.ds(pl.multiple_of(g * 1024 + core * 512, 512), 512)
+        other = pl.ds(pl.multiple_of(g * 1024 + (1 - core) * 512, 512), 512)
+        keep_ref[g * 512 : (g + 1) * 512] = dk_ref[own] * SCORE_SCALE
+        send_ref[g * 512 : (g + 1) * 512] = (dk_ref[other] * SCORE_SCALE).astype(BF)
+
+
 def total_of(ref, rows):
     total = ref[0, rows].astype(F32)
     for i in range(1, 4):
@@ -247,11 +263,12 @@
 
 
 def x_sum_kernel(dq_ref, keep_ref, recv_ref, dq_out, out_ref):
+    other = 1 - lax.axis_index("core")
     dq_out[...] = total_of(dq_ref, slice(0, 256)).astype(BF)
     grad = total_of(dq_ref, slice(256, 288)) + total_of(dq_ref, slice(288, 320))
     for y in range(4):
         at = slice(y * 256, (y + 1) * 256)
-        out_ref[y, 0:256] = (keep_ref[at] + recv_ref[at].astype(F32)).astype(BF)
+        out_ref[y, 0:256] = (keep_ref[at] + recv_ref[other, at].astype(F32)).astype(BF)
         out_ref[y, 256:272] = pair(grad[y * 8 : (y + 1) * 8])
 
 
@@ -319,12 +336,17 @@
     )
 
 
+def both_cores(value):
+    return lax.all_gather(value, "core", axis=0)
+
+
 def body(normed, w_down, query, key, value_base, cotangent, master, first, second):
-    part, keep, send = call(
+    (part,) = call(low_kernel, [((8, HALF, RANK), BF)], (), (normed.T, w_down), limit=56)
+    keep, send = call(
         pack_kernel,
-        [((8, HALF, RANK), BF), ((2, HALF, 512), BF), ((2, HALF, 512), BF)],
+        [((2, HALF, 512), BF), ((2, HALF, 512), BF)],
         (),
-        (normed.T, w_down, query.T, cotangent.T, key.T, value_base.T, master),
+        (query.T, cotangent.T, key.T, value_base.T, master),
         [pltpu.VMEM((2, TOK, 512), BF), pltpu.VMEM((8, 256), F32)],
         limit=56,
     )
@@ -333,26 +355,30 @@
     (pieces,) = call(route_kernel, [((4, HALF, 640), BF)], (part, keep, recv))
     pieces = exchange(pieces, "zh").reshape(256, 640)
     k_own = exchange(copies(pieces[:, 256:640], 4), "y")
-    k_other = swap(k_own)
     (q_tile,) = call(mix_kernel, [((4, 256, 256), BF)], (pieces, k_own))
+    k_low = both_cores(k_own[0:512]).reshape(1024, 384)
+    k_high = both_cores(k_own[512:1024]).reshape(1024, 384)
     q_tile = exchange(q_tile, "x").reshape(N_Q, 256)
 
     stat, top, weight, d_prob = call(
         first_kernel,
         [((4, 2, N_Q), F32), ((1, N_Q), F32), ((N_K, N_Q), F32), ((N_K, N_Q), F32)],
-        (q_tile, k_own, k_other),
+        (q_tile, k_low, k_high),
         scratch=[pltpu.VMEM((N_K, LANES), BF)],
-        limit=16,
+        limit=24,
     )
     stats = exchange(stat, "x")
-    dq, dk_keep, dk_send = call(
+    dq, dk = call(
         second_kernel,
-        [((4, 320, LANES), BF), ((1024, LANES), F32), ((1024, LANES), BF)],
-        (q_tile, k_own, k_other, weight, d_prob, top, stats),
+        [((4, 320, LANES), BF), ((N_K, LANES), F32)],
+        (q_tile, k_low, k_high, weight, d_prob, top, stats),
         scratch=[pltpu.VMEM((N_K, LANES), BF), pltpu.VMEM((LANES, N_Q), F32)],
         limit=16,
     )
-    dk_recv = swap(dk_send)
+    dk_keep, dk_send = call(
+        scale_kernel, [((1024, LANES), F32), ((1024, LANES), BF)], (dk,)
+    )
+    dk_recv = both_cores(dk_send)
     dq, dk = call(
         x_sum_kernel,
         [((256, LANES), BF), ((4, 272, LANES), BF)],
@@ -360,7 +386,7 @@
     )
     (back,) = call(y_sum_kernel, [((4, HALF + 16, 256), BF)], (exchange(dk, "y"), dq))
     back = exchange(back, "zh")
-    back = lax.all_gather(back, "core", axis=0)
+    back = both_cores(back)
     q_grad, k_grad, new_master, new_first, new_second = call(
         last_kernel,
         [((2 * HEAD, TOK), BF)] * 2 + [((2, 2 * HEAD), F32)] * 3,

time: 144 us -> 137 us (0.951); the launches traced: 143 us -> 135 us
  blocking collectives: 102 us -> 97.2 us
  starting transfers between devices: 24 us -> 19.6 us
    all_to_all x7 -> x5, blocking collectives: 97.4 us -> 70.2 us  [exchange(): return lax.all_to_all(value, axes, split_axis=0, concat_axis=0, tiled=True)]
    all_gather x1 -> x4, blocking collectives: 4.53 us -> 27 us  [both_cores(): return lax.all_gather(value, 'core', axis=0)]
    ppermute x3 -> x1, starting transfers between devices: 13.9 us -> 2.02 us  [swap(): return lax.ppermute(value, 'core', [(0, 1), (1, 0)])]
    all_to_all x1 -> x3, starting transfers between devices: 10.1 us -> 17.6 us  [exchange(): return lax.all_to_all(value, axes, split_axis=0, concat_axis=0, tiled=True)]
    pallas_call x8 -> x10, Pallas kernels: 12.7 us -> 13.4 us  [call(): pl.pallas_call(kernel, out_shape=[(pltpu.VMEM if pinned else jax.ShapeDty...]
  transfers between devices with their start and end apart: 4 -> 4, of which waited for: 2 -> 3; matrix products, arithmetic and copies ran while one was open for 0% -> 0% of each run, Pallas kernels for 0% -> 1%
where the time goes in v4:
time: 137 us; the launch traced here: 135 us
  blocking collectives  97.2 us (71%)
  starting transfers between devices  19.6 us (14%)
  Pallas kernels  13.4 us (10%)
  waiting for transfers between devices  3.72 us (3%)
    all_to_all x5, blocking collectives, exchange(): return lax.all_to_all(value, axes, split_axis=0, concat_axis=0, tiled=True)  70.2 us
    all_gather x4, blocking collectives, both_cores(): return lax.all_gather(value, 'core', axis=0)  27 us
    all_to_all x3, starting transfers between devices, exchange(): return lax.all_to_all(value, axes, split_axis=0, concat_axis=0, tiled=True)  17.6 us
    pallas_call x10, Pallas kernels, call(): pl.pallas_call(kernel, out_shape=[(pltpu.VMEM if pinned else jax.ShapeDty...  13.4 us
  transfers between devices with their start and end apart: 4, of which 3 were waited for; matrix products, arithmetic and copies ran while one was open for 0% of the time, Pallas kernels for 1%

profile of v4, /device:TPU:1, one launch (start us, length us, event | category | flops | bytes accessed | tf_op | source)
XLA Modules:
  0.0 134.8 jit_solution(5951734476015039668)
XLA Ops:
  0.6 1.8 %shard_map.128 = bf16[8,64,128]{2,1,0:T(8,128)(2,1)} custom-call(bf16[448,128]{1,0:T(8,128)(2,1)} %bitcast.29, bf16[448,128]{1,0:T(8,128)(2,1)} %wd_ref.1), custom_call_target="tpu_custom_call" | custom-call | tf_op jit(solution)/shard_map/pallas_call | solution.py:40
  2.5 10.1 %all-to-all-start = ((bf16[8,64,128]{2,1,0:T(8,128)(2,1)}), bf16[8,64,128]{2,1,0:T(8,128)(2,1)S(1)}, u32[]{:S(2)}, u32[]{:S(2)}) async-start(bf16[8,64,128]{2,1,0:T(8,128)(2,1)} %shard_map.128), calls=%async_computation | async-start | bytes 262144 | tf_op jit(solution)/shard_map/all_to_all | solution.py:326
  12.6 1.2 shard_map.129
  13.8 2.0 %collective-permute-start = (bf16[2,64,512]{2,1,0:T(8,128)(2,1)S(1)}, bf16[2,64,512]{2,1,0:T(8,128)(2,1)S(1)}, u32[]{:S(2)}, u32[]{:S(2)}) collective-permute-start(bf16[2,64,512]{2,1,0:T(8,128)(2,1)S(1)} %get-tuple-element.23), channel_id=1, source_target_pairs={{0,1},{1,0},{2,3},{3,2},{4,5},{5,4},{6,7},{7,6},{8,9},{9,8},{10,11... | collective-permute-start | bytes 393224 | tf_op jit(solution)/shard_map/ppermute | solution.py:330
  15.9 1.2 collective-permute-done.recv_ref
  17.1 1.4 %all-to-all-done.part_ref = bf16[8,64,128]{2,1,0:T(8,128)(2,1)S(1)} async-done(((bf16[8,64,128]{2,1,0:T(8,128)(2,1)}), bf16[8,64,128]{2,1,0:T(8,128)(2,1)S(1)}, u32[]{:S(2)}, u32[]{:S(2)}) %all-to-all-start) | async-done | bytes 131104 | tf_op jit(solution)/shard_map/all_to_all | solution.py:326
  18.5 0.1 shard_map.130
  18.6 26.2 %all_to_all.43 = bf16[4,64,640]{2,1,0:T(8,128)(2,1)S(1)} all-to-all(bf16[4,64,640]{2,1,0:T(8,128)(2,1)S(1)} %shard_map.130), channel_id=1, replica_groups=mesh['y'=4,'zh'=4,'x'=4,'zl'=4,'core'=2] {'zh'}, dimensions={0} | all-to-all | bytes 655360 | tf_op jit(solution)/shard_map/all_to_all | solution.py:326
  44.8 0.1 broadcast_in_dim.2
  44.9 12.3 %all_to_all.44 = bf16[4,256,384]{2,1,0:T(8,128)(2,1)S(1)} all-to-all(bf16[4,256,384]{2,1,0:T(8,128)(2,1)S(1)} %broadcast_in_dim.2), channel_id=1, replica_groups=mesh['y'=4,'zh'=4,'x'=4,'zl'=4,'core'=2] {'y'}, dimensions={0} | all-to-all | bytes 1572864 | tf_op jit(solution)/shard_map/all_to_all | solution.py:326
  57.2 0.9 shard_map.131
  58.1 4.0 %all-to-all-start.3 = ((bf16[4,256,256]{2,1,0:T(8,128)(2,1)}), bf16[4,256,256]{2,1,0:T(8,128)(2,1)S(1)}, u32[]{:S(2)}, u32[]{:S(2)}) async-start(bf16[4,256,256]{2,1,0:T(8,128)(2,1)} %shard_map.131), calls=%async_computation.3 | async-start | bytes 1048576 | tf_op jit(solution)/shard_map/all_to_all | solution.py:326
  62.1 0.1 fusion
  62.2 11.7 %all_gather.25 = bf16[2,512,384]{2,1,0:T(8,128)(2,1)S(1)} all-gather(bf16[1,512,384]{2,1,0:T(8,128)(2,1)S(1)} %bitcast.28), channel_id=1, replica_groups=mesh['y'=4,'zh'=4,'x'=4,'zl'=4,'core'=2] {'core'}, dimensions={0}, use_global_device_ids=true | all-gather | bytes 1179648 | tf_op jit(solution)/shard_map/all_gather | solution.py:340
  74.0 2.4 %all_gather.27 = bf16[2,512,384]{2,1,0:T(8,128)(2,1)S(1)} all-gather(bf16[1,512,384]{2,1,0:T(8,128)(2,1)S(1)} %bitcast.27), channel_id=1, replica_groups=mesh['y'=4,'zh'=4,'x'=4,'zl'=4,'core'=2] {'core'}, dimensions={0}, use_global_device_ids=true | all-gather | bytes 1179648 | tf_op jit(solution)/shard_map/all_gather | solution.py:340
  76.3 0.0 all-to-all-done.3
  76.3 4.4 %shard_map.132 = (f32[4,2,1024]{2,1,0:T(2,128)S(1)}, f32[1,1024]{1,0:T(1,128)S(1)}, f32[2048,1024]{1,0:T(8,128)S(1)}, f32[2048,1024]{1,0:T(8,128)S(1)}) custom-call(bf16[1024,256]{1,0:T(8,128)(2,1)S(1)} %bitcast.21, bf16[1024,384]{1,0:T(8,128)(2,1)S(1)} %bitcast.17, bf16[1024,384]{1,0:T(8,128)(2,1)S(1)} %bitcast.19), custom_call_target="tpu_custom_call" | custom-call | tf_op jit(solution)/shard_map/pallas_call | solution.py:40
  80.7 8.6 %all_to_all.45.stat_ref = f32[4,2,1024]{2,1,0:T(2,128)S(1)} all-to-all(f32[4,2,1024]{2,1,0:T(2,128)S(1)} %get-tuple-element.27), channel_id=1, replica_groups=mesh['y'=4,'zh'=4,'x'=4,'zl'=4,'core'=2] {'x'}, dimensions={0} | all-to-all | bytes 65536 | tf_op jit(solution)/shard_map/all_to_all | solution.py:326
  89.4 0.0 copy-start
  89.4 0.0 copy-start.1
  89.4 0.0 copy-start.2
  89.4 3.8 %shard_map.133 = (bf16[4,320,128]{2,1,0:T(8,128)(2,1)}, f32[2048,128]{1,0:T(8,128)S(1)}) custom-call(bf16[1024,256]{1,0:T(8,128)(2,1)S(1)} %bitcast.22, bf16[1024,384]{1,0:T(8,128)(2,1)S(1)} %bitcast.18, bf16[1024,384]{1,0:T(8,128)(2,1)S(1)} %bitcast.20, f32[2048,1024]{1,0:T(8,128)S(1)} %get-tuple-element.24.w_ref, ...), custom_call_target="tpu_custom_call" | custom-call | tf_op jit(solution)/shard_map/pallas_call | solution.py:40
  93.2 3.5 %all-to-all-start.5 = ((bf16[4,320,128]{2,1,0:T(8,128)(2,1)}), bf16[4,320,128]{2,1,0:T(8,128)(2,1)S(1)}, u32[]{:S(2)}, u32[]{:S(2)}) async-start(bf16[4,320,128]{2,1,0:T(8,128)(2,1)} %get-tuple-element.28), calls=%async_computation.5 | async-start | bytes 655360 | tf_op jit(solution)/shard_map/all_to_all | solution.py:326
  96.7 0.1 shard_map.134
  96.8 4.6 %all-gather = bf16[2048,128]{1,0:T(8,128)(2,1)S(1)} all-gather(bf16[1024,128]{1,0:T(8,128)(2,1)S(1)} %get-tuple-element.31), channel_id=2, replica_groups=mesh['y'=4,'zh'=4,'x'=4,'zl'=4,'core'=2] {'core'}, dimensions={0}, use_global_device_ids=true | all-gather | bytes 786432 | tf_op jit(solution)/shard_map/all_gather | solution.py:340
  101.4 1.1 all-to-all-done.5.dq_ref
  102.5 0.1 shard_map.135
  102.6 8.0 %all_to_all.46.dk_ref = bf16[4,272,128]{2,1,0:T(8,128)(2,1)S(1)} all-to-all(bf16[4,272,128]{2,1,0:T(8,128)(2,1)S(1)} %get-tuple-element.32), channel_id=1, replica_groups=mesh['y'=4,'zh'=4,'x'=4,'zl'=4,'core'=2] {'y'}, dimensions={0} | all-to-all | bytes 557056 | tf_op jit(solution)/shard_map/all_to_all | solution.py:326
  110.6 15.1 %all_to_all.47 = bf16[4,80,256]{2,1,0:T(8,128)(2,1)S(1)} all-to-all(bf16[4,80,256]{2,1,0:T(8,128)(2,1)S(1)} %shard_map.136), channel_id=1, replica_groups=mesh['y'=4,'zh'=4,'x'=4,'zl'=4,'core'=2] {'zh'}, dimensions={0} | all-to-all | bytes 327680 | tf_op jit(solution)/shard_map/all_to_all | solution.py:326
  125.8 8.2 %all-gather.1 = bf16[8,80,256]{2,1,0:T(8,128)(2,1)S(1)} all-gather(bf16[4,80,256]{2,1,0:T(8,128)(2,1)S(1)} %all_to_all.47), channel_id=3, replica_groups=mesh['y'=4,'zh'=4,'x'=4,'zl'=4,'core'=2] {'core'}, dimensions={0}, use_global_device_ids=true | all-gather | bytes 491520 | tf_op jit(solution)/shard_map/all_gather | solution.py:340
  134.0 0.0 copy-done
  134.0 0.0 copy-done.1
  134.0 0.0 copy-done.2
  134.0 0.8 shard_map.137
  (2 shorter events, 0.1 us)
Async XLA Ops:
  2.5 16.0 %all-to-all-start = ((bf16[8,64,128]{2,1,0:T(8,128)(2,1)}), bf16[8,64,128]{2,1,0:T(8,128)(2,1)S(1)}, u32[]{:S(2)}, u32[]{:S(2)}) async-start(bf16[8,64,128]{2,1,0:T(8,128)(2,1)} %shard_map.128), calls=%async_computation | async-start | bytes 262144 | tf_op jit(solution)/shard_map/all_to_all | solution.py:326
  13.8 3.2 %collective-permute-start = (bf16[2,64,512]{2,1,0:T(8,128)(2,1)S(1)}, bf16[2,64,512]{2,1,0:T(8,128)(2,1)S(1)}, u32[]{:S(2)}, u32[]{:S(2)}) collective-permute-start(bf16[2,64,512]{2,1,0:T(8,128)(2,1)S(1)} %get-tuple-element.23), channel_id=1, source_target_pairs={{0,1},{1,0},{2,3},{3,2},{4,5},{5,4},{6,7},{7,6},{8,9},{9,8},{10,11... | collective-permute-start | bytes 393224 | tf_op jit(solution)/shard_map/ppermute | solution.py:330
  58.1 18.2 %all-to-all-start.3 = ((bf16[4,256,256]{2,1,0:T(8,128)(2,1)}), bf16[4,256,256]{2,1,0:T(8,128)(2,1)S(1)}, u32[]{:S(2)}, u32[]{:S(2)}) async-start(bf16[4,256,256]{2,1,0:T(8,128)(2,1)} %shard_map.131), calls=%async_computation.3 | async-start | bytes 1048576 | tf_op jit(solution)/shard_map/all_to_all | solution.py:326
  89.4 44.6 %copy-start = (f32[2,224]{1,0:T(2,128)S(1)}, f32[2,224]{1,0:T(2,128)}, u32[]{:S(2)}) copy-start(f32[2,224]{1,0:T(2,128)} %master_ref.1) | copy-start | bytes 5380
  89.4 44.6 %copy-start.1 = (f32[2,224]{1,0:T(2,128)S(1)}, f32[2,224]{1,0:T(2,128)}, u32[]{:S(2)}) copy-start(f32[2,224]{1,0:T(2,128)} %first_ref.1) | copy-start | bytes 5380
  89.4 44.6 %copy-start.2 = (f32[2,224]{1,0:T(2,128)S(1)}, f32[2,224]{1,0:T(2,128)}, u32[]{:S(2)}) copy-start(f32[2,224]{1,0:T(2,128)} %second_ref.1) | copy-start | bytes 5380
  93.2 9.3 %all-to-all-start.5 = ((bf16[4,320,128]{2,1,0:T(8,128)(2,1)}), bf16[4,320,128]{2,1,0:T(8,128)(2,1)S(1)}, u32[]{:S(2)}, u32[]{:S(2)}) async-start(bf16[4,320,128]{2,1,0:T(8,128)(2,1)} %get-tuple-element.28), calls=%async_computation.5 | async-start | bytes 655360 | tf_op jit(solution)/shard_map/all_to_all | solution.py:326

commit v5 on v4

--- a/solution.py
+++ b/solution.py
@@ -78,10 +78,14 @@
 
 
 def low_kernel(x_ref, wd_ref, part_ref):
-    part = dot_tn(x_ref[...], wd_ref[...]).astype(BF)
-    for s in range(8):
-        h = s % 2
-        part_ref[s] = part[h * HALF : (h + 1) * HALF]
+    part_ref[...] = dot_tn(x_ref[...], wd_ref[...])
+
+
+def half_kernel(part_ref, out_ref):
+    rows = pl.ds(pl.multiple_of(lax.axis_index("core") * HALF, HALF), HALF)
+    total = part_ref[0, rows] + part_ref[1, rows]
+    for s in range(4):
+        out_ref[s] = total
 
 
 def pack_kernel(q_ref, do_ref, k_ref, vb_ref, m_ref, keep_ref, send_ref, full, w_pad):
@@ -115,9 +119,7 @@
 
 def route_kernel(part_ref, keep_ref, recv_ref, out_ref):
     core = lax.axis_index("core")
-    total = part_ref[0].astype(F32)
-    for s in range(1, 8):
-        total = total + part_ref[s].astype(F32)
+    total = part_ref[0] + part_ref[1] + part_ref[2] + part_ref[3]
     src, dst = iotas(RANK, RANK)
     order = one_hot(src == rank_of(dst))
     low = jnp.dot(total.astype(BF), order, preferred_element_type=F32).astype(BF)
@@ -341,7 +343,8 @@
 
 
 def body(normed, w_down, query, key, value_base, cotangent, master, first, second):
-    (part,) = call(low_kernel, [((8, HALF, RANK), BF)], (), (normed.T, w_down), limit=56)
+    (part,) = call(low_kernel, [((TOK, RANK), F32)], (), (normed.T, w_down), limit=56)
+    (part,) = call(half_kernel, [((4, HALF, RANK), F32)], (both_cores(part),))
     keep, send = call(
         pack_kernel,
         [((2, HALF, 512), BF), ((2, HALF, 512), BF)],
@@ -350,7 +353,7 @@
         [pltpu.VMEM((2, TOK, 512), BF), pltpu.VMEM((8, 256), F32)],
         limit=56,
     )
-    part = exchange(part, ("zl", "core"))
+    part = exchange(part, "zl")
     recv = swap(send)
     (pieces,) = call(route_kernel, [((4, HALF, 640), BF)], (part, keep, recv))
     pieces = exchange(pieces, "zh").reshape(256, 640)

time: 137 us -> 137 us (level)
  blocking collectives: 97.2 us -> 106 us
  starting transfers between devices: 19.6 us -> 13 us
    all_gather x4 -> x5, blocking collectives: 27 us -> 37.8 us  [both_cores(): return lax.all_gather(value, 'core', axis=0)]
    all_to_all x3, starting transfers between devices: 17.6 us -> 10.8 us  [exchange(): return lax.all_to_all(value, axes, split_axis=0, concat_axis=0, tiled=True)]
    all_to_all x5, blocking collectives: 70.2 us -> 67.7 us  [exchange(): return lax.all_to_all(value, axes, split_axis=0, concat_axis=0, tiled=True)]
    pallas_call x10 -> x11, Pallas kernels: 13.4 us -> 13.4 us  [call(): pl.pallas_call(kernel, out_shape=[(pltpu.VMEM if pinned else jax.ShapeDty...]
where the time goes in v5:
time: 137 us; the launch traced here: 135 us
  blocking collectives  106 us (77%)
  Pallas kernels  13.4 us (10%)
  starting transfers between devices  13 us (9%)
  waiting for transfers between devices  2.46 us (2%)
    all_to_all x5, blocking collectives, exchange(): return lax.all_to_all(value, axes, split_axis=0, concat_axis=0, tiled=True)  67.7 us
    all_gather x5, blocking collectives, both_cores(): return lax.all_gather(value, 'core', axis=0)  37.8 us
    pallas_call x11, Pallas kernels, call(): pl.pallas_call(kernel, out_shape=[(pltpu.VMEM if pinned else jax.ShapeDty...  13.4 us
    all_to_all x3, starting transfers between devices, exchange(): return lax.all_to_all(value, axes, split_axis=0, concat_axis=0, tiled=True)  10.8 us
  transfers between devices with their start and end apart: 4, of which 3 were waited for; matrix products, arithmetic and copies ran while one was open for 0% of the time, Pallas kernels for 1%

profile of v5, /device:TPU:1, one launch (start us, length us, event | category | flops | bytes accessed | tf_op | source)
XLA Modules:
  0.0 135.3 jit_solution(15371114047493861195)
XLA Ops:
  0.6 1.2 shard_map.128
  1.8 8.4 %all-gather = f32[256,128]{1,0:T(8,128)S(1)} all-gather(f32[128,128]{1,0:T(8,128)S(1)} %shard_map.128), channel_id=2, replica_groups=mesh['y'=4,'zh'=4,'x'=4,'zl'=4,'core'=2] {'core'}, dimensions={0}, use_global_device_ids=true | all-gather | bytes 196608 | tf_op jit(solution)/shard_map/all_gather | solution.py:342
  10.2 0.7 shard_map.129
  10.9 3.3 %all-to-all-start = ((f32[4,64,128]{2,1,0:T(8,128)}), f32[4,64,128]{2,1,0:T(8,128)S(1)}, u32[]{:S(2)}, u32[]{:S(2)}) async-start(f32[4,64,128]{2,1,0:T(8,128)} %shard_map.129), calls=%async_computation | async-start | bytes 262144 | tf_op jit(solution)/shard_map/all_to_all | solution.py:328
  14.2 1.2 shard_map.130
  15.4 2.3 %collective-permute-start = (bf16[2,64,512]{2,1,0:T(8,128)(2,1)S(1)}, bf16[2,64,512]{2,1,0:T(8,128)(2,1)S(1)}, u32[]{:S(2)}, u32[]{:S(2)}) collective-permute-start(bf16[2,64,512]{2,1,0:T(8,128)(2,1)S(1)} %get-tuple-element.23), channel_id=1, source_target_pairs={{0,1},{1,0},{2,3},{3,2},{4,5},{5,4},{6,7},{7,6},{8,9},{9,8},{10,11... | collective-permute-start | bytes 393224 | tf_op jit(solution)/shard_map/ppermute | solution.py:332
  17.7 1.0 collective-permute-done.recv_ref
  18.7 0.4 all-to-all-done.part_ref
  19.1 0.1 shard_map.131
  19.2 23.8 %all_to_all.43 = bf16[4,64,640]{2,1,0:T(8,128)(2,1)S(1)} all-to-all(bf16[4,64,640]{2,1,0:T(8,128)(2,1)S(1)} %shard_map.131), channel_id=1, replica_groups=mesh['y'=4,'zh'=4,'x'=4,'zl'=4,'core'=2] {'zh'}, dimensions={0} | all-to-all | bytes 655360 | tf_op jit(solution)/shard_map/all_to_all | solution.py:328
  43.0 0.1 broadcast_in_dim.2
  43.1 12.3 %all_to_all.44 = bf16[4,256,384]{2,1,0:T(8,128)(2,1)S(1)} all-to-all(bf16[4,256,384]{2,1,0:T(8,128)(2,1)S(1)} %broadcast_in_dim.2), channel_id=1, replica_groups=mesh['y'=4,'zh'=4,'x'=4,'zl'=4,'core'=2] {'y'}, dimensions={0} | all-to-all | bytes 1572864 | tf_op jit(solution)/shard_map/all_to_all | solution.py:328
  55.4 0.9 shard_map.132
  56.4 4.0 %all-to-all-start.3 = ((bf16[4,256,256]{2,1,0:T(8,128)(2,1)}), bf16[4,256,256]{2,1,0:T(8,128)(2,1)S(1)}, u32[]{:S(2)}, u32[]{:S(2)}) async-start(bf16[4,256,256]{2,1,0:T(8,128)(2,1)} %shard_map.132), calls=%async_computation.3 | async-start | bytes 1048576 | tf_op jit(solution)/shard_map/all_to_all | solution.py:328
  60.4 0.1 fusion
  60.4 14.0 %all_gather.33 = bf16[2,512,384]{2,1,0:T(8,128)(2,1)S(1)} all-gather(bf16[1,512,384]{2,1,0:T(8,128)(2,1)S(1)} %bitcast.30), channel_id=1, replica_groups=mesh['y'=4,'zh'=4,'x'=4,'zl'=4,'core'=2] {'core'}, dimensions={0}, use_global_device_ids=true | all-gather | bytes 1179648 | tf_op jit(solution)/shard_map/all_gather | solution.py:342
  74.4 2.4 %all_gather.35 = bf16[2,512,384]{2,1,0:T(8,128)(2,1)S(1)} all-gather(bf16[1,512,384]{2,1,0:T(8,128)(2,1)S(1)} %bitcast.29), channel_id=1, replica_groups=mesh['y'=4,'zh'=4,'x'=4,'zl'=4,'core'=2] {'core'}, dimensions={0}, use_global_device_ids=true | all-gather | bytes 1179648 | tf_op jit(solution)/shard_map/all_gather | solution.py:342
  76.8 0.0 all-to-all-done.3
  76.8 4.4 %shard_map.133 = (f32[4,2,1024]{2,1,0:T(2,128)S(1)}, f32[1,1024]{1,0:T(1,128)S(1)}, f32[2048,1024]{1,0:T(8,128)S(1)}, f32[2048,1024]{1,0:T(8,128)S(1)}) custom-call(bf16[1024,256]{1,0:T(8,128)(2,1)S(1)} %bitcast.22, bf16[1024,384]{1,0:T(8,128)(2,1)S(1)} %bitcast.18, bf16[1024,384]{1,0:T(8,128)(2,1)S(1)} %bitcast.20), custom_call_target="tpu_custom_call" | custom-call | tf_op jit(solution)/shard_map/pallas_call | solution.py:40
  81.2 8.6 %all_to_all.45.stat_ref = f32[4,2,1024]{2,1,0:T(2,128)S(1)} all-to-all(f32[4,2,1024]{2,1,0:T(2,128)S(1)} %get-tuple-element.27), channel_id=1, replica_groups=mesh['y'=4,'zh'=4,'x'=4,'zl'=4,'core'=2] {'x'}, dimensions={0} | all-to-all | bytes 65536 | tf_op jit(solution)/shard_map/all_to_all | solution.py:328
  89.8 0.0 copy-start
  89.8 0.0 copy-start.1
  89.8 0.0 copy-start.2
  89.8 3.8 %shard_map.134 = (bf16[4,320,128]{2,1,0:T(8,128)(2,1)}, f32[2048,128]{1,0:T(8,128)S(1)}) custom-call(bf16[1024,256]{1,0:T(8,128)(2,1)S(1)} %bitcast.23, bf16[1024,384]{1,0:T(8,128)(2,1)S(1)} %bitcast.19, bf16[1024,384]{1,0:T(8,128)(2,1)S(1)} %bitcast.21, f32[2048,1024]{1,0:T(8,128)S(1)} %get-tuple-element.24.w_ref, ...), custom_call_target="tpu_custom_call" | custom-call | tf_op jit(solution)/shard_map/pallas_call | solution.py:40
  93.7 3.5 %all-to-all-start.5 = ((bf16[4,320,128]{2,1,0:T(8,128)(2,1)}), bf16[4,320,128]{2,1,0:T(8,128)(2,1)S(1)}, u32[]{:S(2)}, u32[]{:S(2)}) async-start(bf16[4,320,128]{2,1,0:T(8,128)(2,1)} %get-tuple-element.28), calls=%async_computation.5 | async-start | bytes 655360 | tf_op jit(solution)/shard_map/all_to_all | solution.py:328
  97.1 0.1 shard_map.135
  97.2 4.6 %all-gather.1 = bf16[2048,128]{1,0:T(8,128)(2,1)S(1)} all-gather(bf16[1024,128]{1,0:T(8,128)(2,1)S(1)} %get-tuple-element.31), channel_id=3, replica_groups=mesh['y'=4,'zh'=4,'x'=4,'zl'=4,'core'=2] {'core'}, dimensions={0}, use_global_device_ids=true | all-gather | bytes 786432 | tf_op jit(solution)/shard_map/all_gather | solution.py:342
  101.9 1.1 all-to-all-done.5.dq_ref
  103.0 0.1 shard_map.136
  103.1 8.0 %all_to_all.46.dk_ref = bf16[4,272,128]{2,1,0:T(8,128)(2,1)S(1)} all-to-all(bf16[4,272,128]{2,1,0:T(8,128)(2,1)S(1)} %get-tuple-element.32), channel_id=1, replica_groups=mesh['y'=4,'zh'=4,'x'=4,'zl'=4,'core'=2] {'y'}, dimensions={0} | all-to-all | bytes 557056 | tf_op jit(solution)/shard_map/all_to_all | solution.py:328
  111.1 15.0 %all_to_all.47 = bf16[4,80,256]{2,1,0:T(8,128)(2,1)S(1)} all-to-all(bf16[4,80,256]{2,1,0:T(8,128)(2,1)S(1)} %shard_map.137), channel_id=1, replica_groups=mesh['y'=4,'zh'=4,'x'=4,'zl'=4,'core'=2] {'zh'}, dimensions={0} | all-to-all | bytes 327680 | tf_op jit(solution)/shard_map/all_to_all | solution.py:328
  126.1 8.4 %all-gather.2 = bf16[8,80,256]{2,1,0:T(8,128)(2,1)S(1)} all-gather(bf16[4,80,256]{2,1,0:T(8,128)(2,1)S(1)} %all_to_all.47), channel_id=4, replica_groups=mesh['y'=4,'zh'=4,'x'=4,'zl'=4,'core'=2] {'core'}, dimensions={0}, use_global_device_ids=true | all-gather | bytes 491520 | tf_op jit(solution)/shard_map/all_gather | solution.py:342
  134.6 0.0 copy-done
  134.6 0.0 copy-done.1
  134.6 0.0 copy-done.2
  134.6 0.8 shard_map.138
  (2 shorter events, 0.1 us)
Async XLA Ops:
  10.9 8.2 %all-to-all-start = ((f32[4,64,128]{2,1,0:T(8,128)}), f32[4,64,128]{2,1,0:T(8,128)S(1)}, u32[]{:S(2)}, u32[]{:S(2)}) async-start(f32[4,64,128]{2,1,0:T(8,128)} %shard_map.129), calls=%async_computation | async-start | bytes 262144 | tf_op jit(solution)/shard_map/all_to_all | solution.py:328
  15.4 3.2 %collective-permute-start = (bf16[2,64,512]{2,1,0:T(8,128)(2,1)S(1)}, bf16[2,64,512]{2,1,0:T(8,128)(2,1)S(1)}, u32[]{:S(2)}, u32[]{:S(2)}) collective-permute-start(bf16[2,64,512]{2,1,0:T(8,128)(2,1)S(1)} %get-tuple-element.23), channel_id=1, source_target_pairs={{0,1},{1,0},{2,3},{3,2},{4,5},{5,4},{6,7},{7,6},{8,9},{9,8},{10,11... | collective-permute-start | bytes 393224 | tf_op jit(solution)/shard_map/ppermute | solution.py:332
  56.4 20.4 %all-to-all-start.3 = ((bf16[4,256,256]{2,1,0:T(8,128)(2,1)}), bf16[4,256,256]{2,1,0:T(8,128)(2,1)S(1)}, u32[]{:S(2)}, u32[]{:S(2)}) async-start(bf16[4,256,256]{2,1,0:T(8,128)(2,1)} %shard_map.132), calls=%async_computation.3 | async-start | bytes 1048576 | tf_op jit(solution)/shard_map/all_to_all | solution.py:328
  89.8 44.7 %copy-start = (f32[2,224]{1,0:T(2,128)S(1)}, f32[2,224]{1,0:T(2,128)}, u32[]{:S(2)}) copy-start(f32[2,224]{1,0:T(2,128)} %master_ref.1) | copy-start | bytes 5380
  89.8 44.7 %copy-start.1 = (f32[2,224]{1,0:T(2,128)S(1)}, f32[2,224]{1,0:T(2,128)}, u32[]{:S(2)}) copy-start(f32[2,224]{1,0:T(2,128)} %first_ref.1) | copy-start | bytes 5380
  89.8 44.7 %copy-start.2 = (f32[2,224]{1,0:T(2,128)S(1)}, f32[2,224]{1,0:T(2,128)}, u32[]{:S(2)}) copy-start(f32[2,224]{1,0:T(2,128)} %second_ref.1) | copy-start | bytes 5380
  93.7 9.3 %all-to-all-start.5 = ((bf16[4,320,128]{2,1,0:T(8,128)(2,1)}), bf16[4,320,128]{2,1,0:T(8,128)(2,1)S(1)}, u32[]{:S(2)}, u32[]{:S(2)}) async-start(bf16[4,320,128]{2,1,0:T(8,128)(2,1)} %get-tuple-element.28), calls=%async_computation.5 | async-start | bytes 655360 | tf_op jit(solution)/shard_map/all_to_all | solution.py:328

commit v6 on v5

--- a/solution.py
+++ b/solution.py
@@ -98,7 +98,7 @@
     w_pad[...] = jnp.zeros_like(w_pad)
     w_pad[0:2, 0 : 2 * HEAD] = m_ref[...]
     rows = w_pad[...].astype(BF)
-    src, dst = iotas(8, LANES)
+    src, dst = iotas(16, LANES)
     for h in range(2):
         spread = sum(
             dot_tn(
@@ -350,7 +350,7 @@
         [((2, HALF, 512), BF), ((2, HALF, 512), BF)],
         (),
         (query.T, cotangent.T, key.T, value_base.T, master),
-        [pltpu.VMEM((2, TOK, 512), BF), pltpu.VMEM((8, 256), F32)],
+        [pltpu.VMEM((2, TOK, 512), BF), pltpu.VMEM((16, 256), F32)],
         limit=56,
     )
     part = exchange(part, "zl")

time: 137 us -> 137 us (level)
  no operation moved by 1% of the time
where the time goes in v6:
time: 137 us; the launch traced here: 135 us
  blocking collectives  106 us (77%)
  Pallas kernels  13.4 us (10%)
  starting transfers between devices  13 us (9%)
  waiting for transfers between devices  2.46 us (2%)
    all_to_all x5, blocking collectives, exchange(): return lax.all_to_all(value, axes, split_axis=0, concat_axis=0, tiled=True)  67.7 us
    all_gather x5, blocking collectives, both_cores(): return lax.all_gather(value, 'core', axis=0)  37.8 us
    pallas_call x11, Pallas kernels, call(): pl.pallas_call(kernel, out_shape=[(pltpu.VMEM if pinned else jax.ShapeDty...  13.4 us
    all_to_all x3, starting transfers between devices, exchange(): return lax.all_to_all(value, axes, split_axis=0, concat_axis=0, tiled=True)  10.8 us
  transfers between devices with their start and end apart: 4, of which 3 were waited for; matrix products, arithmetic and copies ran while one was open for 0% of the time, Pallas kernels for 1%

profile of v6, /device:TPU:1, one launch (start us, length us, event | category | flops | bytes accessed | tf_op | source)
XLA Modules:
  0.0 135.3 jit_solution(13490136658114603294)
XLA Ops:
  0.6 1.2 shard_map.128
  1.8 8.4 %all-gather = f32[256,128]{1,0:T(8,128)S(1)} all-gather(f32[128,128]{1,0:T(8,128)S(1)} %shard_map.128), channel_id=2, replica_groups=mesh['y'=4,'zh'=4,'x'=4,'zl'=4,'core'=2] {'core'}, dimensions={0}, use_global_device_ids=true | all-gather | bytes 196608 | tf_op jit(solution)/shard_map/all_gather | solution.py:342
  10.2 0.7 shard_map.129
  10.9 3.3 %all-to-all-start = ((f32[4,64,128]{2,1,0:T(8,128)}), f32[4,64,128]{2,1,0:T(8,128)S(1)}, u32[]{:S(2)}, u32[]{:S(2)}) async-start(f32[4,64,128]{2,1,0:T(8,128)} %shard_map.129), calls=%async_computation | async-start | bytes 262144 | tf_op jit(solution)/shard_map/all_to_all | solution.py:328
  14.2 1.2 shard_map.130
  15.4 2.3 %collective-permute-start = (bf16[2,64,512]{2,1,0:T(8,128)(2,1)S(1)}, bf16[2,64,512]{2,1,0:T(8,128)(2,1)S(1)}, u32[]{:S(2)}, u32[]{:S(2)}) collective-permute-start(bf16[2,64,512]{2,1,0:T(8,128)(2,1)S(1)} %get-tuple-element.23), channel_id=1, source_target_pairs={{0,1},{1,0},{2,3},{3,2},{4,5},{5,4},{6,7},{7,6},{8,9},{9,8},{10,11... | collective-permute-start | bytes 393224 | tf_op jit(solution)/shard_map/ppermute | solution.py:332
  17.7 1.0 collective-permute-done.recv_ref
  18.7 0.4 all-to-all-done.part_ref
  19.1 0.1 shard_map.131
  19.2 23.8 %all_to_all.43 = bf16[4,64,640]{2,1,0:T(8,128)(2,1)S(1)} all-to-all(bf16[4,64,640]{2,1,0:T(8,128)(2,1)S(1)} %shard_map.131), channel_id=1, replica_groups=mesh['y'=4,'zh'=4,'x'=4,'zl'=4,'core'=2] {'zh'}, dimensions={0} | all-to-all | bytes 655360 | tf_op jit(solution)/shard_map/all_to_all | solution.py:328
  43.0 0.1 broadcast_in_dim.2
  43.1 12.3 %all_to_all.44 = bf16[4,256,384]{2,1,0:T(8,128)(2,1)S(1)} all-to-all(bf16[4,256,384]{2,1,0:T(8,128)(2,1)S(1)} %broadcast_in_dim.2), channel_id=1, replica_groups=mesh['y'=4,'zh'=4,'x'=4,'zl'=4,'core'=2] {'y'}, dimensions={0} | all-to-all | bytes 1572864 | tf_op jit(solution)/shard_map/all_to_all | solution.py:328
  55.4 0.9 shard_map.132
  56.4 4.0 %all-to-all-start.3 = ((bf16[4,256,256]{2,1,0:T(8,128)(2,1)}), bf16[4,256,256]{2,1,0:T(8,128)(2,1)S(1)}, u32[]{:S(2)}, u32[]{:S(2)}) async-start(bf16[4,256,256]{2,1,0:T(8,128)(2,1)} %shard_map.132), calls=%async_computation.3 | async-start | bytes 1048576 | tf_op jit(solution)/shard_map/all_to_all | solution.py:328
  60.4 0.1 fusion
  60.4 14.0 %all_gather.33 = bf16[2,512,384]{2,1,0:T(8,128)(2,1)S(1)} all-gather(bf16[1,512,384]{2,1,0:T(8,128)(2,1)S(1)} %bitcast.30), channel_id=1, replica_groups=mesh['y'=4,'zh'=4,'x'=4,'zl'=4,'core'=2] {'core'}, dimensions={0}, use_global_device_ids=true | all-gather | bytes 1179648 | tf_op jit(solution)/shard_map/all_gather | solution.py:342
  74.4 2.4 %all_gather.35 = bf16[2,512,384]{2,1,0:T(8,128)(2,1)S(1)} all-gather(bf16[1,512,384]{2,1,0:T(8,128)(2,1)S(1)} %bitcast.29), channel_id=1, replica_groups=mesh['y'=4,'zh'=4,'x'=4,'zl'=4,'core'=2] {'core'}, dimensions={0}, use_global_device_ids=true | all-gather | bytes 1179648 | tf_op jit(solution)/shard_map/all_gather | solution.py:342
  76.8 0.0 all-to-all-done.3
  76.8 4.4 %shard_map.133 = (f32[4,2,1024]{2,1,0:T(2,128)S(1)}, f32[1,1024]{1,0:T(1,128)S(1)}, f32[2048,1024]{1,0:T(8,128)S(1)}, f32[2048,1024]{1,0:T(8,128)S(1)}) custom-call(bf16[1024,256]{1,0:T(8,128)(2,1)S(1)} %bitcast.22, bf16[1024,384]{1,0:T(8,128)(2,1)S(1)} %bitcast.18, bf16[1024,384]{1,0:T(8,128)(2,1)S(1)} %bitcast.20), custom_call_target="tpu_custom_call" | custom-call | tf_op jit(solution)/shard_map/pallas_call | solution.py:40
  81.2 8.6 %all_to_all.45.stat_ref = f32[4,2,1024]{2,1,0:T(2,128)S(1)} all-to-all(f32[4,2,1024]{2,1,0:T(2,128)S(1)} %get-tuple-element.27), channel_id=1, replica_groups=mesh['y'=4,'zh'=4,'x'=4,'zl'=4,'core'=2] {'x'}, dimensions={0} | all-to-all | bytes 65536 | tf_op jit(solution)/shard_map/all_to_all | solution.py:328
  89.8 0.0 copy-start
  89.8 0.0 copy-start.1
  89.8 0.0 copy-start.2
  89.8 3.8 %shard_map.134 = (bf16[4,320,128]{2,1,0:T(8,128)(2,1)}, f32[2048,128]{1,0:T(8,128)S(1)}) custom-call(bf16[1024,256]{1,0:T(8,128)(2,1)S(1)} %bitcast.23, bf16[1024,384]{1,0:T(8,128)(2,1)S(1)} %bitcast.19, bf16[1024,384]{1,0:T(8,128)(2,1)S(1)} %bitcast.21, f32[2048,1024]{1,0:T(8,128)S(1)} %get-tuple-element.24.w_ref, ...), custom_call_target="tpu_custom_call" | custom-call | tf_op jit(solution)/shard_map/pallas_call | solution.py:40
  93.7 3.5 %all-to-all-start.5 = ((bf16[4,320,128]{2,1,0:T(8,128)(2,1)}), bf16[4,320,128]{2,1,0:T(8,128)(2,1)S(1)}, u32[]{:S(2)}, u32[]{:S(2)}) async-start(bf16[4,320,128]{2,1,0:T(8,128)(2,1)} %get-tuple-element.28), calls=%async_computation.5 | async-start | bytes 655360 | tf_op jit(solution)/shard_map/all_to_all | solution.py:328
  97.1 0.1 shard_map.135
  97.2 4.6 %all-gather.1 = bf16[2048,128]{1,0:T(8,128)(2,1)S(1)} all-gather(bf16[1024,128]{1,0:T(8,128)(2,1)S(1)} %get-tuple-element.31), channel_id=3, replica_groups=mesh['y'=4,'zh'=4,'x'=4,'zl'=4,'core'=2] {'core'}, dimensions={0}, use_global_device_ids=true | all-gather | bytes 786432 | tf_op jit(solution)/shard_map/all_gather | solution.py:342
  101.9 1.1 all-to-all-done.5.dq_ref
  103.0 0.1 shard_map.136
  103.1 8.0 %all_to_all.46.dk_ref = bf16[4,272,128]{2,1,0:T(8,128)(2,1)S(1)} all-to-all(bf16[4,272,128]{2,1,0:T(8,128)(2,1)S(1)} %get-tuple-element.32), channel_id=1, replica_groups=mesh['y'=4,'zh'=4,'x'=4,'zl'=4,'core'=2] {'y'}, dimensions={0} | all-to-all | bytes 557056 | tf_op jit(solution)/shard_map/all_to_all | solution.py:328
  111.1 15.0 %all_to_all.47 = bf16[4,80,256]{2,1,0:T(8,128)(2,1)S(1)} all-to-all(bf16[4,80,256]{2,1,0:T(8,128)(2,1)S(1)} %shard_map.137), channel_id=1, replica_groups=mesh['y'=4,'zh'=4,'x'=4,'zl'=4,'core'=2] {'zh'}, dimensions={0} | all-to-all | bytes 327680 | tf_op jit(solution)/shard_map/all_to_all | solution.py:328
  126.1 8.4 %all-gather.2 = bf16[8,80,256]{2,1,0:T(8,128)(2,1)S(1)} all-gather(bf16[4,80,256]{2,1,0:T(8,128)(2,1)S(1)} %all_to_all.47), channel_id=4, replica_groups=mesh['y'=4,'zh'=4,'x'=4,'zl'=4,'core'=2] {'core'}, dimensions={0}, use_global_device_ids=true | all-gather | bytes 491520 | tf_op jit(solution)/shard_map/all_gather | solution.py:342
  134.6 0.0 copy-done
  134.6 0.0 copy-done.1
  134.6 0.0 copy-done.2
  134.6 0.8 shard_map.138
  (2 shorter events, 0.1 us)
Async XLA Ops:
  10.9 8.2 %all-to-all-start = ((f32[4,64,128]{2,1,0:T(8,128)}), f32[4,64,128]{2,1,0:T(8,128)S(1)}, u32[]{:S(2)}, u32[]{:S(2)}) async-start(f32[4,64,128]{2,1,0:T(8,128)} %shard_map.129), calls=%async_computation | async-start | bytes 262144 | tf_op jit(solution)/shard_map/all_to_all | solution.py:328
  15.4 3.2 %collective-permute-start = (bf16[2,64,512]{2,1,0:T(8,128)(2,1)S(1)}, bf16[2,64,512]{2,1,0:T(8,128)(2,1)S(1)}, u32[]{:S(2)}, u32[]{:S(2)}) collective-permute-start(bf16[2,64,512]{2,1,0:T(8,128)(2,1)S(1)} %get-tuple-element.23), channel_id=1, source_target_pairs={{0,1},{1,0},{2,3},{3,2},{4,5},{5,4},{6,7},{7,6},{8,9},{9,8},{10,11... | collective-permute-start | bytes 393224 | tf_op jit(solution)/shard_map/ppermute | solution.py:332
  56.4 20.4 %all-to-all-start.3 = ((bf16[4,256,256]{2,1,0:T(8,128)(2,1)}), bf16[4,256,256]{2,1,0:T(8,128)(2,1)S(1)}, u32[]{:S(2)}, u32[]{:S(2)}) async-start(bf16[4,256,256]{2,1,0:T(8,128)(2,1)} %shard_map.132), calls=%async_computation.3 | async-start | bytes 1048576 | tf_op jit(solution)/shard_map/all_to_all | solution.py:328
  89.8 44.7 %copy-start = (f32[2,224]{1,0:T(2,128)S(1)}, f32[2,224]{1,0:T(2,128)}, u32[]{:S(2)}) copy-start(f32[2,224]{1,0:T(2,128)} %master_ref.1) | copy-start | bytes 5380
  89.8 44.7 %copy-start.1 = (f32[2,224]{1,0:T(2,128)S(1)}, f32[2,224]{1,0:T(2,128)}, u32[]{:S(2)}) copy-start(f32[2,224]{1,0:T(2,128)} %first_ref.1) | copy-start | bytes 5380
  89.8 44.7 %copy-start.2 = (f32[2,224]{1,0:T(2,128)S(1)}, f32[2,224]{1,0:T(2,128)}, u32[]{:S(2)}) copy-start(f32[2,224]{1,0:T(2,128)} %second_ref.1) | copy-start | bytes 5380
  93.7 9.3 %all-to-all-start.5 = ((bf16[4,320,128]{2,1,0:T(8,128)(2,1)}), bf16[4,320,128]{2,1,0:T(8,128)(2,1)S(1)}, u32[]{:S(2)}, u32[]{:S(2)}) async-start(bf16[4,320,128]{2,1,0:T(8,128)(2,1)} %get-tuple-element.28), calls=%async_computation.5 | async-start | bytes 655360 | tf_op jit(solution)/shard_map/all_to_all | solution.py:328

commit v7 on v6

--- a/solution.py
+++ b/solution.py
@@ -77,19 +77,21 @@
     return high, (value - high.astype(F32)).astype(BF)
 
 
-def low_kernel(x_ref, wd_ref, part_ref):
-    part_ref[...] = dot_tn(x_ref[...], wd_ref[...])
-
-
-def half_kernel(part_ref, out_ref):
-    rows = pl.ds(pl.multiple_of(lax.axis_index("core") * HALF, HALF), HALF)
-    total = part_ref[0, rows] + part_ref[1, rows]
+def half_kernel(part_ref, both_ref, out_ref):
+    other = 1 - lax.axis_index("core")
+    total = (
+        part_ref[...]
+        + both_ref[other, :, 1024:1152].astype(F32)
+        + both_ref[other, :, 1152:1280].astype(F32)
+    )
     for s in range(4):
         out_ref[s] = total
 
 
-def pack_kernel(q_ref, do_ref, k_ref, vb_ref, m_ref, keep_ref, send_ref, full, w_pad):
+def pack_kernel(x_ref, wd_ref, q_ref, do_ref, k_ref, vb_ref, m_ref,
+                part_ref, keep_ref, send_ref, full, w_pad, low):
     core = lax.axis_index("core")
+    low[...] = dot_tn(x_ref[...], wd_ref[...])
     full[...] = jnp.zeros_like(full)
     for i, ref in enumerate((q_ref, do_ref, k_ref, vb_ref)):
         for h in range(2):
@@ -114,10 +116,12 @@
     other = pl.ds(pl.multiple_of((1 - core) * HALF, HALF), HALF)
     for h in range(2):
         keep_ref[h] = full[h, own, :]
-        send_ref[h] = full[h, other, :]
-
-
-def route_kernel(part_ref, keep_ref, recv_ref, out_ref):
+        send_ref[:, h * 512 : (h + 1) * 512] = full[h, other, :]
+    part_ref[...] = low[own, :]
+    send_ref[:, 1024:1152], send_ref[:, 1152:1280] = split(low[other, :])
+
+
+def route_kernel(part_ref, keep_ref, both_ref, out_ref):
     core = lax.axis_index("core")
     total = part_ref[0] + part_ref[1] + part_ref[2] + part_ref[3]
     src, dst = iotas(RANK, RANK)
@@ -127,7 +131,7 @@
         out_ref[j, :, 512:640] = low
     for h in range(2):
         out_ref[core * 2 + h, :, 0:512] = keep_ref[h]
-        out_ref[(1 - core) * 2 + h, :, 0:512] = recv_ref[h]
+        out_ref[(1 - core) * 2 + h, :, 0:512] = both_ref[1 - core, :, h * 512 : (h + 1) * 512]
 
 
 def mix_kernel(piece_ref, k_ref, out_ref):
@@ -274,16 +278,21 @@
         out_ref[y, 256:272] = pair(grad[y * 8 : (y + 1) * 8])
 
 
+def free_lanes():
+    src, dst = iotas(16, LANES)
+    return one_hot(dst == HEAD + src)
+
+
 def y_sum_kernel(dk_ref, dq_ref, out_ref):
-    dk = total_of(dk_ref, slice(0, 256)).astype(BF)
     grad = total_of(dk_ref, slice(256, 272))
-    grad = pair(grad[0:8] + grad[8:16])
+    grad = dot_tn(pair(grad[0:8] + grad[8:16]), free_lanes()).astype(BF)
+    heads = lax.broadcasted_iota(jnp.int32, (256, LANES), 1) < HEAD
+    dk = jnp.where(heads, total_of(dk_ref, slice(0, 256)), 0.0).astype(BF)
+    dq = jnp.where(heads, dq_ref[...].astype(F32), 0.0).astype(BF)
     for z in range(4):
         rows = slice(z * HALF, (z + 1) * HALF)
-        out_ref[z, 0:HALF, 0:128] = dq_ref[rows]
-        out_ref[z, 0:HALF, 128:256] = dk[rows]
-        out_ref[z, HALF : HALF + 16, 0:128] = grad
-        out_ref[z, HALF : HALF + 16, 128:256] = jnp.zeros((16, 128), BF)
+        out_ref[z, :, 0:128] = dq[rows] + grad[0:HALF]
+        out_ref[z, :, 128:256] = dk[rows] + grad[HALF:TOK]
 
 
 def last_kernel(back_ref, master_ref, first_ref, second_ref,
@@ -291,16 +300,22 @@
     z_hi, core = lax.axis_index("zh"), lax.axis_index("core")
     for half in range(2):
         for h in range(2):
-            tile_ref[h, half * HALF : (half + 1) * HALF] = back_ref[half, core * 2 + h, 0:HALF, :]
+            tile_ref[h, half * HALF : (half + 1) * HALF] = back_ref[half, core * 2 + h]
     for out, lane in ((qg_ref, 0), (kg_ref, 128)):
         for h in range(2):
             out[h * HEAD : (h + 1) * HEAD, :] = tile_ref[h, :, lane : lane + LANES].T[0:HEAD]
     row8 = lax.broadcasted_iota(jnp.int32, (8, LANES), 0)
     columns = []
     for h in range(2):
-        rows = (
-            back_ref[0, core * 2 + h, HALF : HALF + 16, 0:128].astype(F32)
-            + back_ref[1, core * 2 + h, HALF : HALF + 16, 0:128].astype(F32)
+        rows = sum(
+            dot_nt(
+                free_lanes(),
+                jnp.concatenate(
+                    [back_ref[i, core * 2 + h, :, 0:128], back_ref[i, core * 2 + h, :, 128:256]],
+                    axis=0,
+                ),
+            )
+            for i in range(2)
         )
         rows = rows[0:8] + rows[8:16]
         columns.append(jnp.concatenate(
@@ -328,10 +343,6 @@
     return lax.all_to_all(value, axes, split_axis=0, concat_axis=0, tiled=True)
 
 
-def swap(value):
-    return lax.ppermute(value, "core", [(0, 1), (1, 0)])
-
-
 def copies(value, count):
     return jnp.broadcast_to(value[None], (count, *value.shape)).reshape(
         count * value.shape[0], *value.shape[1:]
@@ -343,19 +354,18 @@
 
 
 def body(normed, w_down, query, key, value_base, cotangent, master, first, second):
-    (part,) = call(low_kernel, [((TOK, RANK), F32)], (), (normed.T, w_down), limit=56)
-    (part,) = call(half_kernel, [((4, HALF, RANK), F32)], (both_cores(part),))
-    keep, send = call(
+    part, keep, send = call(
         pack_kernel,
-        [((2, HALF, 512), BF), ((2, HALF, 512), BF)],
+        [((HALF, RANK), F32), ((2, HALF, 512), BF), ((HALF, 1280), BF)],
         (),
-        (query.T, cotangent.T, key.T, value_base.T, master),
-        [pltpu.VMEM((2, TOK, 512), BF), pltpu.VMEM((16, 256), F32)],
+        (normed.T, w_down, query.T, cotangent.T, key.T, value_base.T, master),
+        [pltpu.VMEM((2, TOK, 512), BF), pltpu.VMEM((16, 256), F32), pltpu.VMEM((TOK, RANK), F32)],
         limit=56,
     )
+    both = both_cores(send)
+    (part,) = call(half_kernel, [((4, HALF, RANK), F32)], (part, both))
     part = exchange(part, "zl")
-    recv = swap(send)
-    (pieces,) = call(route_kernel, [((4, HALF, 640), BF)], (part, keep, recv))
+    (pieces,) = call(route_kernel, [((4, HALF, 640), BF)], (part, keep, both))
     pieces = exchange(pieces, "zh").reshape(256, 640)
     k_own = exchange(copies(pieces[:, 256:640], 4), "y")
     (q_tile,) = call(mix_kernel, [((4, 256, 256), BF)], (pieces, k_own))
@@ -387,7 +397,7 @@
         [((256, LANES), BF), ((4, 272, LANES), BF)],
         (exchange(dq, "x"), dk_keep, dk_recv),
     )
-    (back,) = call(y_sum_kernel, [((4, HALF + 16, 256), BF)], (exchange(dk, "y"), dq))
+    (back,) = call(y_sum_kernel, [((4, HALF, 256), BF)], (exchange(dk, "y"), dq))
     back = exchange(back, "zh")
     back = both_cores(back)
     q_grad, k_grad, new_master, new_first, new_second = call(

time: 137 us -> 137 us (level)
  blocking collectives: 106 us -> 113 us
  starting transfers between devices: 13 us -> 7.46 us
  Pallas kernels: 13.4 us -> 12 us
    all_to_all x5 -> x6, blocking collectives: 67.7 us -> 76.9 us  [exchange(): return lax.all_to_all(value, axes, split_axis=0, concat_axis=0, tiled=True)]
    all_to_all x3 -> x2, starting transfers between devices: 10.8 us -> 7.46 us  [exchange(): return lax.all_to_all(value, axes, split_axis=0, concat_axis=0, tiled=True)]
    ppermute x1 -> x0, starting transfers between devices: 2.26 us -> none  [swap(): return lax.ppermute(value, 'core', [(0, 1), (1, 0)])]
    all_gather x5, blocking collectives: 37.8 us -> 36 us  [both_cores(): return lax.all_gather(value, 'core', axis=0)]
    pallas_call x11 -> x10, Pallas kernels: 13.4 us -> 12 us  [call(): pl.pallas_call(kernel, out_shape=[(pltpu.VMEM if pinned else jax.ShapeDty...]
  transfers between devices with their start and end apart: 4 -> 2, of which waited for: 3 -> 1; matrix products, arithmetic and copies ran while one was open for 0% -> 0% of each run, Pallas kernels for 1% -> 0%
where the time goes in v7:
time: 137 us; the launch traced here: 134 us
  blocking collectives  113 us (82%)
  Pallas kernels  12 us (9%)
  starting transfers between devices  7.46 us (5%)
    all_to_all x6, blocking collectives, exchange(): return lax.all_to_all(value, axes, split_axis=0, concat_axis=0, tiled=True)  76.9 us
    all_gather x5, blocking collectives, both_cores(): return lax.all_gather(value, 'core', axis=0)  36 us
    pallas_call x10, Pallas kernels, call(): pl.pallas_call(kernel, out_shape=[(pltpu.VMEM if pinned else jax.ShapeDty...  12 us
    all_to_all x2, starting transfers between devices, exchange(): return lax.all_to_all(value, axes, split_axis=0, concat_axis=0, tiled=True)  7.46 us
  transfers between devices with their start and end apart: 2, of which 1 were waited for; matrix products, arithmetic and copies ran while one was open for 0% of the time, Pallas kernels for 0%

profile of v7, /device:TPU:1, one launch (start us, length us, event | category | flops | bytes accessed | tf_op | source)
XLA Modules:
  0.0 134.4 jit_solution(9919612394239260239)
XLA Ops:
  0.6 1.4 %shard_map.128 = (f32[64,128]{1,0:T(8,128)S(1)}, bf16[2,64,512]{2,1,0:T(8,128)(2,1)S(1)}, bf16[64,1280]{1,0:T(8,128)(2,1)S(1)}) custom-call(bf16[448,128]{1,0:T(8,128)(2,1)} %bitcast.32, bf16[448,128]{1,0:T(8,128)(2,1)} %wd_ref.1, bf16[224,128]{1,0:T(8,128)(2,1)} %bitcast.33, bf16[224,128]{1,0:T(8,128)(2,1)} %bitcast.34, bf16[224,128]{1,0:T(8,128)(2,1)} %bitcast.35, ...), custom_call_target="tpu_custom_call" | custom-call | tf_op jit(solution)/shard_map/pallas_call | solution.py:40
  2.0 8.6 %all-gather = bf16[128,1280]{1,0:T(8,128)(2,1)S(1)} all-gather(bf16[64,1280]{1,0:T(8,128)(2,1)S(1)} %get-tuple-element.24), channel_id=2, replica_groups=mesh['y'=4,'zh'=4,'x'=4,'zl'=4,'core'=2] {'core'}, dimensions={0}, use_global_device_ids=true | all-gather | bytes 491520 | tf_op jit(solution)/shard_map/all_gather | solution.py:353
  10.6 7.3 %all_to_all.43.part_ref = f32[4,64,128]{2,1,0:T(8,128)S(1)} all-to-all(f32[4,64,128]{2,1,0:T(8,128)S(1)} %shard_map.129), channel_id=1, replica_groups=mesh['y'=4,'zh'=4,'x'=4,'zl'=4,'core'=2] {'zl'}, dimensions={0} | all-to-all | bytes 262144 | tf_op jit(solution)/shard_map/all_to_all | solution.py:343
  17.8 0.1 shard_map.130
  18.0 23.9 %all_to_all.44 = bf16[4,64,640]{2,1,0:T(8,128)(2,1)S(1)} all-to-all(bf16[4,64,640]{2,1,0:T(8,128)(2,1)S(1)} %shard_map.130), channel_id=1, replica_groups=mesh['y'=4,'zh'=4,'x'=4,'zl'=4,'core'=2] {'zh'}, dimensions={0} | all-to-all | bytes 655360 | tf_op jit(solution)/shard_map/all_to_all | solution.py:343
  42.0 0.1 broadcast_in_dim.2
  42.0 12.3 %all_to_all.45 = bf16[4,256,384]{2,1,0:T(8,128)(2,1)S(1)} all-to-all(bf16[4,256,384]{2,1,0:T(8,128)(2,1)S(1)} %broadcast_in_dim.2), channel_id=1, replica_groups=mesh['y'=4,'zh'=4,'x'=4,'zl'=4,'core'=2] {'y'}, dimensions={0} | all-to-all | bytes 1572864 | tf_op jit(solution)/shard_map/all_to_all | solution.py:343
  54.4 0.9 shard_map.131
  55.3 4.0 %all-to-all-start.3 = ((bf16[4,256,256]{2,1,0:T(8,128)(2,1)}), bf16[4,256,256]{2,1,0:T(8,128)(2,1)S(1)}, u32[]{:S(2)}, u32[]{:S(2)}) async-start(bf16[4,256,256]{2,1,0:T(8,128)(2,1)} %shard_map.131), calls=%async_computation.3 | async-start | bytes 1048576 | tf_op jit(solution)/shard_map/all_to_all | solution.py:343
  59.3 0.1 fusion
  59.4 12.2 %all_gather.33 = bf16[2,512,384]{2,1,0:T(8,128)(2,1)S(1)} all-gather(bf16[1,512,384]{2,1,0:T(8,128)(2,1)S(1)} %bitcast.31), channel_id=1, replica_groups=mesh['y'=4,'zh'=4,'x'=4,'zl'=4,'core'=2] {'core'}, dimensions={0}, use_global_device_ids=true | all-gather | bytes 1179648 | tf_op jit(solution)/shard_map/all_gather | solution.py:353
  71.6 2.4 %all_gather.35 = bf16[2,512,384]{2,1,0:T(8,128)(2,1)S(1)} all-gather(bf16[1,512,384]{2,1,0:T(8,128)(2,1)S(1)} %bitcast.30), channel_id=1, replica_groups=mesh['y'=4,'zh'=4,'x'=4,'zl'=4,'core'=2] {'core'}, dimensions={0}, use_global_device_ids=true | all-gather | bytes 1179648 | tf_op jit(solution)/shard_map/all_gather | solution.py:353
  74.0 0.0 all-to-all-done.3
  74.0 4.4 %shard_map.132 = (f32[4,2,1024]{2,1,0:T(2,128)S(1)}, f32[1,1024]{1,0:T(1,128)S(1)}, f32[2048,1024]{1,0:T(8,128)S(1)}, f32[2048,1024]{1,0:T(8,128)S(1)}) custom-call(bf16[1024,256]{1,0:T(8,128)(2,1)S(1)} %bitcast.22, bf16[1024,384]{1,0:T(8,128)(2,1)S(1)} %bitcast.18, bf16[1024,384]{1,0:T(8,128)(2,1)S(1)} %bitcast.20), custom_call_target="tpu_custom_call" | custom-call | tf_op jit(solution)/shard_map/pallas_call | solution.py:40
  78.4 8.6 %all_to_all.46.stat_ref = f32[4,2,1024]{2,1,0:T(2,128)S(1)} all-to-all(f32[4,2,1024]{2,1,0:T(2,128)S(1)} %get-tuple-element.29), channel_id=1, replica_groups=mesh['y'=4,'zh'=4,'x'=4,'zl'=4,'core'=2] {'x'}, dimensions={0} | all-to-all | bytes 65536 | tf_op jit(solution)/shard_map/all_to_all | solution.py:343
  87.0 0.0 copy-start
  87.0 0.0 copy-start.1
  87.0 0.0 copy-start.2
  87.0 3.8 %shard_map.133 = (bf16[4,320,128]{2,1,0:T(8,128)(2,1)}, f32[2048,128]{1,0:T(8,128)S(1)}) custom-call(bf16[1024,256]{1,0:T(8,128)(2,1)S(1)} %bitcast.23, bf16[1024,384]{1,0:T(8,128)(2,1)S(1)} %bitcast.19, bf16[1024,384]{1,0:T(8,128)(2,1)S(1)} %bitcast.21, f32[2048,1024]{1,0:T(8,128)S(1)} %get-tuple-element.26.w_ref, ...), custom_call_target="tpu_custom_call" | custom-call | tf_op jit(solution)/shard_map/pallas_call | solution.py:40
  90.9 3.5 %all-to-all-start.5 = ((bf16[4,320,128]{2,1,0:T(8,128)(2,1)}), bf16[4,320,128]{2,1,0:T(8,128)(2,1)S(1)}, u32[]{:S(2)}, u32[]{:S(2)}) async-start(bf16[4,320,128]{2,1,0:T(8,128)(2,1)} %get-tuple-element.30), calls=%async_computation.5 | async-start | bytes 655360 | tf_op jit(solution)/shard_map/all_to_all | solution.py:343
  94.3 0.1 shard_map.134
  94.4 4.6 %all-gather.1 = bf16[2048,128]{1,0:T(8,128)(2,1)S(1)} all-gather(bf16[1024,128]{1,0:T(8,128)(2,1)S(1)} %get-tuple-element.33), channel_id=3, replica_groups=mesh['y'=4,'zh'=4,'x'=4,'zl'=4,'core'=2] {'core'}, dimensions={0}, use_global_device_ids=true | all-gather | bytes 786432 | tf_op jit(solution)/shard_map/all_gather | solution.py:353
  99.1 1.1 all-to-all-done.5.dq_ref
  100.2 0.1 shard_map.135
  100.3 8.0 %all_to_all.47.dk_ref = bf16[4,272,128]{2,1,0:T(8,128)(2,1)S(1)} all-to-all(bf16[4,272,128]{2,1,0:T(8,128)(2,1)S(1)} %get-tuple-element.34), channel_id=1, replica_groups=mesh['y'=4,'zh'=4,'x'=4,'zl'=4,'core'=2] {'y'}, dimensions={0} | all-to-all | bytes 557056 | tf_op jit(solution)/shard_map/all_to_all | solution.py:343
  108.2 0.2 shard_map.136
  108.5 16.8 %all_to_all.48 = bf16[4,64,256]{2,1,0:T(8,128)(2,1)S(1)} all-to-all(bf16[4,64,256]{2,1,0:T(8,128)(2,1)S(1)} %shard_map.136), channel_id=1, replica_groups=mesh['y'=4,'zh'=4,'x'=4,'zl'=4,'core'=2] {'zh'}, dimensions={0} | all-to-all | bytes 262144 | tf_op jit(solution)/shard_map/all_to_all | solution.py:343
  125.2 8.2 %all-gather.2 = bf16[8,64,256]{2,1,0:T(8,128)(2,1)S(1)} all-gather(bf16[4,64,256]{2,1,0:T(8,128)(2,1)S(1)} %all_to_all.48), channel_id=4, replica_groups=mesh['y'=4,'zh'=4,'x'=4,'zl'=4,'core'=2] {'core'}, dimensions={0}, use_global_device_ids=true | all-gather | bytes 393216 | tf_op jit(solution)/shard_map/all_gather | solution.py:353
  133.5 0.0 copy-done
  133.5 0.0 copy-done.1
  133.5 0.0 copy-done.2
  133.5 0.9 shard_map.137
  (2 shorter events, 0.0 us)
Async XLA Ops:
  55.3 18.7 %all-to-all-start.3 = ((bf16[4,256,256]{2,1,0:T(8,128)(2,1)}), bf16[4,256,256]{2,1,0:T(8,128)(2,1)S(1)}, u32[]{:S(2)}, u32[]{:S(2)}) async-start(bf16[4,256,256]{2,1,0:T(8,128)(2,1)} %shard_map.131), calls=%async_computation.3 | async-start | bytes 1048576 | tf_op jit(solution)/shard_map/all_to_all | solution.py:343
  87.0 46.4 %copy-start = (f32[2,224]{1,0:T(2,128)S(1)}, f32[2,224]{1,0:T(2,128)}, u32[]{:S(2)}) copy-start(f32[2,224]{1,0:T(2,128)} %master_ref.1) | copy-start | bytes 5380
  87.0 46.4 %copy-start.1 = (f32[2,224]{1,0:T(2,128)S(1)}, f32[2,224]{1,0:T(2,128)}, u32[]{:S(2)}) copy-start(f32[2,224]{1,0:T(2,128)} %first_ref.1) | copy-start | bytes 5380
  87.0 46.4 %copy-start.2 = (f32[2,224]{1,0:T(2,128)S(1)}, f32[2,224]{1,0:T(2,128)}, u32[]{:S(2)}) copy-start(f32[2,224]{1,0:T(2,128)} %second_ref.1) | copy-start | bytes 5380
  90.9 9.3 %all-to-all-start.5 = ((bf16[4,320,128]{2,1,0:T(8,128)(2,1)}), bf16[4,320,128]{2,1,0:T(8,128)(2,1)S(1)}, u32[]{:S(2)}, u32[]{:S(2)}) async-start(bf16[4,320,128]{2,1,0:T(8,128)(2,1)} %get-tuple-element.30), calls=%async_computation.5 | async-start | bytes 655360 | tf_op jit(solution)/shard_map/all_to_all | solution.py:343

commit v8 on v7

--- a/solution.py
+++ b/solution.py
@@ -216,6 +216,11 @@
         stat_ref[i, 1:2] = delta / safe
 
 
+def free_lanes():
+    src, dst = iotas(16, LANES)
+    return one_hot(dst == HEAD + src)
+
+
 def second_kernel(q_ref, low_ref, high_ref, w_ref, d_ref, top_ref, stat_ref,
                   dq_ref, dk_ref, dv_ref, dq_acc):
     lse = [stat_ref[i, 0:1, :] for i in range(4)]
@@ -242,9 +247,13 @@
     low = jnp.concatenate([low_ref[:, 256:384], high_ref[:, 256:384]], axis=0)
     high, rest = split(dot_tn(low, dv_ref[...]) * INV_RANK)
     for i in range(4):
-        dq_ref[i, 0:256] = d_query[i * 256 : (i + 1) * 256]
-        dq_ref[i, 256:288] = high[i * 32 : (i + 1) * 32]
-        dq_ref[i, 288:320] = rest[i * 32 : (i + 1) * 32]
+        for j in range(2):
+            start = i * 256 + j * TOK
+            part = high[i * 32 + j * 16 : i * 32 + (j + 1) * 16]
+            dq_ref[i, j * TOK : (j + 1) * TOK] = (
+                d_query[start : start + TOK] + dot_tn(part, free_lanes()).astype(BF)
+            )
+        dq_ref[i, 256:288] = rest[i * 32 : (i + 1) * 32]
 
 
 def scale_kernel(dk_ref, keep_ref, send_ref):
@@ -270,24 +279,27 @@
 
 def x_sum_kernel(dq_ref, keep_ref, recv_ref, dq_out, out_ref):
     other = 1 - lax.axis_index("core")
-    dq_out[...] = total_of(dq_ref, slice(0, 256)).astype(BF)
-    grad = total_of(dq_ref, slice(256, 288)) + total_of(dq_ref, slice(288, 320))
+    dq = total_of(dq_ref, slice(0, 256))
+    dq_out[...] = dq.astype(BF)
+    grad = total_of(dq_ref, slice(256, 288)) + jnp.concatenate(
+        [dq[0:TOK].T[HEAD:LANES], dq[TOK:256].T[HEAD:LANES]], axis=0
+    )
+    heads = lax.broadcasted_iota(jnp.int32, (256, LANES), 1) < HEAD
     for y in range(4):
         at = slice(y * 256, (y + 1) * 256)
-        out_ref[y, 0:256] = (keep_ref[at] + recv_ref[other, at].astype(F32)).astype(BF)
-        out_ref[y, 256:272] = pair(grad[y * 8 : (y + 1) * 8])
-
-
-def free_lanes():
-    src, dst = iotas(16, LANES)
-    return one_hot(dst == HEAD + src)
+        dk = keep_ref[at] + recv_ref[other, at].astype(F32)
+        dk = jnp.where(heads, dk, 0.0).astype(BF)
+        placed = dot_tn(pair(grad[y * 8 : (y + 1) * 8]), free_lanes()).astype(BF)
+        out_ref[y, 0:TOK] = dk[0:TOK] + placed
+        out_ref[y, TOK:256] = dk[TOK:256]
 
 
 def y_sum_kernel(dk_ref, dq_ref, out_ref):
-    grad = total_of(dk_ref, slice(256, 272))
+    dk = total_of(dk_ref, slice(0, 256))
+    grad = dk[0:TOK].T[HEAD:LANES]
     grad = dot_tn(pair(grad[0:8] + grad[8:16]), free_lanes()).astype(BF)
     heads = lax.broadcasted_iota(jnp.int32, (256, LANES), 1) < HEAD
-    dk = jnp.where(heads, total_of(dk_ref, slice(0, 256)), 0.0).astype(BF)
+    dk = jnp.where(heads, dk, 0.0).astype(BF)
     dq = jnp.where(heads, dq_ref[...].astype(F32), 0.0).astype(BF)
     for z in range(4):
         rows = slice(z * HALF, (z + 1) * HALF)
@@ -383,7 +395,7 @@
     stats = exchange(stat, "x")
     dq, dk = call(
         second_kernel,
-        [((4, 320, LANES), BF), ((N_K, LANES), F32)],
+        [((4, 288, LANES), BF), ((N_K, LANES), F32)],
         (q_tile, k_low, k_high, weight, d_prob, top, stats),
         scratch=[pltpu.VMEM((N_K, LANES), BF), pltpu.VMEM((LANES, N_Q), F32)],
         limit=16,
@@ -394,7 +406,7 @@
     dk_recv = both_cores(dk_send)
     dq, dk = call(
         x_sum_kernel,
-        [((256, LANES), BF), ((4, 272, LANES), BF)],
+        [((256, LANES), BF), ((4, 256, LANES), BF)],
         (exchange(dq, "x"), dk_keep, dk_recv),
     )
     (back,) = call(y_sum_kernel, [((4, HALF, 256), BF)], (exchange(dk, "y"), dq))

time: 137 us -> 137 us (level)
  no operation moved by 1% of the time
where the time goes in v8:
time: 137 us; the launch traced here: 135 us
  blocking collectives  113 us (82%)
  Pallas kernels  12.6 us (9%)
  starting transfers between devices  7.46 us (5%)
    all_to_all x6, blocking collectives, exchange(): return lax.all_to_all(value, axes, split_axis=0, concat_axis=0, tiled=True)  76.8 us
    all_gather x5, blocking collectives, both_cores(): return lax.all_gather(value, 'core', axis=0)  36 us
    pallas_call x10, Pallas kernels, call(): pl.pallas_call(kernel, out_shape=[(pltpu.VMEM if pinned else jax.ShapeDty...  12.6 us
    all_to_all x2, starting transfers between devices, exchange(): return lax.all_to_all(value, axes, split_axis=0, concat_axis=0, tiled=True)  7.46 us
  transfers between devices with their start and end apart: 2, of which 1 were waited for; matrix products, arithmetic and copies ran while one was open for 0% of the time, Pallas kernels for 0%

profile of v8, /device:TPU:1, one launch (start us, length us, event | category | flops | bytes accessed | tf_op | source)
XLA Modules:
  0.0 134.7 jit_solution(7985303106194341436)
XLA Ops:
  0.6 1.4 %shard_map.128 = (f32[64,128]{1,0:T(8,128)S(1)}, bf16[2,64,512]{2,1,0:T(8,128)(2,1)S(1)}, bf16[64,1280]{1,0:T(8,128)(2,1)S(1)}) custom-call(bf16[448,128]{1,0:T(8,128)(2,1)} %bitcast.32, bf16[448,128]{1,0:T(8,128)(2,1)} %wd_ref.1, bf16[224,128]{1,0:T(8,128)(2,1)} %bitcast.33, bf16[224,128]{1,0:T(8,128)(2,1)} %bitcast.34, bf16[224,128]{1,0:T(8,128)(2,1)} %bitcast.35, ...), custom_call_target="tpu_custom_call" | custom-call | tf_op jit(solution)/shard_map/pallas_call | solution.py:40
  2.0 8.6 %all-gather = bf16[128,1280]{1,0:T(8,128)(2,1)S(1)} all-gather(bf16[64,1280]{1,0:T(8,128)(2,1)S(1)} %get-tuple-element.24), channel_id=2, replica_groups=mesh['y'=4,'zh'=4,'x'=4,'zl'=4,'core'=2] {'core'}, dimensions={0}, use_global_device_ids=true | all-gather | bytes 491520 | tf_op jit(solution)/shard_map/all_gather | solution.py:365
  10.6 7.3 %all_to_all.43.part_ref = f32[4,64,128]{2,1,0:T(8,128)S(1)} all-to-all(f32[4,64,128]{2,1,0:T(8,128)S(1)} %shard_map.129), channel_id=1, replica_groups=mesh['y'=4,'zh'=4,'x'=4,'zl'=4,'core'=2] {'zl'}, dimensions={0} | all-to-all | bytes 262144 | tf_op jit(solution)/shard_map/all_to_all | solution.py:355
  17.8 0.1 shard_map.130
  18.0 23.9 %all_to_all.44 = bf16[4,64,640]{2,1,0:T(8,128)(2,1)S(1)} all-to-all(bf16[4,64,640]{2,1,0:T(8,128)(2,1)S(1)} %shard_map.130), channel_id=1, replica_groups=mesh['y'=4,'zh'=4,'x'=4,'zl'=4,'core'=2] {'zh'}, dimensions={0} | all-to-all | bytes 655360 | tf_op jit(solution)/shard_map/all_to_all | solution.py:355
  42.0 0.1 broadcast_in_dim.2
  42.0 12.3 %all_to_all.45 = bf16[4,256,384]{2,1,0:T(8,128)(2,1)S(1)} all-to-all(bf16[4,256,384]{2,1,0:T(8,128)(2,1)S(1)} %broadcast_in_dim.2), channel_id=1, replica_groups=mesh['y'=4,'zh'=4,'x'=4,'zl'=4,'core'=2] {'y'}, dimensions={0} | all-to-all | bytes 1572864 | tf_op jit(solution)/shard_map/all_to_all | solution.py:355
  54.4 0.9 shard_map.131
  55.3 4.0 %all-to-all-start.3 = ((bf16[4,256,256]{2,1,0:T(8,128)(2,1)}), bf16[4,256,256]{2,1,0:T(8,128)(2,1)S(1)}, u32[]{:S(2)}, u32[]{:S(2)}) async-start(bf16[4,256,256]{2,1,0:T(8,128)(2,1)} %shard_map.131), calls=%async_computation.3 | async-start | bytes 1048576 | tf_op jit(solution)/shard_map/all_to_all | solution.py:355
  59.3 0.1 fusion
  59.4 12.2 %all_gather.33 = bf16[2,512,384]{2,1,0:T(8,128)(2,1)S(1)} all-gather(bf16[1,512,384]{2,1,0:T(8,128)(2,1)S(1)} %bitcast.31), channel_id=1, replica_groups=mesh['y'=4,'zh'=4,'x'=4,'zl'=4,'core'=2] {'core'}, dimensions={0}, use_global_device_ids=true | all-gather | bytes 1179648 | tf_op jit(solution)/shard_map/all_gather | solution.py:365
  71.6 2.4 %all_gather.35 = bf16[2,512,384]{2,1,0:T(8,128)(2,1)S(1)} all-gather(bf16[1,512,384]{2,1,0:T(8,128)(2,1)S(1)} %bitcast.30), channel_id=1, replica_groups=mesh['y'=4,'zh'=4,'x'=4,'zl'=4,'core'=2] {'core'}, dimensions={0}, use_global_device_ids=true | all-gather | bytes 1179648 | tf_op jit(solution)/shard_map/all_gather | solution.py:365
  74.0 0.0 all-to-all-done.3
  74.0 4.4 %shard_map.132 = (f32[4,2,1024]{2,1,0:T(2,128)S(1)}, f32[1,1024]{1,0:T(1,128)S(1)}, f32[2048,1024]{1,0:T(8,128)S(1)}, f32[2048,1024]{1,0:T(8,128)S(1)}) custom-call(bf16[1024,256]{1,0:T(8,128)(2,1)S(1)} %bitcast.22, bf16[1024,384]{1,0:T(8,128)(2,1)S(1)} %bitcast.18, bf16[1024,384]{1,0:T(8,128)(2,1)S(1)} %bitcast.20), custom_call_target="tpu_custom_call" | custom-call | tf_op jit(solution)/shard_map/pallas_call | solution.py:40
  78.4 8.6 %all_to_all.46.stat_ref = f32[4,2,1024]{2,1,0:T(2,128)S(1)} all-to-all(f32[4,2,1024]{2,1,0:T(2,128)S(1)} %get-tuple-element.29), channel_id=1, replica_groups=mesh['y'=4,'zh'=4,'x'=4,'zl'=4,'core'=2] {'x'}, dimensions={0} | all-to-all | bytes 65536 | tf_op jit(solution)/shard_map/all_to_all | solution.py:355
  87.0 0.0 copy-start
  87.0 0.0 copy-start.1
  87.0 0.0 copy-start.2
  87.0 4.1 %shard_map.133 = (bf16[4,288,128]{2,1,0:T(8,128)(2,1)}, f32[2048,128]{1,0:T(8,128)S(1)}) custom-call(bf16[1024,256]{1,0:T(8,128)(2,1)S(1)} %bitcast.23, bf16[1024,384]{1,0:T(8,128)(2,1)S(1)} %bitcast.19, bf16[1024,384]{1,0:T(8,128)(2,1)S(1)} %bitcast.21, f32[2048,1024]{1,0:T(8,128)S(1)} %get-tuple-element.26.w_ref, ...), custom_call_target="tpu_custom_call" | custom-call | tf_op jit(solution)/shard_map/pallas_call | solution.py:40
  91.1 3.5 %all-to-all-start.5 = ((bf16[4,288,128]{2,1,0:T(8,128)(2,1)}), bf16[4,288,128]{2,1,0:T(8,128)(2,1)S(1)}, u32[]{:S(2)}, u32[]{:S(2)}) async-start(bf16[4,288,128]{2,1,0:T(8,128)(2,1)} %get-tuple-element.30), calls=%async_computation.5 | async-start | bytes 589824 | tf_op jit(solution)/shard_map/all_to_all | solution.py:355
  94.6 0.1 shard_map.134
  94.7 4.6 %all-gather.1 = bf16[2048,128]{1,0:T(8,128)(2,1)S(1)} all-gather(bf16[1024,128]{1,0:T(8,128)(2,1)S(1)} %get-tuple-element.33), channel_id=3, replica_groups=mesh['y'=4,'zh'=4,'x'=4,'zl'=4,'core'=2] {'core'}, dimensions={0}, use_global_device_ids=true | all-gather | bytes 786432 | tf_op jit(solution)/shard_map/all_gather | solution.py:365
  99.3 0.9 all-to-all-done.5.dq_ref
  100.3 0.3 shard_map.135
  100.6 7.9 %all_to_all.47.dk_ref = bf16[4,256,128]{2,1,0:T(8,128)(2,1)S(1)} all-to-all(bf16[4,256,128]{2,1,0:T(8,128)(2,1)S(1)} %get-tuple-element.34), channel_id=1, replica_groups=mesh['y'=4,'zh'=4,'x'=4,'zl'=4,'core'=2] {'y'}, dimensions={0} | all-to-all | bytes 524288 | tf_op jit(solution)/shard_map/all_to_all | solution.py:355
  108.5 0.3 shard_map.136
  108.8 16.8 %all_to_all.48 = bf16[4,64,256]{2,1,0:T(8,128)(2,1)S(1)} all-to-all(bf16[4,64,256]{2,1,0:T(8,128)(2,1)S(1)} %shard_map.136), channel_id=1, replica_groups=mesh['y'=4,'zh'=4,'x'=4,'zl'=4,'core'=2] {'zh'}, dimensions={0} | all-to-all | bytes 262144 | tf_op jit(solution)/shard_map/all_to_all | solution.py:355
  125.6 8.2 %all-gather.2 = bf16[8,64,256]{2,1,0:T(8,128)(2,1)S(1)} all-gather(bf16[4,64,256]{2,1,0:T(8,128)(2,1)S(1)} %all_to_all.48), channel_id=4, replica_groups=mesh['y'=4,'zh'=4,'x'=4,'zl'=4,'core'=2] {'core'}, dimensions={0}, use_global_device_ids=true | all-gather | bytes 393216 | tf_op jit(solution)/shard_map/all_gather | solution.py:365
  133.8 0.0 copy-done
  133.8 0.0 copy-done.1
  133.8 0.0 copy-done.2
  133.8 0.9 shard_map.137
  (2 shorter events, 0.0 us)
Async XLA Ops:
  55.3 18.7 %all-to-all-start.3 = ((bf16[4,256,256]{2,1,0:T(8,128)(2,1)}), bf16[4,256,256]{2,1,0:T(8,128)(2,1)S(1)}, u32[]{:S(2)}, u32[]{:S(2)}) async-start(bf16[4,256,256]{2,1,0:T(8,128)(2,1)} %shard_map.131), calls=%async_computation.3 | async-start | bytes 1048576 | tf_op jit(solution)/shard_map/all_to_all | solution.py:355
  87.0 46.8 %copy-start = (f32[2,224]{1,0:T(2,128)S(1)}, f32[2,224]{1,0:T(2,128)}, u32[]{:S(2)}) copy-start(f32[2,224]{1,0:T(2,128)} %master_ref.1) | copy-start | bytes 5380
  87.0 46.8 %copy-start.1 = (f32[2,224]{1,0:T(2,128)S(1)}, f32[2,224]{1,0:T(2,128)}, u32[]{:S(2)}) copy-start(f32[2,224]{1,0:T(2,128)} %first_ref.1) | copy-start | bytes 5380
  87.0 46.8 %copy-start.2 = (f32[2,224]{1,0:T(2,128)S(1)}, f32[2,224]{1,0:T(2,128)}, u32[]{:S(2)}) copy-start(f32[2,224]{1,0:T(2,128)} %second_ref.1) | copy-start | bytes 5380
  91.1 9.1 %all-to-all-start.5 = ((bf16[4,288,128]{2,1,0:T(8,128)(2,1)}), bf16[4,288,128]{2,1,0:T(8,128)(2,1)S(1)}, u32[]{:S(2)}, u32[]{:S(2)}) async-start(bf16[4,288,128]{2,1,0:T(8,128)(2,1)} %get-tuple-element.30), calls=%async_computation.5 | async-start | bytes 589824 | tf_op jit(solution)/shard_map/all_to_all | solution.py:355

commit v9 on v8

--- a/solution.py
+++ b/solution.py
@@ -355,12 +355,6 @@
     return lax.all_to_all(value, axes, split_axis=0, concat_axis=0, tiled=True)
 
 
-def copies(value, count):
-    return jnp.broadcast_to(value[None], (count, *value.shape)).reshape(
-        count * value.shape[0], *value.shape[1:]
-    )
-
-
 def both_cores(value):
     return lax.all_gather(value, "core", axis=0)
 
@@ -379,7 +373,7 @@
     part = exchange(part, "zl")
     (pieces,) = call(route_kernel, [((4, HALF, 640), BF)], (part, keep, both))
     pieces = exchange(pieces, "zh").reshape(256, 640)
-    k_own = exchange(copies(pieces[:, 256:640], 4), "y")
+    k_own = lax.all_gather(pieces[:, 256:640], "y", axis=0, tiled=True)
     (q_tile,) = call(mix_kernel, [((4, 256, 256), BF)], (pieces, k_own))
     k_low = both_cores(k_own[0:512]).reshape(1024, 384)
     k_high = both_cores(k_own[512:1024]).reshape(1024, 384)

time: 137 us -> 137 us (level); the launches traced: 135 us -> 136 us
    all_gather x0 -> x1, blocking collectives: none -> 11.5 us  [body(): k_own = lax.all_gather(pieces[:, 256:640], 'y', axis=0, tiled=True)]
    all_to_all x6 -> x5, blocking collectives: 76.8 us -> 66.3 us  [exchange(): return lax.all_to_all(value, axes, split_axis=0, concat_axis=0, tiled=True)]
where the time goes in v9:
time: 137 us; the launch traced here: 136 us
  blocking collectives  114 us (83%)
  Pallas kernels  12.6 us (9%)
  starting transfers between devices  7.47 us (5%)
    all_to_all x5, blocking collectives, exchange(): return lax.all_to_all(value, axes, split_axis=0, concat_axis=0, tiled=True)  66.3 us
    all_gather x5, blocking collectives, both_cores(): return lax.all_gather(value, 'core', axis=0)  36.6 us
    pallas_call x10, Pallas kernels, call(): pl.pallas_call(kernel, out_shape=[(pltpu.VMEM if pinned else jax.ShapeDty...  12.6 us
    all_gather x1, blocking collectives, body(): k_own = lax.all_gather(pieces[:, 256:640], 'y', axis=0, tiled=True)  11.5 us
    all_to_all x2, starting transfers between devices, exchange(): return lax.all_to_all(value, axes, split_axis=0, concat_axis=0, tiled=True)  7.47 us
  transfers between devices with their start and end apart: 2, of which 1 were waited for; matrix products, arithmetic and copies ran while one was open for 0% of the time, Pallas kernels for 0%

profile of v9, /device:TPU:1, one launch (start us, length us, event | category | flops | bytes accessed | tf_op | source)
XLA Modules:
  0.0 136.2 jit_solution(3159383376003531275)
XLA Ops:
  0.6 1.4 %shard_map.128 = (f32[64,128]{1,0:T(8,128)S(1)}, bf16[2,64,512]{2,1,0:T(8,128)(2,1)S(1)}, bf16[64,1280]{1,0:T(8,128)(2,1)S(1)}) custom-call(bf16[448,128]{1,0:T(8,128)(2,1)} %bitcast.20, bf16[448,128]{1,0:T(8,128)(2,1)} %wd_ref.1, bf16[224,128]{1,0:T(8,128)(2,1)} %bitcast.21, bf16[224,128]{1,0:T(8,128)(2,1)} %bitcast.22, bf16[224,128]{1,0:T(8,128)(2,1)} %bitcast.23, ...), custom_call_target="tpu_custom_call" | custom-call | tf_op jit(solution)/shard_map/pallas_call | solution.py:40
  2.0 8.6 %all-gather = bf16[128,1280]{1,0:T(8,128)(2,1)S(1)} all-gather(bf16[64,1280]{1,0:T(8,128)(2,1)S(1)} %get-tuple-element.24), channel_id=2, replica_groups=mesh['y'=4,'zh'=4,'x'=4,'zl'=4,'core'=2] {'core'}, dimensions={0}, use_global_device_ids=true | all-gather | bytes 491520 | tf_op jit(solution)/shard_map/all_gather | solution.py:359
  10.6 7.3 %all_to_all.35.part_ref = f32[4,64,128]{2,1,0:T(8,128)S(1)} all-to-all(f32[4,64,128]{2,1,0:T(8,128)S(1)} %shard_map.129), channel_id=1, replica_groups=mesh['y'=4,'zh'=4,'x'=4,'zl'=4,'core'=2] {'zl'}, dimensions={0} | all-to-all | bytes 262144 | tf_op jit(solution)/shard_map/all_to_all | solution.py:355
  17.8 0.1 shard_map.130
  18.0 23.9 %all_to_all.36 = bf16[4,64,640]{2,1,0:T(8,128)(2,1)S(1)} all-to-all(bf16[4,64,640]{2,1,0:T(8,128)(2,1)S(1)} %shard_map.130), channel_id=1, replica_groups=mesh['y'=4,'zh'=4,'x'=4,'zl'=4,'core'=2] {'zh'}, dimensions={0} | all-to-all | bytes 655360 | tf_op jit(solution)/shard_map/all_to_all | solution.py:355
  42.0 11.5 %all_gather.35.k_ref = bf16[1024,384]{1,0:T(8,128)(2,1)S(1)} all-gather(bf16[256,384]{1,0:T(8,128)(2,1)S(1)} %slice.12), channel_id=1, replica_groups=mesh['y'=4,'zh'=4,'x'=4,'zl'=4,'core'=2] {'y'}, dimensions={0}, use_global_device_ids=true | all-gather | bytes 983040 | tf_op jit(solution)/shard_map/all_gather | solution.py:376
  53.5 0.9 shard_map.131
  54.4 0.1 fusion
  54.5 4.0 %all-to-all-start.2 = ((bf16[4,256,256]{2,1,0:T(8,128)(2,1)}), bf16[4,256,256]{2,1,0:T(8,128)(2,1)S(1)}, u32[]{:S(2)}, u32[]{:S(2)}) async-start(bf16[4,256,256]{2,1,0:T(8,128)(2,1)} %shard_map.131), calls=%async_computation.2 | async-start | bytes 1048576 | tf_op jit(solution)/shard_map/all_to_all | solution.py:355
  58.5 13.1 %all-gather.2.high_ref = bf16[1024,384]{1,0:T(8,128)(2,1)S(1)} all-gather(bf16[512,384]{1,0:T(8,128)(2,1)S(1)} %get-tuple-element.41), channel_id=4, replica_groups=mesh['y'=4,'zh'=4,'x'=4,'zl'=4,'core'=2] {'core'}, dimensions={0}, use_global_device_ids=true | all-gather | bytes 1179648 | tf_op jit(solution)/shard_map/all_gather | solution.py:359
  71.6 2.4 %all-gather.1.low_ref = bf16[1024,384]{1,0:T(8,128)(2,1)S(1)} all-gather(bf16[512,384]{1,0:T(8,128)(2,1)S(1)} %get-tuple-element.42), channel_id=3, replica_groups=mesh['y'=4,'zh'=4,'x'=4,'zl'=4,'core'=2] {'core'}, dimensions={0}, use_global_device_ids=true | all-gather | bytes 1179648 | tf_op jit(solution)/shard_map/all_gather | solution.py:359
  74.0 0.0 all-to-all-done.2
  74.0 4.4 %shard_map.132 = (f32[4,2,1024]{2,1,0:T(2,128)S(1)}, f32[1,1024]{1,0:T(1,128)S(1)}, f32[2048,1024]{1,0:T(8,128)S(1)}, f32[2048,1024]{1,0:T(8,128)S(1)}) custom-call(bf16[1024,256]{1,0:T(8,128)(2,1)S(1)} %bitcast.12, bf16[1024,384]{1,0:T(8,128)(2,1)S(1)} %all-gather.1.low_ref, bf16[1024,384]{1,0:T(8,128)(2,1)S(1)} %all-gather.2.high_ref), custom_call_target="tpu_custom_call" | custom-call | tf_op jit(solution)/shard_map/pallas_call | solution.py:40
  78.4 8.6 %all_to_all.37.stat_ref = f32[4,2,1024]{2,1,0:T(2,128)S(1)} all-to-all(f32[4,2,1024]{2,1,0:T(2,128)S(1)} %get-tuple-element.29), channel_id=1, replica_groups=mesh['y'=4,'zh'=4,'x'=4,'zl'=4,'core'=2] {'x'}, dimensions={0} | all-to-all | bytes 65536 | tf_op jit(solution)/shard_map/all_to_all | solution.py:355
  87.0 0.0 copy-start
  87.0 0.0 copy-start.1
  87.0 0.0 copy-start.2
  87.0 4.1 %shard_map.133 = (bf16[4,288,128]{2,1,0:T(8,128)(2,1)}, f32[2048,128]{1,0:T(8,128)S(1)}) custom-call(bf16[1024,256]{1,0:T(8,128)(2,1)S(1)} %bitcast.13, bf16[1024,384]{1,0:T(8,128)(2,1)S(1)} %all-gather.1.low_ref, bf16[1024,384]{1,0:T(8,128)(2,1)S(1)} %all-gather.2.high_ref, f32[2048,1024]{1,0:T(8,128)S(1)} %get-tuple-element.26.w_ref, ...), custom_call_target="tpu_custom_call" | custom-call | tf_op jit(solution)/shard_map/pallas_call | solution.py:40
  91.1 3.5 %all-to-all-start.4 = ((bf16[4,288,128]{2,1,0:T(8,128)(2,1)}), bf16[4,288,128]{2,1,0:T(8,128)(2,1)S(1)}, u32[]{:S(2)}, u32[]{:S(2)}) async-start(bf16[4,288,128]{2,1,0:T(8,128)(2,1)} %get-tuple-element.30), calls=%async_computation.4 | async-start | bytes 589824 | tf_op jit(solution)/shard_map/all_to_all | solution.py:355
  94.6 0.1 shard_map.134
  94.7 4.7 %all-gather.3 = bf16[2048,128]{1,0:T(8,128)(2,1)S(1)} all-gather(bf16[1024,128]{1,0:T(8,128)(2,1)S(1)} %get-tuple-element.33), channel_id=5, replica_groups=mesh['y'=4,'zh'=4,'x'=4,'zl'=4,'core'=2] {'core'}, dimensions={0}, use_global_device_ids=true | all-gather | bytes 786432 | tf_op jit(solution)/shard_map/all_gather | solution.py:359
  99.4 0.8 all-to-all-done.4.dq_ref
  100.3 0.3 shard_map.135
  100.6 8.8 %all_to_all.38.dk_ref = bf16[4,256,128]{2,1,0:T(8,128)(2,1)S(1)} all-to-all(bf16[4,256,128]{2,1,0:T(8,128)(2,1)S(1)} %get-tuple-element.34), channel_id=1, replica_groups=mesh['y'=4,'zh'=4,'x'=4,'zl'=4,'core'=2] {'y'}, dimensions={0} | all-to-all | bytes 524288 | tf_op jit(solution)/shard_map/all_to_all | solution.py:355
  109.4 0.3 shard_map.136
  109.7 17.6 %all_to_all.39 = bf16[4,64,256]{2,1,0:T(8,128)(2,1)S(1)} all-to-all(bf16[4,64,256]{2,1,0:T(8,128)(2,1)S(1)} %shard_map.136), channel_id=1, replica_groups=mesh['y'=4,'zh'=4,'x'=4,'zl'=4,'core'=2] {'zh'}, dimensions={0} | all-to-all | bytes 262144 | tf_op jit(solution)/shard_map/all_to_all | solution.py:355
  127.3 7.9 %all-gather.4 = bf16[8,64,256]{2,1,0:T(8,128)(2,1)S(1)} all-gather(bf16[4,64,256]{2,1,0:T(8,128)(2,1)S(1)} %all_to_all.39), channel_id=6, replica_groups=mesh['y'=4,'zh'=4,'x'=4,'zl'=4,'core'=2] {'core'}, dimensions={0}, use_global_device_ids=true | all-gather | bytes 393216 | tf_op jit(solution)/shard_map/all_gather | solution.py:359
  135.3 0.0 copy-done
  135.3 0.0 copy-done.1
  135.3 0.0 copy-done.2
  135.3 0.9 shard_map.137
  (2 shorter events, 0.0 us)
Async XLA Ops:
  54.5 19.5 %all-to-all-start.2 = ((bf16[4,256,256]{2,1,0:T(8,128)(2,1)}), bf16[4,256,256]{2,1,0:T(8,128)(2,1)S(1)}, u32[]{:S(2)}, u32[]{:S(2)}) async-start(bf16[4,256,256]{2,1,0:T(8,128)(2,1)} %shard_map.131), calls=%async_computation.2 | async-start | bytes 1048576 | tf_op jit(solution)/shard_map/all_to_all | solution.py:355
  87.0 48.2 %copy-start = (f32[2,224]{1,0:T(2,128)S(1)}, f32[2,224]{1,0:T(2,128)}, u32[]{:S(2)}) copy-start(f32[2,224]{1,0:T(2,128)} %master_ref.1) | copy-start | bytes 5380
  87.0 48.2 %copy-start.1 = (f32[2,224]{1,0:T(2,128)S(1)}, f32[2,224]{1,0:T(2,128)}, u32[]{:S(2)}) copy-start(f32[2,224]{1,0:T(2,128)} %first_ref.1) | copy-start | bytes 5380
  87.0 48.2 %copy-start.2 = (f32[2,224]{1,0:T(2,128)S(1)}, f32[2,224]{1,0:T(2,128)}, u32[]{:S(2)}) copy-start(f32[2,224]{1,0:T(2,128)} %second_ref.1) | copy-start | bytes 5380
  91.1 9.1 %all-to-all-start.4 = ((bf16[4,288,128]{2,1,0:T(8,128)(2,1)}), bf16[4,288,128]{2,1,0:T(8,128)(2,1)S(1)}, u32[]{:S(2)}, u32[]{:S(2)}) async-start(bf16[4,288,128]{2,1,0:T(8,128)(2,1)} %get-tuple-element.30), calls=%async_computation.4 | async-start | bytes 589824 | tf_op jit(solution)/shard_map/all_to_all | solution.py:355
